TPU v7x, 256 devices: a whole 4x4x8 slice. The times are simulated.
256 devices in a mesh: gx: 16 (over z, core), gy: 16 (over x, y).
Axes of the slice: x: 4, y: 4, z: 8, core: 2. Of those that a mesh axis runs over, the one named last changes fastest.
Arguments:
- velocity_guess: float32 [3, 256, 256, 256], P(None, 'gx', 'gy'), may hold values from -1.2 to 1.2
- forcing: float32 [3, 256, 256, 256], P(None, 'gx', 'gy'), may hold values from -6 to 6
- cell_type: int32 [256, 256, 256], P('gx', 'gy'), may hold values from 0 to 3
- viscosities: float32 [4], replicated, may hold values from 0.2 to 5
Outputs:
- level0_iterate: float32 [3, 256, 256, 256], P(None, 'gx', 'gy')
- level1_correction: float32 [3, 128, 128, 128], P(None, 'gx', 'gy')
- level2_correction: float32 [3, 64, 64, 64], P(None, 'gx', 'gy')
- level3_correction: float32 [3, 32, 32, 32], P(None, 'gx', 'gy')
- level4_correction: float32 [3, 16, 16, 16], P(None, 'gx', 'gy')
- coarsest_residual: float32 [3, 16, 16, 16], P(None, 'gx', 'gy')
All inputs are finite; a program needn't handle non-finite values.
Results may differ from a plain program's by a relative error of at most 0.00027.
Values sent between devices are 32-bit elements; how exact they have to be, the bound alone decides.
No kernel may reach another device: no remote copies, remote signals or barrier semaphores. Data moves between devices by JAX's collectives and lax.ppermute only.
A program may use at most 128 MiB of HBM per device.

v0:
```python
import jax
import jax.numpy as jnp
from jax import lax
from jax.sharding import PartitionSpec as P

SWEEPS = 3
LEVELS = 4


damping = 0.8
mass_term = 0.05


def passed_along(value, axis, steps):
    count = lax.axis_size(axis)
    initial, last = (max(0, -steps), min(count, count - steps))
    return lax.ppermute(value, axis, [(source, source + steps) for source in range(initial, last)])


def swapped(block, axis, stride):
    count = lax.axis_size(axis)
    route = []
    for low in range(count):
        high = low | 1 << stride
        if high != low and high < count:
            route += [(low, high), (high, low)]
    return lax.ppermute(block, axis, route)


def with_halo(shard, sides, width):
    for axis, dim in sides:
        devices, length = (lax.axis_size(axis), shard.shape[dim])
        up = [(i, (i + 1) % devices) for i in range(devices - 1)]
        down = [(j, i) for i, j in up]
        last = lax.slice_in_dim(shard, length - width, length, axis=dim)
        initial = lax.slice_in_dim(shard, 0, width, axis=dim)
        before = lax.ppermute(last, axis, up)
        after = lax.ppermute(initial, axis, down)
        shard = jnp.concatenate([before, shard, after], axis=dim)
    return shard


def coefficients(viscosity, level_scale):
    padded = jnp.pad(viscosity, ((0, 0), (0, 0), (1, 1)))
    centre = padded[1:-1, 1:-1, 1:-1]
    face_terms = (
        0.5 * (centre + padded[:-2, 1:-1, 1:-1]),
        0.5 * (centre + padded[2:, 1:-1, 1:-1]),
        0.5 * (centre + padded[1:-1, :-2, 1:-1]),
        0.5 * (centre + padded[1:-1, 2:, 1:-1]),
        0.5 * (centre + padded[1:-1, 1:-1, :-2]),
        0.5 * (centre + padded[1:-1, 1:-1, 2:]),
    )
    face_sum = (
        face_terms[0]
        + face_terms[1]
        + face_terms[2]
        + face_terms[3]
        + face_terms[4]
        + face_terms[5]
    )
    return (face_terms, mass_term + level_scale * face_sum)


def operate(velocity, face_terms, diagonal, level_scale):
    padded = jnp.pad(velocity, ((0, 0), (0, 0), (0, 0), (1, 1)))
    centre = padded[:, 1:-1, 1:-1, 1:-1]
    flux = (
        face_terms[0] * padded[:, :-2, 1:-1, 1:-1]
        + face_terms[1] * padded[:, 2:, 1:-1, 1:-1]
        + face_terms[2] * padded[:, 1:-1, :-2, 1:-1]
        + face_terms[3] * padded[:, 1:-1, 2:, 1:-1]
        + face_terms[4] * padded[:, 1:-1, 1:-1, :-2]
        + face_terms[5] * padded[:, 1:-1, 1:-1, 2:]
    )
    return diagonal * centre - level_scale * flux


def restrict(values):
    channels, rows_x, rows_y, rows_z = values.shape
    return values.reshape(channels, rows_x // 2, 2, rows_y // 2, 2, rows_z // 2, 2).mean(
        axis=(2, 4, 6)
    )


def own_part(values, axis_dim, position, groups):
    share_rows = values.shape[axis_dim] // groups
    return lax.dynamic_slice_in_dim(values, position % groups * share_rows, share_rows, axis_dim)


def neighbour_rows(block_data, step_x, step_y):
    if step_x > 0:
        lower_rows = passed_along(block_data[:, -1:], "gx", step_x)
        upper_rows = passed_along(block_data[:, :1], "gx", -step_x)
    else:
        lower_rows = jnp.zeros_like(block_data[:, :1])
        upper_rows = lower_rows
    block_data = jnp.concatenate([lower_rows, block_data, upper_rows], axis=1)
    if step_y > 0:
        lower_rows = passed_along(block_data[:, :, -1:], "gy", step_y)
        upper_rows = passed_along(block_data[:, :, :1], "gy", -step_y)
    else:
        lower_rows = jnp.zeros_like(block_data[:, :, :1])
        upper_rows = lower_rows
    return jnp.concatenate([lower_rows, block_data, upper_rows], axis=2)


def pair_up(packet, grid_level, place_x, place_y):
    stride = 2 ** (grid_level - 1)
    partner = swapped(packet, "gx", grid_level - 1)
    is_lower = place_x // stride % 2 == 0
    packet = jnp.where(
        is_lower,
        jnp.concatenate([packet, partner], axis=1),
        jnp.concatenate([partner, packet], axis=1),
    )
    partner = swapped(packet, "gy", grid_level - 1)
    is_lower = place_y // stride % 2 == 0
    packet = jnp.where(
        is_lower,
        jnp.concatenate([packet, partner], axis=2),
        jnp.concatenate([partner, packet], axis=2),
    )
    return packet


def coarse_level(packet, grid_level, step_x, step_y):
    level_scale = 0.25**grid_level
    visc_pad = neighbour_rows(packet[3:], step_x, step_y)
    face_terms, diagonal = coefficients(visc_pad[0], level_scale)
    source = packet[:3]
    velocity = damping * source / diagonal
    for sweep_index in range(1, SWEEPS):
        velocity = (
            velocity
            + damping
            * (
                source
                - operate(
                    neighbour_rows(velocity, step_x, step_y), face_terms, diagonal, level_scale
                )
            )
            / diagonal
        )
    residual = source - operate(
        neighbour_rows(velocity, step_x, step_y), face_terms, diagonal, level_scale
    )
    return (velocity, residual)


def on_device(velocity_guess, forcing, cell_type, viscosities):
    width_x = lax.axis_size("gx")
    width_y = lax.axis_size("gy")
    place_x = lax.axis_index("gx")
    place_y = lax.axis_index("gy")
    type_ids = jnp.arange(viscosities.shape[0], dtype=jnp.int32)
    viscosity = jnp.sum(
        jnp.where(
            cell_type[None] == type_ids[:, None, None, None],
            viscosities[:, None, None, None],
            jnp.float32(0.0),
        ),
        axis=0,
    )
    stacked = jnp.concatenate([velocity_guess, viscosity[None]], axis=0)
    padded = with_halo(stacked, (("gx", 1), ("gy", 2)), 1)
    face_terms, diagonal = coefficients(padded[3], 1.0)
    velocity_pad = padded[:3]
    for sweep_index in range(SWEEPS):
        velocity = (
            velocity_pad[:, 1:-1, 1:-1]
            + damping * (forcing - operate(velocity_pad, face_terms, diagonal, 1.0)) / diagonal
        )
        velocity_pad = with_halo(velocity, (("gx", 1), ("gy", 2)), 1)
    residual = forcing - operate(velocity_pad, face_terms, diagonal, 1.0)
    velocity = velocity_pad[:, 1:-1, 1:-1]
    results = [velocity]
    packet = restrict(jnp.concatenate([residual, viscosity[None]], axis=0))
    replicate_from = LEVELS + 1
    for grid_level in range(1, LEVELS + 1):
        packet = pair_up(packet, grid_level, place_x, place_y)
        entire = grid_level >= replicate_from
        step_x = 0 if entire or 2**grid_level >= width_x else 2**grid_level
        step_y = 0 if entire or 2**grid_level >= width_y else 2**grid_level
        velocity, residual = coarse_level(packet, grid_level, step_x, step_y)
        groups_x = min(2**grid_level, width_x)
        groups_y = min(2**grid_level, width_y)
        results.append(own_part(own_part(velocity, 1, place_x, groups_x), 2, place_y, groups_y))
        if grid_level == LEVELS:
            residual = own_part(own_part(residual, 1, place_x, groups_x), 2, place_y, groups_y)
        else:
            packet = restrict(jnp.concatenate([residual, packet[3:]], axis=0))
    return (results[0], results[1], results[2], results[3], results[4], residual)


def solution(mesh):
    return jax.shard_map(
        on_device,
        mesh=mesh,
        in_specs=(P(None, "gx", "gy", None), P(None, "gx", "gy", None), P("gx", "gy", None), P()),
        out_specs=(
            P(None, "gx", "gy", None),
            P(None, "gx", "gy", None),
            P(None, "gx", "gy", None),
            P(None, "gx", "gy", None),
            P(None, "gx", "gy", None),
            P(None, "gx", "gy", None),
        ),
        check_vma=False,
    )
```

profile of v0, /device:TPU:32, one launch (start us, length us, event | category | flops | bytes accessed | tf_op | source)
XLA Modules:
  0.0 560.5 jit_solution(15770652911933556070)
XLA Ops:
  79.5 18.9 %concatenate.406 = f32[1,8,2,8,2,128,2]{6,5,4,3,2,1,0:T(8,128)} reshape(f32[16,16,256]{2,1,0:T(8,128)} %copy-done.2) | data formatting | bytes 524288 | tf_op jit(solution)/shard_map/concatenate | solution.py:178
  98.3 10.6 %copy.195 = f32[1,8,2,8,2,128,2]{5,3,6,4,2,1,0:T(8,128)} copy(f32[1,8,2,8,2,128,2]{6,5,4,3,2,1,0:T(8,128)} %concatenate.406) | data formatting | bytes 524288 | tf_op jit(solution)/shard_map/concatenate | solution.py:178
  113.8 52.3 %reshape.65 = f32[3,8,2,8,2,128,2]{6,5,2,1,4,3,0:T(8,128)} reshape(f32[3,16,16,256]{3,1,2,0:T(8,128)} %fusion.4) | data formatting | bytes 1572864 | tf_op jit(solution)/shard_map/concatenate | solution.py:178
  166.2 28.9 %copy.194 = f32[3,8,2,8,2,128,2]{5,3,6,4,2,1,0:T(8,128)S(1)} copy(f32[3,8,2,8,2,128,2]{6,5,2,1,4,3,0:T(8,128)} %reshape.65) | data formatting | bytes 1572864 | tf_op jit(solution)/shard_map/concatenate | solution.py:178
  202.3 6.8 %collective-permute-done.17 = f32[4,16,8,128]{3,2,1,0:T(8,128)S(1)} collective-permute-done((f32[4,16,8,128]{3,2,1,0:T(8,128)S(1)}, f32[4,16,8,128]{3,2,1,0:T(8,128)S(1)}, u32[]{:S(2)}, u32[]{:S(2)}) %collective-permute-start.17) | collective-permute-done | bytes 262176 | tf_op jit(solution)/shard_map/ppermute | solution.py:27
  209.1 5.9 %collective-permute-start.18 = (f32[1,1,16,128]{3,2,1,0:T(8,128)S(1)}, f32[1,1,16,128]{3,2,1,0:T(8,128)S(1)}, u32[]{:S(2)}, u32[]{:S(2)}) collective-permute-start(f32[1,1,16,128]{3,2,1,0:T(8,128)S(1)} %get-tuple-element.97), channel_id=1, source_target_pairs={{0,32},{16,48},{32,64},{48,80},{64,96},{80,112},{96,128},{112,144}... | collective-permute-start | bytes 24584 | tf_op jit(solution)/shard_map/ppermute | solution.py:17
  217.0 5.5 collective-permute-done.19
  222.5 5.5 collective-permute-start.20
  229.4 5.7 %collective-permute-done.21 = f32[1,18,1,128]{3,2,1,0:T(1,128)S(1)} collective-permute-done((f32[1,18,1,128]{3,2,1,0:T(1,128)S(1)}, f32[1,18,1,128]{3,2,1,0:T(1,128)S(1)}, u32[]{:S(2)}, u32[]{:S(2)}) %collective-permute-start.21) | collective-permute-done | bytes 9248 | tf_op jit(solution)/shard_map/ppermute | solution.py:17
  245.0 5.8 %collective-permute-start.24 = (f32[3,18,1,128]{3,2,1,0:T(1,128)S(1)}, f32[3,18,1,128]{3,2,1,0:T(1,128)S(1)}, u32[]{:S(2)}, u32[]{:S(2)}) collective-permute-start(f32[3,18,1,128]{3,2,1,0:T(1,128)S(1)} %get-tuple-element.117), channel_id=1, source_target_pairs={{0,2},{1,3},{2,4},{3,5},{4,6},{5,7},{6,8},{7,9},{8,10},{9,11},{10,... | collective-permute-start | bytes 82952 | tf_op jit(solution)/shard_map/ppermute | solution.py:17
  252.3 5.7 %collective-permute-done.25 = f32[3,18,1,128]{3,2,1,0:T(1,128)S(1)} collective-permute-done((f32[3,18,1,128]{3,2,1,0:T(1,128)S(1)}, f32[3,18,1,128]{3,2,1,0:T(1,128)S(1)}, u32[]{:S(2)}, u32[]{:S(2)}) %collective-permute-start.25) | collective-permute-done | bytes 27680 | tf_op jit(solution)/shard_map/ppermute | solution.py:17
  273.6 5.7 %collective-permute-done.29 = f32[3,18,1,128]{3,2,1,0:T(1,128)S(1)} collective-permute-done((f32[3,18,1,128]{3,2,1,0:T(1,128)S(1)}, f32[3,18,1,128]{3,2,1,0:T(1,128)S(1)}, u32[]{:S(2)}, u32[]{:S(2)}) %collective-permute-start.29) | collective-permute-done | bytes 27680 | tf_op jit(solution)/shard_map/ppermute | solution.py:17
  289.3 5.5 collective-permute-start.32
  296.3 5.7 %collective-permute-done.33 = f32[3,18,1,128]{3,2,1,0:T(1,128)S(1)} collective-permute-done((f32[3,18,1,128]{3,2,1,0:T(1,128)S(1)}, f32[3,18,1,128]{3,2,1,0:T(1,128)S(1)}, u32[]{:S(2)}, u32[]{:S(2)}) %collective-permute-start.33) | collective-permute-done | bytes 27680 | tf_op jit(solution)/shard_map/ppermute | solution.py:17
  303.2 8.7 %copy.196 = f32[4,16,16,128]{0,3,2,1:T(8,128)} copy(f32[4,16,16,128]{3,2,1,0:T(8,128)S(1)} %pad_maximum_fusion.50) | data formatting | bytes 1048576 | tf_op jit(solution)/shard_map/concatenate | solution.py:192
  311.9 11.7 %reduce_sum.47 = f32[4,8,8,64]{0,3,2,1:T(8,128)S(1)} reduce(f32[4,8,2,8,2,64,2]{0,6,5,4,3,2,1:T(2,128)} %bitcast.26, f32[]{:T(128)} %constant.287.clone.1), dimensions={2,4,6}, to_apply=%region_2.3 | reduce | flops 114688 | bytes 589828 | tf_op jit(solution)/shard_map/reduce_sum | solution.py:81
  331.1 6.4 %collective-permute-done.35 = f32[4,16,8,64]{3,2,1,0:T(8,128)S(1)} collective-permute-done((f32[4,16,8,64]{3,2,1,0:T(8,128)S(1)}, f32[4,16,8,64]{3,2,1,0:T(8,128)S(1)}, u32[]{:S(2)}, u32[]{:S(2)}) %collective-permute-start.35) | collective-permute-done | bytes 131104 | tf_op jit(solution)/shard_map/ppermute | solution.py:27
  361.6 5.1 collective-permute-done.41
  380.1 5.1 collective-permute-done.45
  417.1 9.0 %reduce_sum.48 = f32[4,8,8,32]{0,3,2,1:T(8,128)S(1)} reduce(f32[4,8,2,8,2,32,2]{0,6,5,4,3,2,1:T(2,128)} %bitcast.27, f32[]{:T(128)} %constant.287.clone.1), dimensions={2,4,6}, to_apply=%region_3.4 | reduce | flops 57344 | bytes 294916 | tf_op jit(solution)/shard_map/reduce_sum | solution.py:81
  432.9 6.3 %collective-permute-done.53 = f32[4,16,8,32]{3,2,1,0:T(8,128)S(1)} collective-permute-done((f32[4,16,8,32]{3,2,1,0:T(8,128)S(1)}, f32[4,16,8,32]{3,2,1,0:T(8,128)S(1)}, u32[]{:S(2)}, u32[]{:S(2)}) %collective-permute-start.53) | collective-permute-done | bytes 65568 | tf_op jit(solution)/shard_map/ppermute | solution.py:27
  442.9 8.1 %collective-permute-done.55 = f32[1,1,16,32]{3,2,1,0:T(8,128)S(1)} collective-permute-done((f32[1,1,16,32]{3,2,1,0:T(8,128)S(1)}, f32[1,1,16,32]{3,2,1,0:T(8,128)S(1)}, u32[]{:S(2)}, u32[]{:S(2)}) %collective-permute-start.55) | collective-permute-done | bytes 2080 | tf_op jit(solution)/shard_map/ppermute | solution.py:17
  452.4 6.0 %collective-permute-start.56 = (f32[1,18,1,32]{3,2,1,0:T(1,128)S(1)}, f32[1,18,1,32]{3,2,1,0:T(1,128)S(1)}, u32[]{:S(2)}, u32[]{:S(2)}) collective-permute-start(f32[1,18,1,32]{3,2,1,0:T(1,128)S(1)} %get-tuple-element.137), channel_id=1, source_target_pairs={{0,8},{1,9},{2,10},{3,11},{4,12},{5,13},{6,14},{7,15},{16,24},{17,... | collective-permute-start | bytes 6920 | tf_op jit(solution)/shard_map/ppermute | solution.py:17
  463.4 8.1 %collective-permute-done.59 = f32[3,1,16,32]{3,2,1,0:T(8,128)S(1)} collective-permute-done((f32[3,1,16,32]{3,2,1,0:T(8,128)S(1)}, f32[3,1,16,32]{3,2,1,0:T(8,128)S(1)}, u32[]{:S(2)}, u32[]{:S(2)}) %collective-permute-start.59) | collective-permute-done | bytes 6176 | tf_op jit(solution)/shard_map/ppermute | solution.py:17
  471.6 5.7 %collective-permute-start.60 = (f32[3,18,1,32]{3,2,1,0:T(1,128)S(1)}, f32[3,18,1,32]{3,2,1,0:T(1,128)S(1)}, u32[]{:S(2)}, u32[]{:S(2)}) collective-permute-start(f32[3,18,1,32]{3,2,1,0:T(1,128)S(1)} %get-tuple-element.105), channel_id=1, source_target_pairs={{0,8},{1,9},{2,10},{3,11},{4,12},{5,13},{6,14},{7,15},{16,24},{17,... | collective-permute-start | bytes 20744 | tf_op jit(solution)/shard_map/ppermute | solution.py:17
  478.8 5.7 %collective-permute-done.61 = f32[3,18,1,32]{3,2,1,0:T(1,128)S(1)} collective-permute-done((f32[3,18,1,32]{3,2,1,0:T(1,128)S(1)}, f32[3,18,1,32]{3,2,1,0:T(1,128)S(1)}, u32[]{:S(2)}, u32[]{:S(2)}) %collective-permute-start.61) | collective-permute-done | bytes 6944 | tf_op jit(solution)/shard_map/ppermute | solution.py:17
  488.5 8.1 %collective-permute-done.63 = f32[3,1,16,32]{3,2,1,0:T(8,128)S(1)} collective-permute-done((f32[3,1,16,32]{3,2,1,0:T(8,128)S(1)}, f32[3,1,16,32]{3,2,1,0:T(8,128)S(1)}, u32[]{:S(2)}, u32[]{:S(2)}) %collective-permute-start.63) | collective-permute-done | bytes 6176 | tf_op jit(solution)/shard_map/ppermute | solution.py:17
  499.8 5.7 %collective-permute-done.65 = f32[3,18,1,32]{3,2,1,0:T(1,128)S(1)} collective-permute-done((f32[3,18,1,32]{3,2,1,0:T(1,128)S(1)}, f32[3,18,1,32]{3,2,1,0:T(1,128)S(1)}, u32[]{:S(2)}, u32[]{:S(2)}) %collective-permute-start.65) | collective-permute-done | bytes 6944 | tf_op jit(solution)/shard_map/ppermute | solution.py:17
  511.3 6.6 %collective-permute-done.67 = f32[3,1,16,32]{3,2,1,0:T(8,128)S(1)} collective-permute-done((f32[3,1,16,32]{3,2,1,0:T(8,128)S(1)}, f32[3,1,16,32]{3,2,1,0:T(8,128)S(1)}, u32[]{:S(2)}, u32[]{:S(2)}) %collective-permute-start.67) | collective-permute-done | bytes 6176 | tf_op jit(solution)/shard_map/ppermute | solution.py:17
  521.5 5.3 collective-permute-done.69
  538.5 9.6 %collective-permute-done.70 = f32[4,8,8,16]{3,2,1,0:T(8,128)S(1)} collective-permute-done((f32[4,8,8,16]{3,2,1,0:T(8,128)S(1)}, f32[4,8,8,16]{3,2,1,0:T(8,128)S(1)}, u32[]{:S(2)}, u32[]{:S(2)}) %collective-permute-start.70) | collective-permute-done | bytes 16416 | tf_op jit(solution)/shard_map/ppermute | solution.py:27
  548.9 7.3 %collective-permute-done.71 = f32[4,16,8,16]{3,2,1,0:T(8,128)S(1)} collective-permute-done((f32[4,16,8,16]{3,2,1,0:T(8,128)S(1)}, f32[4,16,8,16]{3,2,1,0:T(8,128)S(1)}, u32[]{:S(2)}, u32[]{:S(2)}) %collective-permute-start.71) | collective-permute-done | bytes 32800 | tf_op jit(solution)/shard_map/ppermute | solution.py:27
  (277 shorter events, 260.5 us)
Async XLA Ops:
  14.7 6.8 %collective-permute-start.3 = (f32[4,18,1,256]{3,1,2,0:T(8,128)S(1)}, f32[4,18,1,256]{3,1,2,0:T(8,128)S(1)}, u32[]{:S(2)}, u32[]{:S(2)}) collective-permute-start(f32[4,18,1,256]{3,1,2,0:T(8,128)S(1)} %get-tuple-element.74), channel_id=1, source_target_pairs={{1,0},{2,1},{3,2},{4,3},{5,4},{6,5},{7,6},{8,7},{9,8},{10,9},{11,1... | collective-permute-start | bytes 221192 | tf_op jit(solution)/shard_map/ppermute | solution.py:38
  52.0 6.4 %collective-permute-start.10 = (f32[3,18,1,256]{3,1,2,0:T(8,128)S(1)}, f32[3,18,1,256]{3,1,2,0:T(8,128)S(1)}, u32[]{:S(2)}, u32[]{:S(2)}) collective-permute-start(f32[3,18,1,256]{3,1,2,0:T(8,128)S(1)} %get-tuple-element.79), channel_id=1, source_target_pairs={{0,1},{1,2},{2,3},{3,4},{4,5},{5,6},{6,7},{7,8},{8,9},{9,10},{10,1... | collective-permute-start | bytes 165896 | tf_op jit(solution)/shard_map/ppermute | solution.py:37
  73.1 35.9 %collective-permute-start.14 = (f32[3,18,1,256]{3,1,2,0:T(8,128)}, f32[3,18,1,256]{3,1,2,0:T(8,128)}, u32[]{:S(2)}, u32[]{:S(2)}) collective-permute-start(f32[3,18,1,256]{3,1,2,0:T(8,128)} %get-tuple-element.77), channel_id=1, source_target_pairs={{0,1},{1,2},{2,3},{3,4},{4,5},{5,6},{6,7},{7,8},{8,9},{9,10},{10,1... | collective-permute-start | bytes 165896 | tf_op jit(solution)/shard_map/ppermute | solution.py:37
  77.7 31.2 %collective-permute-start.15 = (f32[3,18,1,256]{3,1,2,0:T(8,128)}, f32[3,18,1,256]{3,1,2,0:T(8,128)}, u32[]{:S(2)}, u32[]{:S(2)}) collective-permute-start(f32[3,18,1,256]{3,1,2,0:T(8,128)} %get-tuple-element.78), channel_id=1, source_target_pairs={{1,0},{2,1},{3,2},{4,3},{5,4},{6,5},{7,6},{8,7},{9,8},{10,9},{11,1... | collective-permute-start | bytes 165896 | tf_op jit(solution)/shard_map/ppermute | solution.py:38
  199.8 9.3 %collective-permute-start.17 = (f32[4,16,8,128]{3,2,1,0:T(8,128)S(1)}, f32[4,16,8,128]{3,2,1,0:T(8,128)S(1)}, u32[]{:S(2)}, u32[]{:S(2)}) collective-permute-start(f32[4,16,8,128]{3,2,1,0:T(8,128)S(1)} %maximum_select_fusion.4), channel_id=1, source_target_pairs={{0,1},{1,0},{2,3},{3,2},{4,5},{5,4},{6,7},{7,6},{8,9},{9,8},{10,11... | collective-permute-start | bytes 786440 | tf_op jit(solution)/shard_map/ppermute | solution.py:27
  209.1 7.8 %collective-permute-start.18 = (f32[1,1,16,128]{3,2,1,0:T(8,128)S(1)}, f32[1,1,16,128]{3,2,1,0:T(8,128)S(1)}, u32[]{:S(2)}, u32[]{:S(2)}) collective-permute-start(f32[1,1,16,128]{3,2,1,0:T(8,128)S(1)} %get-tuple-element.97), channel_id=1, source_target_pairs={{0,32},{16,48},{32,64},{48,80},{64,96},{80,112},{96,128},{112,144}... | collective-permute-start | bytes 24584 | tf_op jit(solution)/shard_map/ppermute | solution.py:17
  215.0 7.5 %collective-permute-start.19 = (f32[1,1,16,128]{3,2,1,0:T(8,128)S(1)}, f32[1,1,16,128]{3,2,1,0:T(8,128)S(1)}, u32[]{:S(2)}, u32[]{:S(2)}) collective-permute-start(f32[1,1,16,128]{3,2,1,0:T(8,128)S(1)} %get-tuple-element.98), channel_id=1, source_target_pairs={{32,0},{48,16},{64,32},{80,48},{96,64},{112,80},{128,96},{144,112}... | collective-permute-start | bytes 24584 | tf_op jit(solution)/shard_map/ppermute | solution.py:17
  222.5 6.8 %collective-permute-start.20 = (f32[1,18,1,128]{3,2,1,0:T(1,128)S(1)}, f32[1,18,1,128]{3,2,1,0:T(1,128)S(1)}, u32[]{:S(2)}, u32[]{:S(2)}) collective-permute-start(f32[1,18,1,128]{3,2,1,0:T(1,128)S(1)} %get-tuple-element.141), channel_id=1, source_target_pairs={{0,2},{1,3},{2,4},{3,5},{4,6},{5,7},{6,8},{7,9},{8,10},{9,11},{10,... | collective-permute-start | bytes 27656 | tf_op jit(solution)/shard_map/ppermute | solution.py:17
  228.0 7.1 %collective-permute-start.21 = (f32[1,18,1,128]{3,2,1,0:T(1,128)S(1)}, f32[1,18,1,128]{3,2,1,0:T(1,128)S(1)}, u32[]{:S(2)}, u32[]{:S(2)}) collective-permute-start(f32[1,18,1,128]{3,2,1,0:T(1,128)S(1)} %get-tuple-element.142), channel_id=1, source_target_pairs={{2,0},{3,1},{4,2},{5,3},{6,4},{7,5},{8,6},{9,7},{10,8},{11,9},{12,... | collective-permute-start | bytes 27656 | tf_op jit(solution)/shard_map/ppermute | solution.py:17
  245.0 7.3 %collective-permute-start.24 = (f32[3,18,1,128]{3,2,1,0:T(1,128)S(1)}, f32[3,18,1,128]{3,2,1,0:T(1,128)S(1)}, u32[]{:S(2)}, u32[]{:S(2)}) collective-permute-start(f32[3,18,1,128]{3,2,1,0:T(1,128)S(1)} %get-tuple-element.117), channel_id=1, source_target_pairs={{0,2},{1,3},{2,4},{3,5},{4,6},{5,7},{6,8},{7,9},{8,10},{9,11},{10,... | collective-permute-start | bytes 82952 | tf_op jit(solution)/shard_map/ppermute | solution.py:17
  250.8 7.3 %collective-permute-start.25 = (f32[3,18,1,128]{3,2,1,0:T(1,128)S(1)}, f32[3,18,1,128]{3,2,1,0:T(1,128)S(1)}, u32[]{:S(2)}, u32[]{:S(2)}) collective-permute-start(f32[3,18,1,128]{3,2,1,0:T(1,128)S(1)} %get-tuple-element.118), channel_id=1, source_target_pairs={{2,0},{3,1},{4,2},{5,3},{6,4},{7,5},{8,6},{9,7},{10,8},{11,9},{12,... | collective-permute-start | bytes 82952 | tf_op jit(solution)/shard_map/ppermute | solution.py:17
  272.0 7.3 %collective-permute-start.29 = (f32[3,18,1,128]{3,2,1,0:T(1,128)S(1)}, f32[3,18,1,128]{3,2,1,0:T(1,128)S(1)}, u32[]{:S(2)}, u32[]{:S(2)}) collective-permute-start(f32[3,18,1,128]{3,2,1,0:T(1,128)S(1)} %get-tuple-element.116), channel_id=1, source_target_pairs={{2,0},{3,1},{4,2},{5,3},{6,4},{7,5},{8,6},{9,7},{10,8},{11,9},{12,... | collective-permute-start | bytes 82952 | tf_op jit(solution)/shard_map/ppermute | solution.py:17
  289.3 7.0 %collective-permute-start.32 = (f32[3,18,1,128]{3,2,1,0:T(1,128)S(1)}, f32[3,18,1,128]{3,2,1,0:T(1,128)S(1)}, u32[]{:S(2)}, u32[]{:S(2)}) collective-permute-start(f32[3,18,1,128]{3,2,1,0:T(1,128)S(1)} %get-tuple-element.113), channel_id=1, source_target_pairs={{0,2},{1,3},{2,4},{3,5},{4,6},{5,7},{6,8},{7,9},{8,10},{9,11},{10,... | collective-permute-start | bytes 82952 | tf_op jit(solution)/shard_map/ppermute | solution.py:17
  294.8 7.3 %collective-permute-start.33 = (f32[3,18,1,128]{3,2,1,0:T(1,128)S(1)}, f32[3,18,1,128]{3,2,1,0:T(1,128)S(1)}, u32[]{:S(2)}, u32[]{:S(2)}) collective-permute-start(f32[3,18,1,128]{3,2,1,0:T(1,128)S(1)} %get-tuple-element.114), channel_id=1, source_target_pairs={{2,0},{3,1},{4,2},{5,3},{6,4},{7,5},{8,6},{9,7},{10,8},{11,9},{12,... | collective-permute-start | bytes 82952 | tf_op jit(solution)/shard_map/ppermute | solution.py:17
  329.6 8.0 %collective-permute-start.35 = (f32[4,16,8,64]{3,2,1,0:T(8,128)S(1)}, f32[4,16,8,64]{3,2,1,0:T(8,128)S(1)}, u32[]{:S(2)}, u32[]{:S(2)}) collective-permute-start(f32[4,16,8,64]{3,2,1,0:T(8,128)S(1)} %maximum_select_fusion.5), channel_id=1, source_target_pairs={{0,2},{2,0},{1,3},{3,1},{4,6},{6,4},{5,7},{7,5},{8,10},{10,8},{9,1... | collective-permute-start | bytes 393224 | tf_op jit(solution)/shard_map/ppermute | solution.py:27
  341.4 6.4 %collective-permute-start.37 = (f32[1,1,16,64]{3,2,1,0:T(8,128)S(1)}, f32[1,1,16,64]{3,2,1,0:T(8,128)S(1)}, u32[]{:S(2)}, u32[]{:S(2)}) collective-permute-start(f32[1,1,16,64]{3,2,1,0:T(8,128)S(1)} %get-tuple-element.96), channel_id=1, source_target_pairs={{64,0},{80,16},{96,32},{112,48},{128,64},{144,80},{160,96},{176,11... | collective-permute-start | bytes 12296 | tf_op jit(solution)/shard_map/ppermute | solution.py:17
  360.1 6.6 %collective-permute-start.41 = (f32[3,1,16,64]{3,2,1,0:T(8,128)S(1)}, f32[3,1,16,64]{3,2,1,0:T(8,128)S(1)}, u32[]{:S(2)}, u32[]{:S(2)}) collective-permute-start(f32[3,1,16,64]{3,2,1,0:T(8,128)S(1)} %get-tuple-element.130), channel_id=1, source_target_pairs={{64,0},{80,16},{96,32},{112,48},{128,64},{144,80},{160,96},{176,11... | collective-permute-start | bytes 36872 | tf_op jit(solution)/shard_map/ppermute | solution.py:17
  378.6 6.6 %collective-permute-start.45 = (f32[3,1,16,64]{3,2,1,0:T(8,128)S(1)}, f32[3,1,16,64]{3,2,1,0:T(8,128)S(1)}, u32[]{:S(2)}, u32[]{:S(2)}) collective-permute-start(f32[3,1,16,64]{3,2,1,0:T(8,128)S(1)} %get-tuple-element.128), channel_id=1, source_target_pairs={{64,0},{80,16},{96,32},{112,48},{128,64},{144,80},{160,96},{176,11... | collective-permute-start | bytes 36872 | tf_op jit(solution)/shard_map/ppermute | solution.py:17
  396.9 6.6 %collective-permute-start.49 = (f32[3,1,16,64]{3,2,1,0:T(8,128)S(1)}, f32[3,1,16,64]{3,2,1,0:T(8,128)S(1)}, u32[]{:S(2)}, u32[]{:S(2)}) collective-permute-start(f32[3,1,16,64]{3,2,1,0:T(8,128)S(1)} %get-tuple-element.126), channel_id=1, source_target_pairs={{64,0},{80,16},{96,32},{112,48},{128,64},{144,80},{160,96},{176,11... | collective-permute-start | bytes 36872 | tf_op jit(solution)/shard_map/ppermute | solution.py:17
  432.7 6.5 %collective-permute-start.53 = (f32[4,16,8,32]{3,2,1,0:T(8,128)S(1)}, f32[4,16,8,32]{3,2,1,0:T(8,128)S(1)}, u32[]{:S(2)}, u32[]{:S(2)}) collective-permute-start(f32[4,16,8,32]{3,2,1,0:T(8,128)S(1)} %maximum_select_fusion.6), channel_id=1, source_target_pairs={{0,4},{4,0},{1,5},{5,1},{2,6},{6,2},{3,7},{7,3},{8,12},{12,8},{9,1... | collective-permute-start | bytes 196616 | tf_op jit(solution)/shard_map/ppermute | solution.py:27
  441.6 9.5 %collective-permute-start.55 = (f32[1,1,16,32]{3,2,1,0:T(8,128)S(1)}, f32[1,1,16,32]{3,2,1,0:T(8,128)S(1)}, u32[]{:S(2)}, u32[]{:S(2)}) collective-permute-start(f32[1,1,16,32]{3,2,1,0:T(8,128)S(1)} %get-tuple-element.94), channel_id=1, source_target_pairs={{128,0},{144,16},{160,32},{176,48},{192,64},{208,80},{224,96},{240... | collective-permute-start | bytes 6152 | tf_op jit(solution)/shard_map/ppermute | solution.py:17
  451.1 7.4 %collective-permute-start.57 = (f32[1,18,1,32]{3,2,1,0:T(1,128)S(1)}, f32[1,18,1,32]{3,2,1,0:T(1,128)S(1)}, u32[]{:S(2)}, u32[]{:S(2)}) collective-permute-start(f32[1,18,1,32]{3,2,1,0:T(1,128)S(1)} %get-tuple-element.138), channel_id=1, source_target_pairs={{8,0},{9,1},{10,2},{11,3},{12,4},{13,5},{14,6},{15,7},{24,16},{25,... | collective-permute-start | bytes 6920 | tf_op jit(solution)/shard_map/ppermute | solution.py:17
  452.4 7.4 %collective-permute-start.56 = (f32[1,18,1,32]{3,2,1,0:T(1,128)S(1)}, f32[1,18,1,32]{3,2,1,0:T(1,128)S(1)}, u32[]{:S(2)}, u32[]{:S(2)}) collective-permute-start(f32[1,18,1,32]{3,2,1,0:T(1,128)S(1)} %get-tuple-element.137), channel_id=1, source_target_pairs={{0,8},{1,9},{2,10},{3,11},{4,12},{5,13},{6,14},{7,15},{16,24},{17,... | collective-permute-start | bytes 6920 | tf_op jit(solution)/shard_map/ppermute | solution.py:17
  461.9 9.6 %collective-permute-start.59 = (f32[3,1,16,32]{3,2,1,0:T(8,128)S(1)}, f32[3,1,16,32]{3,2,1,0:T(8,128)S(1)}, u32[]{:S(2)}, u32[]{:S(2)}) collective-permute-start(f32[3,1,16,32]{3,2,1,0:T(8,128)S(1)} %get-tuple-element.124), channel_id=1, source_target_pairs={{128,0},{144,16},{160,32},{176,48},{192,64},{208,80},{224,96},{240... | collective-permute-start | bytes 18440 | tf_op jit(solution)/shard_map/ppermute | solution.py:17
  471.6 7.2 %collective-permute-start.60 = (f32[3,18,1,32]{3,2,1,0:T(1,128)S(1)}, f32[3,18,1,32]{3,2,1,0:T(1,128)S(1)}, u32[]{:S(2)}, u32[]{:S(2)}) collective-permute-start(f32[3,18,1,32]{3,2,1,0:T(1,128)S(1)} %get-tuple-element.105), channel_id=1, source_target_pairs={{0,8},{1,9},{2,10},{3,11},{4,12},{5,13},{6,14},{7,15},{16,24},{17,... | collective-permute-start | bytes 20744 | tf_op jit(solution)/shard_map/ppermute | solution.py:17
  477.3 7.3 %collective-permute-start.61 = (f32[3,18,1,32]{3,2,1,0:T(1,128)S(1)}, f32[3,18,1,32]{3,2,1,0:T(1,128)S(1)}, u32[]{:S(2)}, u32[]{:S(2)}) collective-permute-start(f32[3,18,1,32]{3,2,1,0:T(1,128)S(1)} %get-tuple-element.106), channel_id=1, source_target_pairs={{8,0},{9,1},{10,2},{11,3},{12,4},{13,5},{14,6},{15,7},{24,16},{25,... | collective-permute-start | bytes 20744 | tf_op jit(solution)/shard_map/ppermute | solution.py:17
  487.0 9.6 %collective-permute-start.63 = (f32[3,1,16,32]{3,2,1,0:T(8,128)S(1)}, f32[3,1,16,32]{3,2,1,0:T(8,128)S(1)}, u32[]{:S(2)}, u32[]{:S(2)}) collective-permute-start(f32[3,1,16,32]{3,2,1,0:T(8,128)S(1)} %get-tuple-element.122), channel_id=1, source_target_pairs={{128,0},{144,16},{160,32},{176,48},{192,64},{208,80},{224,96},{240... | collective-permute-start | bytes 18440 | tf_op jit(solution)/shard_map/ppermute | solution.py:17
  498.3 7.3 %collective-permute-start.65 = (f32[3,18,1,32]{3,2,1,0:T(1,128)S(1)}, f32[3,18,1,32]{3,2,1,0:T(1,128)S(1)}, u32[]{:S(2)}, u32[]{:S(2)}) collective-permute-start(f32[3,18,1,32]{3,2,1,0:T(1,128)S(1)} %get-tuple-element.104), channel_id=1, source_target_pairs={{8,0},{9,1},{10,2},{11,3},{12,4},{13,5},{14,6},{15,7},{24,16},{25,... | collective-permute-start | bytes 20744 | tf_op jit(solution)/shard_map/ppermute | solution.py:17
  508.2 9.6 %collective-permute-start.67 = (f32[3,1,16,32]{3,2,1,0:T(8,128)S(1)}, f32[3,1,16,32]{3,2,1,0:T(8,128)S(1)}, u32[]{:S(2)}, u32[]{:S(2)}) collective-permute-start(f32[3,1,16,32]{3,2,1,0:T(8,128)S(1)} %get-tuple-element.120), channel_id=1, source_target_pairs={{128,0},{144,16},{160,32},{176,48},{192,64},{208,80},{224,96},{240... | collective-permute-start | bytes 18440 | tf_op jit(solution)/shard_map/ppermute | solution.py:17
  519.5 7.3 %collective-permute-start.69 = (f32[3,18,1,32]{3,2,1,0:T(1,128)S(1)}, f32[3,18,1,32]{3,2,1,0:T(1,128)S(1)}, u32[]{:S(2)}, u32[]{:S(2)}) collective-permute-start(f32[3,18,1,32]{3,2,1,0:T(1,128)S(1)} %get-tuple-element.102), channel_id=1, source_target_pairs={{8,0},{9,1},{10,2},{11,3},{12,4},{13,5},{14,6},{15,7},{24,16},{25,... | collective-permute-start | bytes 20744 | tf_op jit(solution)/shard_map/ppermute | solution.py:17
  537.8 10.4 %collective-permute-start.70 = (f32[4,8,8,16]{3,2,1,0:T(8,128)S(1)}, f32[4,8,8,16]{3,2,1,0:T(8,128)S(1)}, u32[]{:S(2)}, u32[]{:S(2)}) collective-permute-start(f32[4,8,8,16]{3,2,1,0:T(8,128)S(1)} %broadcast_multiply_fusion), channel_id=1, source_target_pairs={{0,128},{128,0},{16,144},{144,16},{32,160},{160,32},{48,176},{176,... | collective-permute-start | bytes 49160 | tf_op jit(solution)/shard_map/ppermute | solution.py:27
  548.2 8.0 %collective-permute-start.71 = (f32[4,16,8,16]{3,2,1,0:T(8,128)S(1)}, f32[4,16,8,16]{3,2,1,0:T(8,128)S(1)}, u32[]{:S(2)}, u32[]{:S(2)}) collective-permute-start(f32[4,16,8,16]{3,2,1,0:T(8,128)S(1)} %maximum_select_fusion.7), channel_id=1, source_target_pairs={{0,8},{8,0},{1,9},{9,1},{2,10},{10,2},{3,11},{11,3},{4,12},{12,4},... | collective-permute-start | bytes 98312 | tf_op jit(solution)/shard_map/ppermute | solution.py:27
  (52 other events, 420.6 us)
where the time goes:
time: 570 us; the launch traced here: 561 us
  waiting for transfers between devices  196 us (34%)
  starting transfers between devices  171 us (30%)
  local copies, waits for them, and re-layouts  136 us (24%)
  other arithmetic  55 us (10%)
    ppermute x48, waiting for transfers between devices, passed_along(): lax.ppermute(value, axis, [(source, source + steps) for source in range(i...  127 us
    ppermute x48, starting transfers between devices, passed_along(): lax.ppermute(value, axis, [(source, source + steps) for source in range(i...  117 us
    concatenate x4, local copies, waits for them, and re-layouts, on_device(): packet = restrict(jnp.concatenate([residual, viscosity[None]], axis=0))  111 us
    ppermute x8, waiting for transfers between devices, swapped(): return lax.ppermute(block, axis, route)  46.4 us
    reduce_sum x4, other arithmetic, restrict(): values.reshape(channels, rows_x // 2, 2, rows_y // 2, 2, rows_z // 2, 2)  25.9 us
    ppermute x8, starting transfers between devices, with_halo(): before = lax.ppermute(last, axis, up)  25.8 us
    ppermute x8, waiting for transfers between devices, with_halo(): after = lax.ppermute(initial, axis, down)  20.2 us
    ppermute x8, starting transfers between devices, with_halo(): after = lax.ppermute(initial, axis, down)  18.1 us
  transfers between devices with their start and end apart: 72, of which 56 were waited for; matrix products, arithmetic and copies ran while one was open for 6% of the time, Pallas kernels for 0%

commit v1 on v0

v1 whole, which is shorter than its diff:
```python
import functools

import jax
import jax.numpy as jnp
from jax import lax
from jax.experimental import pallas as pl
from jax.experimental.pallas import tpu as pltpu
from jax.sharding import PartitionSpec as P

SWEEPS = 3
LEVELS = 4
HALO = SWEEPS + 1

damping = 0.8
mass_term = 0.05


def passed_along(value, axis, steps):
    count = lax.axis_size(axis)
    initial, last = (max(0, -steps), min(count, count - steps))
    return lax.ppermute(value, axis, [(source, source + steps) for source in range(initial, last)])


def split_dot(rows, pool):
    total = None
    for part in range(3):
        piece = rows.astype(jnp.bfloat16)
        term = jnp.dot(piece, pool, preferred_element_type=jnp.float32)
        total = term if total is None else total + term
        if part < 2:
            rows = rows - piece.astype(jnp.float32)
    return total


def pair_pool(lanes):
    source = lax.broadcasted_iota(jnp.int32, (lanes, 128), 0)
    target = lax.broadcasted_iota(jnp.int32, (lanes, 128), 1)
    return jnp.where(source // 2 == target, 0.125, 0.0).astype(jnp.bfloat16)


def make_coefficients(scale, m, cx, cym, cyp, czm, czp, weight, diag):
    planes, rows, lanes = m.shape
    half = 0.5 * scale
    lane = lax.broadcasted_iota(jnp.int32, (rows, lanes), 1)
    cx[0] = half * (m[0] + m[1])

    def plane(i, _):
        centre = m[i]
        upper = m[i + 1]
        y_lower = pltpu.roll(centre, 1, 0)
        y_upper = pltpu.roll(centre, rows - 1, 0)
        z_lower = jnp.where(lane == 0, 0.0, pltpu.roll(centre, 1, 1))
        z_upper = jnp.where(lane == lanes - 1, 0.0, pltpu.roll(centre, lanes - 1, 1))
        f_xl, f_xu = half * (centre + m[i - 1]), half * (centre + upper)
        f_yl, f_yu = half * (centre + y_lower), half * (centre + y_upper)
        f_zl, f_zu = half * (centre + z_lower), half * (centre + z_upper)
        total = mass_term + (f_xl + f_xu + f_yl + f_yu + f_zl + f_zu)
        cx[i] = f_xu
        cym[i], cyp[i] = f_yl, f_yu
        czm[i] = jnp.where(lane == 0, 0.0, f_zl)
        czp[i] = jnp.where(lane == lanes - 1, 0.0, f_zu)
        diag[i] = total
        weight[i] = jnp.where(centre > 0.0, damping / total, 0.0)
        return 0

    lax.fori_loop(1, planes - 1, plane, 0)


def flux_of(u, c, i, cx, cym, cyp, czm, czp):
    rows, lanes = u.shape[2:]
    centre = u[c, i]
    flux = cx[i - 1] * u[c, i - 1] + cx[i] * u[c, i + 1]
    flux += cym[i] * pltpu.roll(centre, 1, 0) + cyp[i] * pltpu.roll(centre, rows - 1, 0)
    flux += czm[i] * pltpu.roll(centre, 1, 1) + czp[i] * pltpu.roll(centre, lanes - 1, 1)
    return centre, flux


def relax(lo, hi, source, target, f, weight, faces, out=None):
    def plane(i, _):
        for c in range(3):
            centre, flux = flux_of(source, c, i, *faces)
            target[c, i] = (1.0 - damping) * centre + weight[i] * (f[c, i] + flux)
        return 0

    lax.fori_loop(lo, hi, plane, 0)


def start_from_zero(lo, hi, target, f, weight):
    def plane(i, _):
        for c in range(3):
            target[c, i] = weight[i] * f[c, i]
        return 0

    lax.fori_loop(lo, hi, plane, 0)


def residual_pairs(own, own_rows, u, f, m, diag, faces, pairs):
    def pair(p, _):
        i = HALO + 2 * p
        for c in range(3):
            both = None
            for j in (i, i + 1):
                centre, flux = flux_of(u, c, j, *faces)
                value = f[c, j] + flux - diag[j] * centre
                both = value if both is None else both + value
            pairs[c, p] = both[:own_rows]
        pairs[3, p] = (m[i] + m[i + 1])[:own_rows]
        return 0

    lax.fori_loop(0, own // 2, pair, 0)


def fine_kernel(u_in, f_in, m_in, ylo, yhi, xlo, xhi, u_out, packet,
                ua, ub, f, m, cx, cym, cyp, czm, czp, weight, diag, pairs, pooled):
    own, rows = u_in.shape[1:3]
    body = pl.ds(HALO, own)
    for c in range(3):
        ua[c, body, :rows] = u_in[c]
        ua[c, body, rows:rows + HALO] = yhi[c]
        ua[c, body, rows + HALO:] = ylo[c]
        ua[c, :HALO] = xlo[HALO * c:HALO * (c + 1)]
        ua[c, HALO + own:] = xhi[HALO * c:HALO * (c + 1)]
        f[c, body, :rows] = f_in[c]
        f[c, body, rows:rows + HALO] = yhi[3 + c]
        f[c, body, rows + HALO:] = ylo[3 + c]
        at = 3 * HALO + (HALO - 1) * c
        f[c, 1:HALO] = xlo[at:at + HALO - 1]
        f[c, HALO + own:HALO + own + HALO - 1] = xhi[at:at + HALO - 1]
    m[body, :rows] = m_in[...]
    m[body, rows:rows + HALO] = yhi[6]
    m[body, rows + HALO:] = ylo[6]
    at = 3 * HALO + 3 * (HALO - 1)
    m[:HALO] = xlo[at:]
    m[HALO + own:] = xhi[at:]
    planes = own + 2 * HALO
    make_coefficients(1.0, m, cx, cym, cyp, czm, czp, weight, diag)
    faces = (cx, cym, cyp, czm, czp)
    relax(1, planes - 1, ua, ub, f, weight, faces)
    relax(2, planes - 2, ub, ua, f, weight, faces)
    relax(3, planes - 3, ua, ub, f, weight, faces)
    for c in range(3):
        u_out[c] = ub[c, body, :rows]
    residual_pairs(own, rows, ub, f, m, diag, faces, pairs)
    lanes = pairs.shape[-1]
    summed = split_dot(pairs[...].reshape(-1, lanes), pair_pool(lanes))
    pooled[...] = summed.reshape(pooled.shape)
    packet[...] = pooled[:, pl.ds(0, rows // 2, 2), :] + pooled[:, pl.ds(1, rows // 2, 2), :]


def middle_kernel(scale, p_in, ylo, yhi, xlo, xhi, u_out, packet,
                  ua, ub, f, m, cx, cym, cyp, czm, czp, weight, diag, pairs, pooled):
    own, rows = p_in.shape[1:3]
    body = pl.ds(HALO, own)
    planes = own + 2 * HALO
    total_rows = m.shape[1]
    for c in range(4):
        if c < 3:
            place = f.at[c]
        else:
            place = m
        if total_rows > rows + 2 * HALO:
            place[body] = jnp.zeros((own,) + m.shape[1:], jnp.float32)
        place[body, :rows] = p_in[c]
        place[body, rows:rows + HALO] = yhi[c]
        place[body, total_rows - HALO:] = ylo[c]
        place[:HALO] = xlo[c]
        place[HALO + own:] = xhi[c]
    make_coefficients(scale, m, cx, cym, cyp, czm, czp, weight, diag)
    faces = (cx, cym, cyp, czm, czp)
    start_from_zero(1, planes - 1, ub, f, weight)
    relax(2, planes - 2, ub, ua, f, weight, faces)
    relax(3, planes - 3, ua, ub, f, weight, faces)
    lanes = u_out.shape[-1]
    for c in range(3):
        u_out[c] = ub[c, body, :rows, :lanes]
    residual_pairs(own, rows, ub, f, m, diag, faces, pairs)
    if rows > 4:
        lanes = pairs.shape[-1]
        summed = split_dot(pairs[...].reshape(-1, lanes), pair_pool(lanes))
        pooled[...] = summed.reshape(pooled.shape)
        packet[...] = pooled[:, pl.ds(0, rows // 2, 2), :] + pooled[:, pl.ds(1, rows // 2, 2), :]
    else:
        for c in range(4):
            for p in range(own // 2):
                for q in range(rows // 2):
                    at = 128 * (p * (rows // 2) + q)
                    pooled[c:c + 1, at:at + 128] = (
                        pairs[c, p, 2 * q:2 * q + 1] + pairs[c, p, 2 * q + 1:2 * q + 2]
                    )
        depth = pooled.shape[1]
        source = lax.broadcasted_iota(jnp.int32, (depth, 128), 0)
        target = lax.broadcasted_iota(jnp.int32, (depth, 128), 1)
        hit = (source // 128 * 32 + source % 128 // 2 == target) & (source % 128 < 64)
        pool = jnp.where(hit, 0.125, 0.0).astype(jnp.bfloat16)
        packet[...] = split_dot(pooled[...], pool)[:4]


def last_kernel(place, g, u3_out, u4_out, r4_out, ua, ub, f, m, faces, weight, diag,
                f4, m4, faces4, weight4, diag4, va, vb):
    count = g.shape[0]
    rows, lanes = g.shape[2:]
    shape = (rows, lanes)
    lane = lax.broadcasted_iota(jnp.int32, shape, 1)
    row = lax.broadcasted_iota(jnp.int32, shape, 0)
    x_bit, y_bit, z = lane // 64, lane // 32 % 2, lane % 32
    zero = jnp.zeros(shape, jnp.float32)

    def neighbours3(at, i):
        centre = at(i)
        flipped = pltpu.roll(centre, 64, 1)
        from_lower_row = jnp.where(row == 0, 0.0, pltpu.roll(flipped, 1, 0))
        from_upper_row = jnp.where(row == rows - 1, 0.0, pltpu.roll(flipped, rows - 1, 0))
        xl = jnp.where(x_bit == 1, flipped, from_lower_row)
        xu = jnp.where(x_bit == 0, flipped, from_upper_row)
        below = pltpu.roll(at(i - 1), lanes - 32, 1) if i > 0 else zero
        above = pltpu.roll(at(i + 1), 32, 1) if i < count - 1 else zero
        yl = jnp.where(y_bit == 1, pltpu.roll(centre, 32, 1), below)
        yu = jnp.where(y_bit == 0, pltpu.roll(centre, lanes - 32, 1), above)
        zl = jnp.where(z == 0, 0.0, pltpu.roll(centre, 1, 1))
        zu = jnp.where(z == 31, 0.0, pltpu.roll(centre, lanes - 1, 1))
        return centre, (xl, xu, yl, yu, zl, zu)

    def neighbours4(at, i):
        centre = at(i)
        xl = jnp.where(row == 0, 0.0, pltpu.roll(centre, 1, 0))
        xu = jnp.where(row == rows - 1, 0.0, pltpu.roll(centre, rows - 1, 0))
        yl = at(i - 1) if i > 0 else zero
        yu = at(i + 1) if i < count - 1 else zero
        zl = jnp.where(z < 2, 0.0, pltpu.roll(centre, 2, 1))
        zu = jnp.where(z >= 30, 0.0, pltpu.roll(centre, lanes - 2, 1))
        return centre, (xl, xu, yl, yu, zl, zu)

    def level(scale, neighbours, f_at, m_at, faces, weight, diag, ua, ub, residual):
        half = 0.5 * scale
        for i in range(count):
            centre, near = neighbours(m_at, i)
            total = jnp.full(shape, mass_term, jnp.float32)
            for k in range(6):
                face = half * (centre + near[k])
                faces[k, i] = face
                total = total + face
            diag[i] = total
            weight[i] = damping / total
            for c in range(3):
                ua[c, i] = weight[i] * f_at(c, i)
        for source, target in ((ua, ub), (ub, ua)):
            for i in range(count):
                for c in range(3):
                    centre, near = neighbours(lambda j: source[c, j], i)
                    flux = faces[0, i] * near[0]
                    for k in range(1, 6):
                        flux = flux + faces[k, i] * near[k]
                    target[c, i] = (1.0 - damping) * centre + weight[i] * (f_at(c, i) + flux)
        for i in range(count):
            for c in range(3):
                centre, near = neighbours(lambda j: ua[c, j], i)
                flux = faces[0, i] * near[0]
                for k in range(1, 6):
                    flux = flux + faces[k, i] * near[k]
                residual(c, i, f_at(c, i) + flux - diag[i] * centre)

    def pool(value):
        value = value + pltpu.roll(value, 64, 1)
        value = value + pltpu.roll(value, 32, 1)
        return 0.125 * (value + pltpu.roll(value, lanes - 1, 1))

    def to_level4(c, i, value):
        f4[c, i] = pool(value)

    level(0.25**3, neighbours3, lambda c, i: g[i, c], lambda i: g[i, 3],
          faces, weight, diag, ua, ub, to_level4)
    for i in range(count):
        m4[i] = pool(g[i, 3])

    def keep(c, i, value):
        vb[c, i] = value

    level(0.25**4, neighbours4, lambda c, i: f4[c, i], lambda i: m4[i],
          faces4, weight4, diag4, va, vb, keep)
    x_at, y_at = place[0], place[1]
    mine = row == x_at
    for c in range(3):
        u3_out[c:c + 1] = jnp.sum(jnp.where(mine, ua[c, y_at], 0.0), axis=0, keepdims=True)
        u4_out[c:c + 1] = jnp.sum(jnp.where(mine, va[c, y_at], 0.0), axis=0, keepdims=True)
        r4_out[c:c + 1] = jnp.sum(jnp.where(mine, vb[c, y_at], 0.0), axis=0, keepdims=True)


def on_chip(count):
    return [pl.BlockSpec(memory_space=pltpu.VMEM)] * count


def planes_scratch(planes, rows, lanes, own, own_rows, pooled):
    block = (planes, rows, lanes)
    return (
        [pltpu.VMEM((3,) + block, jnp.float32)] * 3
        + [pltpu.VMEM(block, jnp.float32)] * 8
        + [pltpu.VMEM((4, own // 2, own_rows, lanes), jnp.float32), pltpu.VMEM(pooled, jnp.float32)]
    )


LIMIT = pltpu.CompilerParams(vmem_limit_bytes=48 * 1024 * 1024)


def on_device(velocity_guess, forcing, cell_type, viscosities):
    f32 = jnp.float32
    viscosity = jnp.where(
        cell_type < 2,
        jnp.where(cell_type == 0, viscosities[0], viscosities[1]),
        jnp.where(cell_type == 2, viscosities[2], viscosities[3]),
    )
    own, rows, lanes = viscosity.shape
    stacked = jnp.concatenate([velocity_guess, forcing, viscosity[None]], axis=0)
    ylo = passed_along(stacked[:, :, rows - HALO:], "gy", 1)
    yhi = passed_along(stacked[:, :, :HALO], "gy", -1)

    def wide(lo, width_u, width_f, low_side):
        def layers(channels, width):
            first = own - width if low_side else 0
            chosen = slice(first, first + width)
            part = jnp.concatenate(
                [stacked[channels, chosen], yhi[channels, chosen], ylo[channels, chosen]], axis=2
            )
            return part.reshape(-1, rows + 2 * HALO, lanes)

        return jnp.concatenate(
            [layers(slice(0, 3), width_u), layers(slice(3, 6), width_f), layers(slice(6, 7), width_u)], axis=0
        )

    xlo = passed_along(wide(0, HALO, HALO - 1, True), "gx", 1)
    xhi = passed_along(wide(0, HALO, HALO - 1, False), "gx", -1)
    u0, packet = pl.pallas_call(
        fine_kernel,
        out_shape=(
            jax.ShapeDtypeStruct(velocity_guess.shape, f32),
            jax.ShapeDtypeStruct((4 * own // 2, rows // 2, lanes // 2), f32),
        ),
        in_specs=on_chip(7),
        out_specs=tuple(on_chip(2)),
        scratch_shapes=planes_scratch(
            own + 2 * HALO, rows + 2 * HALO, lanes, own, rows, (4 * own // 2, rows, 128)
        ),
        compiler_params=LIMIT,
    )(velocity_guess, forcing, viscosity, ylo, yhi, xlo, xhi)
    results = [u0]
    for grid_level in (1, 2):
        own, rows = own // 2, rows // 2
        packet = packet.reshape(4, own, rows, 128)
        valid = 256 >> grid_level
        ylo = passed_along(packet[:, :, rows - HALO:], "gy", 1)
        yhi = passed_along(packet[:, :, :HALO], "gy", -1)
        parts = [packet, yhi, ylo]
        total_rows = rows + 2 * HALO
        if total_rows % 8:
            parts = [packet, yhi, jnp.zeros_like(yhi), ylo]
            total_rows += HALO
        tall = jnp.concatenate(parts, axis=2)
        xlo = passed_along(tall[:, own - HALO:], "gx", 1)
        xhi = passed_along(tall[:, :HALO], "gx", -1)
        if grid_level == 1:
            packet_shape, pooled_shape = (4 * own // 2, rows // 2, 128), (4 * own // 2, rows, 128)
        else:
            packet_shape, pooled_shape = (4, 128), (8, 512)
        u_own, packet = pl.pallas_call(
            functools.partial(middle_kernel, 0.25**grid_level),
            out_shape=(
                jax.ShapeDtypeStruct((3, own, rows, valid), f32),
                jax.ShapeDtypeStruct(packet_shape, f32),
            ),
            in_specs=on_chip(5),
            out_specs=tuple(on_chip(2)),
            scratch_shapes=planes_scratch(own + 2 * HALO, total_rows, 128, own, rows, pooled_shape),
            compiler_params=LIMIT,
        )(packet, ylo, yhi, xlo, xhi)
        results.append(u_own)
    count_x, count_y = lax.axis_size("gx"), lax.axis_size("gy")
    column = lax.all_to_all(jnp.broadcast_to(packet[None], (count_x, 4, 128)), "gx", 0, 0)
    column = column.transpose(1, 0, 2)
    gathered = lax.all_to_all(
        jnp.broadcast_to(column[None], (count_y, 4, count_x, 128)), "gy", 0, 0
    )
    place = jnp.stack([lax.axis_index("gx"), lax.axis_index("gy")]).astype(jnp.int32)
    block = (count_y, count_x, 128)
    field, vector, six = (pltpu.VMEM(lead + block, f32) for lead in ((), (3,), (6,)))
    u3, u4, r4 = pl.pallas_call(
        last_kernel,
        out_shape=(jax.ShapeDtypeStruct((3, 128), f32),) * 3,
        in_specs=[pl.BlockSpec(memory_space=pltpu.SMEM)] + on_chip(1),
        out_specs=tuple(on_chip(3)),
        scratch_shapes=[vector, vector, vector, field, six, field, field,
                        vector, field, six, field, field, vector, vector],
        compiler_params=LIMIT,
    )(place, gathered)
    results.append(u3.reshape(3, 2, 2, 32))
    results.append(u4[:, :32:2].reshape(3, 1, 1, 16))
    return (*results, r4[:, :32:2].reshape(3, 1, 1, 16))


def solution(mesh):
    return jax.shard_map(
        on_device,
        mesh=mesh,
        in_specs=(P(None, "gx", "gy", None), P(None, "gx", "gy", None), P("gx", "gy", None), P()),
        out_specs=(P(None, "gx", "gy", None),) * 6,
        check_vma=False,
    )
```

time: 570 us -> 156 us (0.27); the launches traced: 561 us -> 155 us
  waiting for transfers between devices: 196 us -> 44.3 us
  local copies, waits for them, and re-layouts: 136 us -> 4.5 us
  starting transfers between devices: 171 us -> 43.2 us
  other arithmetic: 55 us -> 8.27 us
  Pallas kernels: 0 us -> 34.9 us
  blocking collectives: 0 us -> 18.7 us
    concatenate x9 -> x1, local copies, waits for them, and re-layouts: 128 us -> 0.07 us  [on_device(): tall = jnp.concatenate(parts, axis=2)]
    ppermute x48 -> x12, waiting for transfers between devices: 127 us -> 32.6 us  [passed_along(): lax.ppermute(value, axis, [(source, source + steps) for source in range(i...]
    ppermute x48 -> x12, starting transfers between devices: 117 us -> 32.5 us  [passed_along(): lax.ppermute(value, axis, [(source, source + steps) for source in range(i...]
    ppermute x24 -> x0, waiting for transfers between devices: 68.8 us -> none  [the longest x8 46.4 us: swapped(): return lax.ppermute(block, axis, route)]
    ppermute x24 -> x0, starting transfers between devices: 54 us -> none  [the longest x8 25.8 us: with_halo(): before = lax.ppermute(last, axis, up)]
    pallas_call x0 -> x4, Pallas kernels: none -> 34.9 us  [the longest x1 16.6 us: on_device(): pl.pallas_call(last_kernel, out_shape=(jax.ShapeDtypeStruct((3, 128), f32...]
    reduce_sum x5 -> x0, other arithmetic: 27 us -> none  [the longest x4 25.9 us: restrict(): values.reshape(channels, rows_x // 2, 2, rows_y // 2, 2, rows_z // 2, 2)]
    all_to_all x0 -> x1, blocking collectives: none -> 18.7 us  [on_device(): lax.all_to_all(jnp.broadcast_to(packet[None], (count_x, 4, 128)), 'gx', 0...]
  transfers between devices with their start and end apart: 72 -> 13, of which waited for: 56 -> 13; matrix products, arithmetic and copies ran while one was open for 6% -> 2% of each run, Pallas kernels for 0% -> 0%
where the time goes in v1:
time: 156 us; the launch traced here: 155 us
  waiting for transfers between devices  44.3 us (28%)
  starting transfers between devices  43.2 us (28%)
  Pallas kernels  34.9 us (22%)
  blocking collectives  18.7 us (12%)
  other arithmetic  8.27 us (5%)
  local copies, waits for them, and re-layouts  4.5 us (3%)
    ppermute x12, waiting for transfers between devices, passed_along(): lax.ppermute(value, axis, [(source, source + steps) for source in range(i...  32.6 us
    ppermute x12, starting transfers between devices, passed_along(): lax.ppermute(value, axis, [(source, source + steps) for source in range(i...  32.5 us
    all_to_all x1, blocking collectives, on_device(): lax.all_to_all(jnp.broadcast_to(packet[None], (count_x, 4, 128)), 'gx', 0...  18.7 us
    pallas_call x1, Pallas kernels, on_device(): pl.pallas_call(last_kernel, out_shape=(jax.ShapeDtypeStruct((3, 128), f32...  16.6 us
    all_to_all x1, waiting for transfers between devices, on_device(): lax.all_to_all(jnp.broadcast_to(column[None], (count_y, 4, count_x, 128))...  11.7 us
    pallas_call x1, Pallas kernels, on_device(): pl.pallas_call(fine_kernel, out_shape=(jax.ShapeDtypeStruct(velocity_gues...  11.3 us
    all_to_all x1, starting transfers between devices, on_device(): lax.all_to_all(jnp.broadcast_to(column[None], (count_y, 4, count_x, 128))...  10.7 us
    pallas_call x2, Pallas kernels, on_device(): pl.pallas_call(functools.partial(middle_kernel, 0.25 ** grid_level), out_...  7.04 us
  transfers between devices with their start and end apart: 13, of which 13 were waited for; matrix products, arithmetic and copies ran while one was open for 2% of the time, Pallas kernels for 0%

profile of v1, /device:TPU:32, one launch (start us, length us, event | category | flops | bytes accessed | tf_op | source)
XLA Modules:
  0.0 154.8 jit_solution(14486993349325932468)
XLA Ops:
  0.6 1.4 fusion.11
  2.0 3.6 %fusion.12 = f32[1,16,16,256]{3,2,1,0:T(8,128)S(1)} fusion(f32[]{:T(128)} %bitcast.3, f32[]{:T(128)} %bitcast.2, s32[16,16,256]{2,1,0:T(8,128)} %param.6, f32[]{:T(128)} %bitcast.1, f32[]{:T(128)} %bitcast), kind=kLoop, calls=%fused_computation.27 | loop fusion | flops 393216 | bytes 524304 | tf_op jit(solution)/shard_map/broadcast_in_dim | solution.py:312
  5.6 1.6 %pad_maximum_fusion.2 = (f32[7,16,4,256]{3,2,1,0:T(4,128)S(1)}, f32[7,16,4,256]{3,2,1,0:T(4,128)S(1)}) fusion(f32[1,16,16,256]{3,2,1,0:T(8,128)S(1)} %fusion.12, f32[3,16,16,256]{3,2,1,0:T(8,128)} %f_in.1, f32[3,16,16,256]{3,2,1,0:T(8,128)} %u_in.1), kind=kLoop, calls=%fused_computation.2 | loop fusion | flops 458752 | bytes 2752512 | tf_op jit(solution)/shard_map/concatenate | solution.py:312
  7.3 1.4 collective-permute-start.1
  8.7 4.6 %collective-permute-start = (f32[7,16,4,256]{3,2,1,0:T(4,128)S(1)}, f32[7,16,4,256]{3,2,1,0:T(4,128)S(1)}, u32[]{:S(2)}, u32[]{:S(2)}) collective-permute-start(f32[7,16,4,256]{3,2,1,0:T(4,128)S(1)} %get-tuple-element.37), channel_id=1, source_target_pairs={{0,1},{1,2},{2,3},{3,4},{4,5},{5,6},{6,7},{7,8},{8,9},{9,10},{10,1... | collective-permute-start | bytes 1376264 | tf_op jit(solution)/shard_map/ppermute | solution.py:21
  13.4 8.2 %collective-permute-done.1.yhi = f32[7,16,4,256]{3,2,1,0:T(4,128)S(1)} collective-permute-done((f32[7,16,4,256]{3,2,1,0:T(4,128)S(1)}, f32[7,16,4,256]{3,2,1,0:T(4,128)S(1)}, u32[]{:S(2)}, u32[]{:S(2)}) %collective-permute-start.1) | collective-permute-done | bytes 458784 | tf_op jit(solution)/shard_map/ppermute | solution.py:21
  21.6 1.2 collective-permute-done.ylo
  23.0 1.9 %collective-permute-start.3 = (f32[25,24,256]{2,1,0:T(8,128)S(1)}, f32[25,24,256]{2,1,0:T(8,128)S(1)}, u32[]{:S(2)}, u32[]{:S(2)}) collective-permute-start(f32[25,24,256]{2,1,0:T(8,128)S(1)} %pad_maximum_fusion.1), channel_id=1, source_target_pairs={{16,0},{32,16},{48,32},{64,48},{80,64},{96,80},{112,96},{128,112},... | collective-permute-start | bytes 1843208 | tf_op jit(solution)/shard_map/ppermute | solution.py:21
  25.0 2.5 %collective-permute-start.2 = (f32[25,24,256]{2,1,0:T(8,128)S(1)}, f32[25,24,256]{2,1,0:T(8,128)S(1)}, u32[]{:S(2)}, u32[]{:S(2)}) collective-permute-start(f32[25,24,256]{2,1,0:T(8,128)S(1)} %pad_maximum_fusion), channel_id=1, source_target_pairs={{0,16},{16,32},{32,48},{48,64},{64,80},{80,96},{96,112},{112,128},... | collective-permute-start | bytes 1843208 | tf_op jit(solution)/shard_map/ppermute | solution.py:21
  27.6 2.6 %select_select_fusion.m_in = f32[16,16,256]{2,1,0:T(8,128)S(1)} fusion(s32[16,16,256]{2,1,0:T(8,128)S(1)} %copy-done.2, f32[]{:T(128)} %bitcast.3, f32[]{:T(128)} %bitcast.2, f32[]{:T(128)} %bitcast.1, f32[]{:T(128)} %bitcast), kind=kLoop, calls=%fused_computation.8 | loop fusion | flops 393216 | bytes 524304 | tf_op jit(solution)/shard_map/jit(_where)/select_n | solution.py:306
  30.2 2.4 %collective-permute-done.3.xhi = f32[25,24,256]{2,1,0:T(8,128)S(1)} collective-permute-done((f32[25,24,256]{2,1,0:T(8,128)S(1)}, f32[25,24,256]{2,1,0:T(8,128)S(1)}, u32[]{:S(2)}, u32[]{:S(2)}) %collective-permute-start.3) | collective-permute-done | bytes 614432 | tf_op jit(solution)/shard_map/ppermute | solution.py:21
  32.6 4.0 %collective-permute-done.2.xlo = f32[25,24,256]{2,1,0:T(8,128)S(1)} collective-permute-done((f32[25,24,256]{2,1,0:T(8,128)S(1)}, f32[25,24,256]{2,1,0:T(8,128)S(1)}, u32[]{:S(2)}, u32[]{:S(2)}) %collective-permute-start.2) | collective-permute-done | bytes 614432 | tf_op jit(solution)/shard_map/ppermute | solution.py:21
  36.6 11.3 %shard_map.91 = (f32[3,16,16,256]{3,2,1,0:T(8,128)}, f32[32,8,128]{2,1,0:T(8,128)S(1)}) custom-call(f32[3,16,16,256]{3,2,1,0:T(8,128)S(1)} %copy-done, f32[3,16,16,256]{3,2,1,0:T(8,128)S(1)} %copy-done.1, f32[16,16,256]{2,1,0:T(8,128)S(1)} %select_select_fusion.m_in, f32[7,16,4,256]{3,2,1,0:T(4,128)S(1)} %collective-permute-done.ylo, ...), custom_call_target="tpu_custom_call" | custom-call | tf_op jit(solution)/shard_map/pallas_call | solution.py:331
  47.9 4.4 %collective-permute-start.4 = (f32[4,8,4,128]{3,2,1,0:T(4,128)S(1)}, f32[4,8,4,128]{3,2,1,0:T(4,128)S(1)}, u32[]{:S(2)}, u32[]{:S(2)}) collective-permute-start(f32[4,8,4,128]{3,2,1,0:T(4,128)S(1)} %get-tuple-element.59), channel_id=1, source_target_pairs={{0,1},{1,2},{2,3},{3,4},{4,5},{5,6},{6,7},{7,8},{8,9},{9,10},{10,1... | collective-permute-start | bytes 196616 | tf_op jit(solution)/shard_map/ppermute | solution.py:21
  52.3 1.3 collective-permute-start.5
  54.2 4.3 %collective-permute-done.5.yhi = f32[4,8,4,128]{3,2,1,0:T(4,128)S(1)} collective-permute-done((f32[4,8,4,128]{3,2,1,0:T(4,128)S(1)}, f32[4,8,4,128]{3,2,1,0:T(4,128)S(1)}, u32[]{:S(2)}, u32[]{:S(2)}) %collective-permute-start.5) | collective-permute-done | bytes 65568 | tf_op jit(solution)/shard_map/ppermute | solution.py:21
  58.5 1.9 %collective-permute-start.6 = (f32[4,4,16,128]{3,2,1,0:T(8,128)S(1)}, f32[4,4,16,128]{3,2,1,0:T(8,128)S(1)}, u32[]{:S(2)}, u32[]{:S(2)}) collective-permute-start(f32[4,4,16,128]{3,2,1,0:T(8,128)S(1)} %get-tuple-element.55), channel_id=1, source_target_pairs={{0,16},{16,32},{32,48},{48,64},{64,80},{80,96},{96,112},{112,128},... | collective-permute-start | bytes 393224 | tf_op jit(solution)/shard_map/ppermute | solution.py:21
  60.4 3.6 %collective-permute-start.7 = (f32[4,4,16,128]{3,2,1,0:T(8,128)S(1)}, f32[4,4,16,128]{3,2,1,0:T(8,128)S(1)}, u32[]{:S(2)}, u32[]{:S(2)}) collective-permute-start(f32[4,4,16,128]{3,2,1,0:T(8,128)S(1)} %get-tuple-element.54), channel_id=1, source_target_pairs={{16,0},{32,16},{48,32},{64,48},{80,64},{96,80},{112,96},{128,112},... | collective-permute-start | bytes 393224 | tf_op jit(solution)/shard_map/ppermute | solution.py:21
  64.8 1.8 %collective-permute-done.7.xhi = f32[4,4,16,128]{3,2,1,0:T(8,128)S(1)} collective-permute-done((f32[4,4,16,128]{3,2,1,0:T(8,128)S(1)}, f32[4,4,16,128]{3,2,1,0:T(8,128)S(1)}, u32[]{:S(2)}, u32[]{:S(2)}) %collective-permute-start.7) | collective-permute-done | bytes 131104 | tf_op jit(solution)/shard_map/ppermute | solution.py:21
  66.6 4.2 %shard_map.92 = (f32[3,8,8,128]{3,2,1,0:T(8,128)}, f32[16,4,128]{2,1,0:T(4,128)S(1)}) custom-call(f32[4,8,8,128]{3,2,1,0:T(8,128)S(1)} %bitcast.23, f32[4,8,4,128]{3,2,1,0:T(4,128)S(1)} %collective-permute-done.4.ylo, f32[4,8,4,128]{3,2,1,0:T(4,128)S(1)} %collective-permute-done.5.yhi, f32[4,4,16,128]{3,2,1,0:T(8,128)S(1)} %collective-permute-done.6.xlo, ...), custom_call_target="tpu_custom_call" | custom-call | tf_op jit(solution)/shard_map/pallas_call | solution.py:363
  70.8 3.9 %collective-permute-start.8 = (f32[4,4,4,128]{3,2,1,0:T(4,128)S(1)}, f32[4,4,4,128]{3,2,1,0:T(4,128)S(1)}, u32[]{:S(2)}, u32[]{:S(2)}) collective-permute-start(f32[4,4,4,128]{3,2,1,0:T(4,128)S(1)} %bitcast.24), channel_id=1, source_target_pairs={{0,1},{1,2},{2,3},{3,4},{4,5},{5,6},{6,7},{7,8},{8,9},{9,10},{10,1... | collective-permute-start | bytes 98312 | tf_op jit(solution)/shard_map/ppermute | solution.py:21
  74.7 1.3 collective-permute-start.9
  76.3 6.8 %collective-permute-done.9.yhi = f32[4,4,4,128]{3,2,1,0:T(4,128)S(1)} collective-permute-done((f32[4,4,4,128]{3,2,1,0:T(4,128)S(1)}, f32[4,4,4,128]{3,2,1,0:T(4,128)S(1)}, u32[]{:S(2)}, u32[]{:S(2)}) %collective-permute-start.9) | collective-permute-done | bytes 32800 | tf_op jit(solution)/shard_map/ppermute | solution.py:21
  83.2 2.9 %collective-permute-start.10 = (f32[4,4,16,128]{3,2,1,0:T(8,128)S(1)}, f32[4,4,16,128]{3,2,1,0:T(8,128)S(1)}, u32[]{:S(2)}, u32[]{:S(2)}) collective-permute-start(f32[4,4,16,128]{3,2,1,0:T(8,128)S(1)} %pad_maximum_fusion.10), channel_id=1, source_target_pairs={{0,16},{16,32},{32,48},{48,64},{64,80},{80,96},{96,112},{112,128},... | collective-permute-start | bytes 393224 | tf_op jit(solution)/shard_map/ppermute | solution.py:21
  86.1 2.6 %collective-permute-start.11 = (f32[4,4,16,128]{3,2,1,0:T(8,128)S(1)}, f32[4,4,16,128]{3,2,1,0:T(8,128)S(1)}, u32[]{:S(2)}, u32[]{:S(2)}) collective-permute-start(f32[4,4,16,128]{3,2,1,0:T(8,128)S(1)} %pad_maximum_fusion.10), channel_id=1, source_target_pairs={{16,0},{32,16},{48,32},{64,48},{80,64},{96,80},{112,96},{128,112},... | collective-permute-start | bytes 393224 | tf_op jit(solution)/shard_map/ppermute | solution.py:21
  89.5 1.8 %collective-permute-done.11.xhi = f32[4,4,16,128]{3,2,1,0:T(8,128)S(1)} collective-permute-done((f32[4,4,16,128]{3,2,1,0:T(8,128)S(1)}, f32[4,4,16,128]{3,2,1,0:T(8,128)S(1)}, u32[]{:S(2)}, u32[]{:S(2)}) %collective-permute-start.11) | collective-permute-done | bytes 131104 | tf_op jit(solution)/shard_map/ppermute | solution.py:21
  91.3 2.9 %shard_map.93 = (f32[3,4,4,64]{3,2,1,0:T(4,128)}, f32[4,128]{1,0:T(4,128)S(1)}) custom-call(f32[4,4,4,128]{3,2,1,0:T(4,128)S(1)} %bitcast.27, f32[4,4,4,128]{3,2,1,0:T(4,128)S(1)} %collective-permute-done.8.ylo, f32[4,4,4,128]{3,2,1,0:T(4,128)S(1)} %collective-permute-done.9.yhi, f32[4,4,16,128]{3,2,1,0:T(8,128)S(1)} %collective-permute-done.10.xlo, ...), custom_call_target="tpu_custom_call" | custom-call | tf_op jit(solution)/shard_map/pallas_call | solution.py:363
  94.1 18.7 %all_to_all.10 = f32[16,4,128]{2,1,0:T(4,128)S(1)} all-to-all(f32[16,4,128]{2,1,0:T(4,128)S(1)} %broadcast_in_dim.38), channel_id=1, replica_groups=mesh['gx'=16,'gy'=16] {'gx'}, dimensions={0} | all-to-all | bytes 65536 | tf_op jit(solution)/shard_map/all_to_all | solution.py:376
  112.8 0.8 broadcast_in_dim.39
  113.7 10.7 %all-to-all-start.1 = ((f32[16,4,16,128]{3,2,1,0:T(8,128)}), f32[16,4,16,128]{3,2,1,0:T(8,128)S(1)}, u32[]{:S(2)}, u32[]{:S(2)}) async-start(f32[16,4,16,128]{3,2,1,0:T(8,128)} %broadcast_in_dim.39), calls=%async_computation.1 | async-start | bytes 1048576 | tf_op jit(solution)/shard_map/all_to_all | solution.py:378
  124.4 11.7 %all-to-all-done.1.g = f32[16,4,16,128]{3,2,1,0:T(8,128)S(1)} async-done(((f32[16,4,16,128]{3,2,1,0:T(8,128)}), f32[16,4,16,128]{3,2,1,0:T(8,128)S(1)}, u32[]{:S(2)}, u32[]{:S(2)}) %all-to-all-start.1) | async-done | bytes 524320 | tf_op jit(solution)/shard_map/all_to_all | solution.py:378
  136.1 16.6 %shard_map.94 = (f32[3,128]{1,0:T(4,128)S(1)}, f32[3,128]{1,0:T(4,128)S(1)}, f32[3,128]{1,0:T(4,128)S(1)}) custom-call(s32[2]{0:T(128)S(1)} %pad_add_fusion.place, f32[16,4,16,128]{3,2,1,0:T(8,128)S(1)} %all-to-all-done.1.g), custom_call_target="tpu_custom_call" | custom-call | tf_op jit(solution)/shard_map/pallas_call | solution.py:384
  (39 shorter events, 4.9 us)
Async XLA Ops:
  5.6 7.7 %copy-start = (f32[3,16,16,256]{3,2,1,0:T(8,128)S(1)}, f32[3,16,16,256]{3,2,1,0:T(8,128)}, u32[]{:S(2)}) copy-start(f32[3,16,16,256]{3,2,1,0:T(8,128)} %u_in.1) | copy-start | bytes 2359300
  7.3 6.1 %copy-start.1 = (f32[3,16,16,256]{3,2,1,0:T(8,128)S(1)}, f32[3,16,16,256]{3,2,1,0:T(8,128)}, u32[]{:S(2)}) copy-start(f32[3,16,16,256]{3,2,1,0:T(8,128)} %f_in.1) | copy-start | bytes 2359300
  7.3 14.3 %collective-permute-start.1 = (f32[7,16,4,256]{3,2,1,0:T(4,128)S(1)}, f32[7,16,4,256]{3,2,1,0:T(4,128)S(1)}, u32[]{:S(2)}, u32[]{:S(2)}) collective-permute-start(f32[7,16,4,256]{3,2,1,0:T(4,128)S(1)} %get-tuple-element.36), channel_id=1, source_target_pairs={{1,0},{2,1},{3,2},{4,3},{5,4},{6,5},{7,6},{8,7},{9,8},{10,9},{11,1... | collective-permute-start | bytes 1376264 | tf_op jit(solution)/shard_map/ppermute | solution.py:21
  8.7 14.0 %collective-permute-start = (f32[7,16,4,256]{3,2,1,0:T(4,128)S(1)}, f32[7,16,4,256]{3,2,1,0:T(4,128)S(1)}, u32[]{:S(2)}, u32[]{:S(2)}) collective-permute-start(f32[7,16,4,256]{3,2,1,0:T(4,128)S(1)} %get-tuple-element.37), channel_id=1, source_target_pairs={{0,1},{1,2},{2,3},{3,4},{4,5},{5,6},{6,7},{7,8},{8,9},{9,10},{10,1... | collective-permute-start | bytes 1376264 | tf_op jit(solution)/shard_map/ppermute | solution.py:21
  23.0 9.6 %collective-permute-start.3 = (f32[25,24,256]{2,1,0:T(8,128)S(1)}, f32[25,24,256]{2,1,0:T(8,128)S(1)}, u32[]{:S(2)}, u32[]{:S(2)}) collective-permute-start(f32[25,24,256]{2,1,0:T(8,128)S(1)} %pad_maximum_fusion.1), channel_id=1, source_target_pairs={{16,0},{32,16},{48,32},{64,48},{80,64},{96,80},{112,96},{128,112},... | collective-permute-start | bytes 1843208 | tf_op jit(solution)/shard_map/ppermute | solution.py:21
  25.0 2.6 %copy-start.2 = (s32[16,16,256]{2,1,0:T(8,128)S(1)}, s32[16,16,256]{2,1,0:T(8,128)}, u32[]{:S(2)}) copy-start(s32[16,16,256]{2,1,0:T(8,128)} %param.6) | copy-start | bytes 786436
  25.0 11.6 %collective-permute-start.2 = (f32[25,24,256]{2,1,0:T(8,128)S(1)}, f32[25,24,256]{2,1,0:T(8,128)S(1)}, u32[]{:S(2)}, u32[]{:S(2)}) collective-permute-start(f32[25,24,256]{2,1,0:T(8,128)S(1)} %pad_maximum_fusion), channel_id=1, source_target_pairs={{0,16},{16,32},{32,48},{48,64},{64,80},{80,96},{96,112},{112,128},... | collective-permute-start | bytes 1843208 | tf_op jit(solution)/shard_map/ppermute | solution.py:21
  47.9 6.3 %collective-permute-start.4 = (f32[4,8,4,128]{3,2,1,0:T(4,128)S(1)}, f32[4,8,4,128]{3,2,1,0:T(4,128)S(1)}, u32[]{:S(2)}, u32[]{:S(2)}) collective-permute-start(f32[4,8,4,128]{3,2,1,0:T(4,128)S(1)} %get-tuple-element.59), channel_id=1, source_target_pairs={{0,1},{1,2},{2,3},{3,4},{4,5},{5,6},{6,7},{7,8},{8,9},{9,10},{10,1... | collective-permute-start | bytes 196616 | tf_op jit(solution)/shard_map/ppermute | solution.py:21
  52.3 6.2 %collective-permute-start.5 = (f32[4,8,4,128]{3,2,1,0:T(4,128)S(1)}, f32[4,8,4,128]{3,2,1,0:T(4,128)S(1)}, u32[]{:S(2)}, u32[]{:S(2)}) collective-permute-start(f32[4,8,4,128]{3,2,1,0:T(4,128)S(1)} %get-tuple-element.58), channel_id=1, source_target_pairs={{1,0},{2,1},{3,2},{4,3},{5,4},{6,5},{7,6},{8,7},{9,8},{10,9},{11,1... | collective-permute-start | bytes 196616 | tf_op jit(solution)/shard_map/ppermute | solution.py:21
  58.5 6.3 %collective-permute-start.6 = (f32[4,4,16,128]{3,2,1,0:T(8,128)S(1)}, f32[4,4,16,128]{3,2,1,0:T(8,128)S(1)}, u32[]{:S(2)}, u32[]{:S(2)}) collective-permute-start(f32[4,4,16,128]{3,2,1,0:T(8,128)S(1)} %get-tuple-element.55), channel_id=1, source_target_pairs={{0,16},{16,32},{32,48},{48,64},{64,80},{80,96},{96,112},{112,128},... | collective-permute-start | bytes 393224 | tf_op jit(solution)/shard_map/ppermute | solution.py:21
  60.4 6.1 %collective-permute-start.7 = (f32[4,4,16,128]{3,2,1,0:T(8,128)S(1)}, f32[4,4,16,128]{3,2,1,0:T(8,128)S(1)}, u32[]{:S(2)}, u32[]{:S(2)}) collective-permute-start(f32[4,4,16,128]{3,2,1,0:T(8,128)S(1)} %get-tuple-element.54), channel_id=1, source_target_pairs={{16,0},{32,16},{48,32},{64,48},{80,64},{96,80},{112,96},{128,112},... | collective-permute-start | bytes 393224 | tf_op jit(solution)/shard_map/ppermute | solution.py:21
  70.8 5.5 %collective-permute-start.8 = (f32[4,4,4,128]{3,2,1,0:T(4,128)S(1)}, f32[4,4,4,128]{3,2,1,0:T(4,128)S(1)}, u32[]{:S(2)}, u32[]{:S(2)}) collective-permute-start(f32[4,4,4,128]{3,2,1,0:T(4,128)S(1)} %bitcast.24), channel_id=1, source_target_pairs={{0,1},{1,2},{2,3},{3,4},{4,5},{5,6},{6,7},{7,8},{8,9},{9,10},{10,1... | collective-permute-start | bytes 98312 | tf_op jit(solution)/shard_map/ppermute | solution.py:21
  74.7 8.4 %collective-permute-start.9 = (f32[4,4,4,128]{3,2,1,0:T(4,128)S(1)}, f32[4,4,4,128]{3,2,1,0:T(4,128)S(1)}, u32[]{:S(2)}, u32[]{:S(2)}) collective-permute-start(f32[4,4,4,128]{3,2,1,0:T(4,128)S(1)} %bitcast.25), channel_id=1, source_target_pairs={{1,0},{2,1},{3,2},{4,3},{5,4},{6,5},{7,6},{8,7},{9,8},{10,9},{11,1... | collective-permute-start | bytes 98312 | tf_op jit(solution)/shard_map/ppermute | solution.py:21
  83.2 6.3 %collective-permute-start.10 = (f32[4,4,16,128]{3,2,1,0:T(8,128)S(1)}, f32[4,4,16,128]{3,2,1,0:T(8,128)S(1)}, u32[]{:S(2)}, u32[]{:S(2)}) collective-permute-start(f32[4,4,16,128]{3,2,1,0:T(8,128)S(1)} %pad_maximum_fusion.10), channel_id=1, source_target_pairs={{0,16},{16,32},{32,48},{48,64},{64,80},{80,96},{96,112},{112,128},... | collective-permute-start | bytes 393224 | tf_op jit(solution)/shard_map/ppermute | solution.py:21
  86.1 5.2 %collective-permute-start.11 = (f32[4,4,16,128]{3,2,1,0:T(8,128)S(1)}, f32[4,4,16,128]{3,2,1,0:T(8,128)S(1)}, u32[]{:S(2)}, u32[]{:S(2)}) collective-permute-start(f32[4,4,16,128]{3,2,1,0:T(8,128)S(1)} %pad_maximum_fusion.10), channel_id=1, source_target_pairs={{16,0},{32,16},{48,32},{64,48},{80,64},{96,80},{112,96},{128,112},... | collective-permute-start | bytes 393224 | tf_op jit(solution)/shard_map/ppermute | solution.py:21
  113.7 22.5 %all-to-all-start.1 = ((f32[16,4,16,128]{3,2,1,0:T(8,128)}), f32[16,4,16,128]{3,2,1,0:T(8,128)S(1)}, u32[]{:S(2)}, u32[]{:S(2)}) async-start(f32[16,4,16,128]{3,2,1,0:T(8,128)} %broadcast_in_dim.39), calls=%async_computation.1 | async-start | bytes 1048576 | tf_op jit(solution)/shard_map/all_to_all | solution.py:378

commit v2 on v1

v2 whole, which is shorter than its diff:
```python
import functools

import jax
import jax.numpy as jnp
from jax import lax
from jax.experimental import pallas as pl
from jax.experimental.pallas import tpu as pltpu
from jax.sharding import PartitionSpec as P

SWEEPS = 3
LEVELS = 4
HALO = SWEEPS + 1
REACH = 5

damping = 0.8
mass_term = 0.05


def passed_round(value, axis, steps):
    count = lax.axis_size(axis)
    return lax.ppermute(value, axis, [(source, (source + steps) % count) for source in range(count)])


def split_dot(rows, pool):
    total = None
    for part in range(3):
        piece = rows.astype(jnp.bfloat16)
        term = jnp.dot(piece, pool, preferred_element_type=jnp.float32)
        total = term if total is None else total + term
        if part < 2:
            rows = rows - piece.astype(jnp.float32)
    return total


def inside_rows(place, own_rows, total_rows, shape, along_x=True):
    row = lax.broadcasted_iota(jnp.int32, shape, 0)
    above = jnp.where(place[1] < place[3] - 1, own_rows + HALO, own_rows)
    below = jnp.where(place[1] > 0, total_rows - HALO, total_rows)
    above = jnp.where(along_x, above, 0)
    below = jnp.where(along_x, below, total_rows)
    return (row < above) | (row >= below)


def pair_pool(lanes):
    source = lax.broadcasted_iota(jnp.int32, (lanes, 128), 0)
    target = lax.broadcasted_iota(jnp.int32, (lanes, 128), 1)
    return jnp.where(source // 2 == target, 0.125, 0.0).astype(jnp.bfloat16)


def make_coefficients(scale, lo, hi, m, cx, cym, cyp, czm, czp, weight, diag, unroll=False):
    rows, lanes = m.shape[1:]
    half = 0.5 * scale
    lane = lax.broadcasted_iota(jnp.int32, (rows, lanes), 1)
    cx[lo - 1] = half * (m[lo - 1] + m[lo])

    def plane(i, _):
        centre = m[i]
        upper = m[i + 1]
        y_lower = pltpu.roll(centre, 1, 0)
        y_upper = pltpu.roll(centre, rows - 1, 0)
        z_lower = jnp.where(lane == 0, 0.0, pltpu.roll(centre, 1, 1))
        z_upper = jnp.where(lane == lanes - 1, 0.0, pltpu.roll(centre, lanes - 1, 1))
        f_xl, f_xu = half * (centre + m[i - 1]), half * (centre + upper)
        f_yl, f_yu = half * (centre + y_lower), half * (centre + y_upper)
        f_zl, f_zu = half * (centre + z_lower), half * (centre + z_upper)
        total = mass_term + (f_xl + f_xu + f_yl + f_yu + f_zl + f_zu)
        cx[i] = f_xu
        cym[i], cyp[i] = f_yl, f_yu
        czm[i] = jnp.where(lane == 0, 0.0, f_zl)
        czp[i] = jnp.where(lane == lanes - 1, 0.0, f_zu)
        diag[i] = total
        weight[i] = jnp.where(centre > 0.0, damping / total, 0.0)
        return 0

    lax.fori_loop(lo, hi, plane, 0, unroll=unroll)


def flux_of(u, c, i, cx, cym, cyp, czm, czp):
    rows, lanes = u.shape[2:]
    centre = u[c, i]
    flux = cx[i - 1] * u[c, i - 1] + cx[i] * u[c, i + 1]
    flux += cym[i] * pltpu.roll(centre, 1, 0) + cyp[i] * pltpu.roll(centre, rows - 1, 0)
    flux += czm[i] * pltpu.roll(centre, 1, 1) + czp[i] * pltpu.roll(centre, lanes - 1, 1)
    return centre, flux


def relax(lo, hi, source, target, f, weight, faces, unroll=False):
    def plane(i, _):
        for c in range(3):
            centre, flux = flux_of(source, c, i, *faces)
            target[c, i] = (1.0 - damping) * centre + weight[i] * (f[c, i] + flux)
        return 0

    lax.fori_loop(lo, hi, plane, 0, unroll=unroll)


def start_from_zero(lo, hi, target, f, weight, unroll=False):
    def plane(i, _):
        for c in range(3):
            target[c, i] = weight[i] * f[c, i]
        return 0

    lax.fori_loop(lo, hi, plane, 0, unroll=unroll)


def residual_pairs(at, count, first, own_rows, u, f, m, diag, faces, pairs, unroll=False):
    def pair(p, _):
        i = at + 2 * p
        for c in range(3):
            both = None
            for j in (i, i + 1):
                centre, flux = flux_of(u, c, j, *faces)
                value = f[c, j] + flux - diag[j] * centre
                both = value if both is None else both + value
            pairs[c, first + p] = both[:own_rows]
        pairs[3, first + p] = (m[i] + m[i + 1])[:own_rows]
        return 0

    lax.fori_loop(0, count, pair, 0, unroll=unroll)


def pool_pairs(pairs, pooled):
    lanes = pairs.shape[-1]
    rows = pooled.shape[1]
    summed = split_dot(pairs[...].reshape(-1, lanes), pair_pool(lanes))
    pooled[...] = summed.reshape(pooled.shape)
    return pooled[:, pl.ds(0, rows // 2, 2), :] + pooled[:, pl.ds(1, rows // 2, 2), :]


def inner_kernel(place, u_in, f_in, m_in, ylo, yhi, u_mid, packet_mid, u_edge, f_edge, m_edge,
                 ua, ub, f, m, cx, cym, cyp, czm, czp, weight, diag, pairs, pooled):
    own, rows = u_in.shape[1:3]
    body = pl.ds(HALO, own)
    last = HALO + own
    has_lower, has_upper = place[1] > 0, place[1] < place[3] - 1
    for c in range(3):
        ua[c, body, :rows] = u_in[c]
        ua[c, body, rows:rows + HALO] = jnp.where(has_upper, yhi[c], 0.0)
        ua[c, body, rows + HALO:] = jnp.where(has_lower, ylo[c], 0.0)
        f[c, body, :rows] = f_in[c]
        f[c, body, rows:rows + HALO] = yhi[3 + c]
        f[c, body, rows + HALO:] = ylo[3 + c]
    m[body, :rows] = m_in[...]
    m[body, rows:rows + HALO] = jnp.where(has_upper, yhi[6], 0.0)
    m[body, rows + HALO:] = jnp.where(has_lower, ylo[6], 0.0)

    def edges(stage, u, depth):
        u_edge[stage, 0] = u[:, HALO + depth:HALO + depth + 2]
        u_edge[stage, 1] = u[:, last - depth - 2:last - depth]

    edges(0, ua, 0)
    f_edge[0], f_edge[1] = f[:, HALO:2 * HALO], f[:, last - HALO:last]
    m_edge[0], m_edge[1] = m[HALO:2 * HALO + 1], m[last - HALO - 1:last]
    make_coefficients(1.0, HALO + 1, last - 1, m, cx, cym, cyp, czm, czp, weight, diag)
    faces = (cx, cym, cyp, czm, czp)
    relax(HALO + 1, last - 1, ua, ub, f, weight, faces)
    edges(1, ub, 1)
    relax(HALO + 2, last - 2, ub, ua, f, weight, faces)
    edges(2, ua, 2)
    relax(HALO + 3, last - 3, ua, ub, f, weight, faces)
    edges(3, ub, 3)
    u_mid[...] = ub[:, HALO + 3:last - 3, :rows]
    residual_pairs(2 * HALO, own // 2 - HALO, 0, rows, ub, f, m, diag, faces, pairs)
    packet_mid[...] = pool_pairs(pairs, pooled)


def outer_kernel(place, u_mid, packet_mid, u_edge, f_edge, m_edge, xlo, xhi, u_out, packet,
                 ua, ub, f, m, cx, cym, cyp, czm, czp, weight, diag, pairs, pooled):
    own, rows = u_out.shape[1:3]
    planes = m.shape[1]
    count_f = HALO - 1
    at_f, at_m = 3 * HALO, 3 * HALO + 3 * count_f
    half = own // 2
    for end, halo in ((0, xlo), (1, xhi)):
        outer = 0 if end == 0 else planes - HALO
        inner = HALO if end == 0 else 0
        present = place[0] > 0 if end == 0 else place[0] < place[2] - 1
        inside = inside_rows(place, rows, m.shape[2], m.shape[2:], present)
        for c in range(3):
            ua[end, c, outer:outer + HALO] = jnp.where(inside, halo[HALO * c:HALO * (c + 1)], 0.0)
            nearest = HALO if end == 0 else planes - HALO - 2
            ua[end, c, nearest:nearest + 2] = u_edge[0, end, c]
            beyond = 1 if end == 0 else planes - HALO
            f[end, c, beyond:beyond + count_f] = halo[at_f + count_f * c:at_f + count_f * (c + 1)]
            own_f = HALO if end == 0 else planes - 2 * HALO
            f[end, c, own_f:own_f + HALO] = f_edge[end, c]
        m[end, outer:outer + HALO] = jnp.where(inside, halo[at_m:], 0.0)
        m[end, inner:inner + HALO + 1] = m_edge[end]
        parts = (cx.at[end], cym.at[end], cyp.at[end], czm.at[end], czp.at[end])
        u_a, u_b, f_e, w_e, d_e = ua.at[end], ub.at[end], f.at[end], weight.at[end], diag.at[end]
        make_coefficients(1.0, 1, planes - 1, m.at[end], *parts, w_e, d_e)
        for stage, (source, target) in enumerate(((u_a, u_b), (u_b, u_a), (u_a, u_b))):
            first = 1 + stage if end == 0 else planes - 1 - HALO - stage
            relax(first, first + HALO, source, target, f_e, w_e, parts)
            known = first + HALO if end == 0 else first - 2
            for c in range(3):
                target[c, known:known + 2] = u_edge[stage + 1, end, c]
        at = HALO if end == 0 else 1
        residual_pairs(at, HALO // 2, HALO // 2 * end, rows, u_b, f_e, m.at[end], d_e, parts, pairs)
        for c in range(3):
            if end == 0:
                u_out[c, :HALO - 1] = ub[end, c, HALO:2 * HALO - 1, :rows]
            else:
                u_out[c, own - HALO + 1:] = ub[end, c, planes - 2 * HALO + 1:planes - HALO, :rows]
    u_out[:, HALO - 1:own - HALO + 1] = u_mid[...]
    ends = pool_pairs(pairs, pooled)
    for c in range(4):
        at = HALO * c
        packet[half * c:half * c + 2] = ends[at:at + 2]
        packet[half * c + 2:half * (c + 1) - 2] = packet_mid[(half - HALO) * c:(half - HALO) * (c + 1)]
        packet[half * (c + 1) - 2:half * (c + 1)] = ends[at + 2:at + 4]


def middle_kernel(scale, place, p_in, ylo, yhi, xlo, xhi, u_out, packet,
                  ua, ub, f, m, cx, cym, cyp, czm, czp, weight, diag, pairs, pooled):
    own, rows = p_in.shape[1:3]
    body = pl.ds(HALO, own)
    planes = own + 2 * HALO
    total_rows = m.shape[1]
    for c in range(4):
        if c < 3:
            field = f.at[c]
        else:
            field = m
        if total_rows > rows + 2 * HALO:
            field[body] = jnp.zeros((own,) + m.shape[1:], jnp.float32)
        field[body, :rows] = p_in[c]
        field[body, rows:rows + HALO] = yhi[c]
        field[body, total_rows - HALO:] = ylo[c]
        field[:HALO] = xlo[c]
        field[HALO + own:] = xhi[c]
    shape = m.shape[1:]
    in_rows = inside_rows(place, rows, total_rows, shape)
    in_lower = inside_rows(place, rows, total_rows, shape, place[0] > 0)
    in_upper = inside_rows(place, rows, total_rows, shape, place[0] < place[2] - 1)
    m[body] = jnp.where(in_rows, m[body], 0.0)
    m[:HALO] = jnp.where(in_lower, m[:HALO], 0.0)
    m[HALO + own:] = jnp.where(in_upper, m[HALO + own:], 0.0)
    make_coefficients(scale, 1, planes - 1, m, cx, cym, cyp, czm, czp, weight, diag, unroll=True)
    faces = (cx, cym, cyp, czm, czp)
    start_from_zero(1, planes - 1, ub, f, weight, unroll=True)
    relax(2, planes - 2, ub, ua, f, weight, faces, unroll=True)
    relax(3, planes - 3, ua, ub, f, weight, faces, unroll=True)
    lanes = u_out.shape[-1]
    for c in range(3):
        u_out[c] = ub[c, body, :rows, :lanes]
    residual_pairs(HALO, own // 2, 0, rows, ub, f, m, diag, faces, pairs, unroll=True)
    if rows > 4:
        packet[...] = pool_pairs(pairs, pooled)
    else:
        for c in range(4):
            for p in range(own // 2):
                for q in range(rows // 2):
                    at = 128 * (p * (rows // 2) + q)
                    pooled[c:c + 1, at:at + 128] = (
                        pairs[c, p, 2 * q:2 * q + 1] + pairs[c, p, 2 * q + 1:2 * q + 2]
                    )
        depth = pooled.shape[1]
        source = lax.broadcasted_iota(jnp.int32, (depth, 128), 0)
        target = lax.broadcasted_iota(jnp.int32, (depth, 128), 1)
        hit = (source // 128 * 32 + source % 128 // 2 == target) & (source % 128 < 64)
        pool = jnp.where(hit, 0.125, 0.0).astype(jnp.bfloat16)
        packet[...] = split_dot(pooled[...], pool)[:4]


def last_kernel(place, g, u3_out, u4_out, r4_out, fw, mw, ua, ub, faces, weight, diag,
                f4, m4, faces4, weight4, diag4, va, vb, rows_out):
    count = g.shape[0]
    rows, lanes = g.shape[2:]
    shape = (rows, lanes)
    lane = lax.broadcasted_iota(jnp.int32, shape, 1)
    row = lax.broadcasted_iota(jnp.int32, shape, 0)
    x_one, y_one, z = lane // 64 == 1, lane // 32 % 2 == 1, lane % 32
    first_row, last_row = row == 0, row == rows - 1
    zero = jnp.zeros(shape, jnp.float32)
    x_at, y_at = place[0], place[1]
    window = 2 * REACH + 1
    for w in range(window):
        i = y_at + (w - REACH)
        inside = (i >= 0) & (i < count)
        i = jnp.clip(i, 0, count - 1)
        for c in range(3):
            fw[c, w] = jnp.where(inside, g[i, c], 0.0)
        mw[w] = jnp.where(inside, g[i, 3], 0.0)

    def shifted_rows(value):
        return pltpu.roll(value, 1, 0), pltpu.roll(value, rows - 1, 0)

    def near3(get, w):
        centre = get(w)
        other = pltpu.roll(centre, 64, 1)
        lower, upper = shifted_rows(other)
        x_out = jnp.where(x_one, upper, lower)
        y_in = jnp.where(y_one, pltpu.roll(centre, 32, 1), pltpu.roll(centre, lanes - 32, 1))
        below = pltpu.roll(get(w - 1), lanes - 32, 1) if w > 0 else zero
        above = pltpu.roll(get(w + 1), 32, 1) if w < window - 1 else zero
        y_out = jnp.where(y_one, above, below)
        return centre, (other, x_out, y_in, y_out, pltpu.roll(centre, 1, 1), pltpu.roll(centre, lanes - 1, 1))

    x_edge = (x_one & last_row) | (jnp.logical_not(x_one) & first_row)
    outside3 = (None, x_edge, None, None, z == 0, z == 31)

    def near4(get, w):
        centre = get(w)
        lower, upper = shifted_rows(centre)
        return centre, (lower, upper, get(w - 1), get(w + 1),
                        pltpu.roll(centre, 2, 1), pltpu.roll(centre, lanes - 2, 1))

    outside4 = (first_row, last_row, None, None, z < 2, z >= 30)

    def level(scale, near, outside, f, m, faces, weight, diag, ua, ub, spans, residual):
        half = 0.5 * scale
        for w in spans[0]:
            centre, sides = near(lambda j: m[j], w)
            total = jnp.full(shape, mass_term, jnp.float32)
            for k in range(6):
                side = sides[k] if outside[k] is None else jnp.where(outside[k], 0.0, sides[k])
                face = half * (centre + side)
                total = total + face
                faces[k, w] = face if outside[k] is None else jnp.where(outside[k], 0.0, face)
            diag[w] = total
            weight[w] = jnp.where(centre > 0.0, damping / total, 0.0)
            for c in range(3):
                ua[c, w] = weight[w] * f[c, w]

        def flux_at(u, c, w):
            centre, sides = near(lambda j: u[c, j], w)
            flux = faces[0, w] * sides[0]
            for k in range(1, 6):
                flux = flux + faces[k, w] * sides[k]
            return centre, flux

        for source, target, span in ((ua, ub, spans[1]), (ub, ua, spans[2])):
            for w in span:
                for c in range(3):
                    centre, flux = flux_at(source, c, w)
                    target[c, w] = (1.0 - damping) * centre + weight[w] * (f[c, w] + flux)
        for w in spans[3]:
            for c in range(3):
                centre, flux = flux_at(ua, c, w)
                residual(c, w, f[c, w] + flux - diag[w] * centre)

    def pool(value):
        value = value + pltpu.roll(value, 64, 1)
        value = value + pltpu.roll(value, 32, 1)
        return 0.125 * (value + pltpu.roll(value, lanes - 1, 1))

    def to_level4(c, w, value):
        f4[c, w] = pool(value)

    spans = (range(window), range(1, window - 1), range(1, window - 1), range(2, window - 2))
    level(0.25**3, near3, outside3, fw, mw, faces, weight, diag, ua, ub, spans, to_level4)
    for w in range(1, window - 1):
        m4[w] = pool(mw[w])
    mine = row == x_at

    def own_row(value):
        return jnp.sum(jnp.where(mine, value, 0.0), axis=0, keepdims=True)

    def keep(c, w, value):
        rows_out[3 + c:4 + c] = own_row(value)

    spans = tuple(range(2 + k, window - 2 - k) for k in range(4))
    level(0.25**4, near4, outside4, f4, m4, faces4, weight4, diag4, va, vb, spans, keep)
    for c in range(3):
        value = own_row(ua[c, REACH])
        rows_out[c:c + 1] = own_row(va[c, REACH])
        for k in range(4):
            turned = value if k == 0 else pltpu.roll(value, lanes - 32 * k, 1)
            u3_out[c, k // 2, k % 2:k % 2 + 1] = turned[:, :32]
    source = lax.broadcasted_iota(jnp.int32, (lanes, lanes), 0)
    target = lax.broadcasted_iota(jnp.int32, (lanes, lanes), 1)
    take = jnp.where((source == 2 * target) & (target < 16), 1.0, 0.0).astype(jnp.bfloat16)
    ends = split_dot(rows_out[...], take)
    for c in range(3):
        u4_out[c, 0] = ends[c:c + 1, :16]
        r4_out[c, 0] = ends[3 + c:4 + c, :16]


def pack_kernel(viscosities, u_in, f_in, types, up, down, viscosity):
    rows = u_in.shape[2]
    kind = types[...]
    value = jnp.where(
        kind < 2,
        jnp.where(kind == 0, viscosities[0], viscosities[1]),
        jnp.where(kind == 2, viscosities[2], viscosities[3]),
    )
    viscosity[...] = value
    for c in range(3):
        up[c], down[c] = u_in[c, :, rows - HALO:], u_in[c, :, :HALO]
        up[3 + c], down[3 + c] = f_in[c, :, rows - HALO:], f_in[c, :, :HALO]
    up[6], down[6] = value[:, rows - HALO:], value[:, :HALO]


def on_chip(count):
    return [pl.BlockSpec(memory_space=pltpu.VMEM)] * count


def planes_scratch(planes, rows, lanes, pairs, own_rows, pooled, ends=()):
    block = (planes, rows, lanes)
    return (
        [pltpu.VMEM(ends + (3,) + block, jnp.float32)] * 3
        + [pltpu.VMEM(ends + block, jnp.float32)] * 8
        + [pltpu.VMEM((4, pairs, own_rows, lanes), jnp.float32), pltpu.VMEM(pooled, jnp.float32)]
    )


LIMIT = pltpu.CompilerParams(vmem_limit_bytes=20 * 1024 * 1024)


def on_device(velocity_guess, forcing, cell_type, viscosities):
    f32 = jnp.float32
    count_x, count_y = lax.axis_size("gx"), lax.axis_size("gy")
    place = jnp.stack([lax.axis_index("gx"), lax.axis_index("gy"), count_x, count_y]).astype(jnp.int32)
    in_smem = [pl.BlockSpec(memory_space=pltpu.SMEM)]
    own, rows, lanes = cell_type.shape
    edge = jax.ShapeDtypeStruct((7, own, HALO, lanes), f32)
    up, down, viscosity = pl.pallas_call(
        pack_kernel,
        out_shape=(edge, edge, jax.ShapeDtypeStruct(cell_type.shape, f32)),
        in_specs=in_smem + on_chip(3),
        out_specs=tuple(on_chip(3)),
        compiler_params=LIMIT,
    )(viscosities, velocity_guess, forcing, cell_type)
    ylo = passed_round(up, "gy", 1)
    yhi = passed_round(down, "gy", -1)

    def wide(first, *inner):
        def layers(own_part, at, layer):
            part = jnp.concatenate([own_part[:, layer], yhi[at, layer], ylo[at, layer]], axis=2)
            return part.reshape(-1, rows + 2 * HALO, lanes)

        return jnp.concatenate(
            [
                layers(velocity_guess, slice(0, 3), slice(first, first + HALO)),
                layers(forcing, slice(3, 6), slice(*inner)),
                layers(viscosity[None], slice(6, 7), slice(first, first + HALO)),
            ],
            axis=0,
        )

    xlo = passed_round(wide(own - HALO, own - HALO + 1, own), "gx", 1)
    xhi = passed_round(wide(0, 0, HALO - 1), "gx", -1)
    tall = rows + 2 * HALO
    middle = own // 2 - HALO
    state = (
        (3, own - 2 * HALO + 2, rows, lanes),
        (4 * middle, rows // 2, lanes // 2),
        (4, 2, 3, 2, tall, lanes),
        (2, 3, HALO, tall, lanes),
        (2, HALO + 1, tall, lanes),
    )
    known = pl.pallas_call(
        inner_kernel,
        out_shape=tuple(jax.ShapeDtypeStruct(shape, f32) for shape in state),
        in_specs=in_smem + on_chip(5),
        out_specs=tuple(on_chip(5)),
        scratch_shapes=planes_scratch(own + 2 * HALO, tall, lanes, middle, rows, (4 * middle, rows, 128)),
        compiler_params=LIMIT,
        cost_estimate=pl.CostEstimate(flops=60_000_000, bytes_accessed=6_000_000, transcendentals=0),
    )(place, velocity_guess, forcing, viscosity, ylo, yhi)
    u0, packet = pl.pallas_call(
        outer_kernel,
        out_shape=(
            jax.ShapeDtypeStruct(velocity_guess.shape, f32),
            jax.ShapeDtypeStruct((4 * own // 2, rows // 2, lanes // 2), f32),
        ),
        in_specs=in_smem + on_chip(7),
        out_specs=tuple(on_chip(2)),
        scratch_shapes=planes_scratch(2 * HALO + 1, tall, lanes, HALO, rows, (4 * HALO, rows, 128), (2,)),
        compiler_params=LIMIT,
    )(place, *known, xlo, xhi)
    results = [u0]
    for grid_level in (1, 2):
        own, rows = own // 2, rows // 2
        packet = packet.reshape(4, own, rows, 128)
        valid = 256 >> grid_level
        ylo = passed_round(packet[:, :, rows - HALO:], "gy", 1)
        yhi = passed_round(packet[:, :, :HALO], "gy", -1)
        parts = [packet, yhi, ylo]
        total_rows = rows + 2 * HALO
        if total_rows % 8:
            parts = [packet, yhi, jnp.zeros_like(yhi), ylo]
            total_rows += HALO
        tall = jnp.concatenate(parts, axis=2)
        xlo = passed_round(tall[:, own - HALO:], "gx", 1)
        xhi = passed_round(tall[:, :HALO], "gx", -1)
        if grid_level == 1:
            packet_shape, pooled_shape = (4 * own // 2, rows // 2, 128), (4 * own // 2, rows, 128)
        else:
            packet_shape, pooled_shape = (4, 128), (8, 512)
        u_own, packet = pl.pallas_call(
            functools.partial(middle_kernel, 0.25**grid_level),
            out_shape=(
                jax.ShapeDtypeStruct((3, own, rows, valid), f32),
                jax.ShapeDtypeStruct(packet_shape, f32),
            ),
            in_specs=in_smem + on_chip(5),
            out_specs=tuple(on_chip(2)),
            scratch_shapes=planes_scratch(own + 2 * HALO, total_rows, 128, own // 2, rows, pooled_shape),
            compiler_params=LIMIT,
        )(place, packet, ylo, yhi, xlo, xhi)
        results.append(u_own)
    column = lax.all_to_all(jnp.broadcast_to(packet[None], (count_x, 4, 128)), "gx", 0, 0)
    column = column.transpose(1, 0, 2)
    gathered = lax.all_to_all(
        jnp.broadcast_to(column[None], (count_y, 4, count_x, 128)), "gy", 0, 0
    )
    block = (2 * REACH + 1, count_x, 128)
    field, vector, six = (pltpu.VMEM(lead + block, f32) for lead in ((), (3,), (6,)))
    last = pl.pallas_call(
        last_kernel,
        out_shape=tuple(jax.ShapeDtypeStruct(shape, f32) for shape in ((3, 2, 2, 32), (3, 1, 1, 16), (3, 1, 1, 16))),
        in_specs=in_smem + on_chip(1),
        out_specs=tuple(on_chip(3)),
        scratch_shapes=[vector, field, vector, vector, six, field, field,
                        vector, field, six, field, field, vector, vector, pltpu.VMEM((8, 128), f32)],
        compiler_params=LIMIT,
    )(place, gathered)
    return (*results, *last)


def solution(mesh):
    return jax.shard_map(
        on_device,
        mesh=mesh,
        in_specs=(P(None, "gx", "gy", None), P(None, "gx", "gy", None), P("gx", "gy", None), P()),
        out_specs=(P(None, "gx", "gy", None),) * 6,
        check_vma=False,
    )
```

time: 156 us -> 111 us (0.71)
  waiting for transfers between devices: 44.3 us -> 20.3 us
  starting transfers between devices: 43.2 us -> 21.4 us
  blocking collectives: 18.7 us -> 36.9 us
  Pallas kernels: 34.9 us -> 23.8 us
  other arithmetic: 8.27 us -> 2.09 us
    all_to_all x0 -> x1, blocking collectives: none -> 18.3 us  [on_device(): lax.all_to_all(jnp.broadcast_to(column[None], (count_y, 4, count_x, 128))...]
    ppermute x12, waiting for transfers between devices: 32.6 us -> 20.3 us  [passed_round(): lax.ppermute(value, axis, [(source, (source + steps) % count) for source...]
    all_to_all x1 -> x0, waiting for transfers between devices: 11.7 us -> none  [on_device(): lax.all_to_all(jnp.broadcast_to(column[None], (count_y, 4, count_x, 128))...]
    ppermute x12, starting transfers between devices: 32.5 us -> 21.4 us  [passed_round(): lax.ppermute(value, axis, [(source, (source + steps) % count) for source...]
    all_to_all x1 -> x0, starting transfers between devices: 10.7 us -> none  [on_device(): lax.all_to_all(jnp.broadcast_to(column[None], (count_y, 4, count_x, 128))...]
    pallas_call x2 -> x4, Pallas kernels: 27.8 us -> 20.4 us  [the longest x1 7.22 us: on_device(): pl.pallas_call(inner_kernel, out_shape=tuple((jax.ShapeDtypeStruct(shape,...]
    pallas_call x2, Pallas kernels: 7.04 us -> 3.34 us  [on_device(): pl.pallas_call(functools.partial(middle_kernel, 0.25 ** grid_level), out_...]
    broadcast_in_dim x1 -> x0, other arithmetic: 3.59 us -> none  [on_device(): viscosity[None]]
  transfers between devices with their start and end apart: 13 -> 12, of which waited for: 13 -> 6; matrix products, arithmetic and copies ran while one was open for 2% -> 1% of each run, Pallas kernels for 0% -> 7%
where the time goes in v2:
time: 111 us; the launch traced here: 109 us
  blocking collectives  36.9 us (33%)
  Pallas kernels  23.8 us (21%)
  starting transfers between devices  21.4 us (19%)
  waiting for transfers between devices  20.3 us (18%)
  local copies, waits for them, and re-layouts  4.15 us (4%)
  other arithmetic  2.09 us (2%)
    ppermute x12, starting transfers between devices, passed_round(): lax.ppermute(value, axis, [(source, (source + steps) % count) for source...  21.4 us
    ppermute x12, waiting for transfers between devices, passed_round(): lax.ppermute(value, axis, [(source, (source + steps) % count) for source...  20.3 us
    all_to_all x1, blocking collectives, on_device(): lax.all_to_all(jnp.broadcast_to(packet[None], (count_x, 4, 128)), 'gx', 0...  18.6 us
    all_to_all x1, blocking collectives, on_device(): lax.all_to_all(jnp.broadcast_to(column[None], (count_y, 4, count_x, 128))...  18.3 us
    pallas_call x1, Pallas kernels, on_device(): pl.pallas_call(inner_kernel, out_shape=tuple((jax.ShapeDtypeStruct(shape,...  7.22 us
    pallas_call x1, Pallas kernels, on_device(): pl.pallas_call(outer_kernel, out_shape=(jax.ShapeDtypeStruct(velocity_gue...  7.06 us
    pallas_call x1, Pallas kernels, on_device(): pl.pallas_call(last_kernel, out_shape=tuple((jax.ShapeDtypeStruct(shape,...  5.48 us
    unnamed x12, local copies, waits for them, and re-layouts  3.88 us
  transfers between devices with their start and end apart: 12, of which 6 were waited for; matrix products, arithmetic and copies ran while one was open for 1% of the time, Pallas kernels for 7%

profile of v2, /device:TPU:32, one launch (start us, length us, event | category | flops | bytes accessed | tf_op | source)
XLA Modules:
  0.0 109.4 jit_solution(18085755989636956335)
XLA Ops:
  0.6 1.1 %copy-done = f32[3,16,16,256]{3,2,1,0:T(8,128)S(1)} copy-done((f32[3,16,16,256]{3,2,1,0:T(8,128)S(1)}, f32[3,16,16,256]{3,2,1,0:T(8,128)}, u32[]{:S(2)}) %copy-start) | copy-done | bytes 786456
  1.8 1.1 %copy-done.2 = f32[3,16,16,256]{3,2,1,0:T(8,128)S(1)} copy-done((f32[3,16,16,256]{3,2,1,0:T(8,128)S(1)}, f32[3,16,16,256]{3,2,1,0:T(8,128)}, u32[]{:S(2)}) %copy-start.2) | copy-done | bytes 786456
  2.9 0.9 copy-done.4
  3.9 0.7 copy-done.5
  4.5 0.6 shard_map.91
  5.2 1.7 %collective-permute-start = (f32[7,16,4,256]{3,2,1,0:T(4,128)S(1)}, f32[7,16,4,256]{3,2,1,0:T(4,128)S(1)}, u32[]{:S(2)}, u32[]{:S(2)}) collective-permute-start(f32[7,16,4,256]{3,2,1,0:T(4,128)S(1)} %get-tuple-element.24), channel_id=1, source_target_pairs={{0,1},{1,2},{2,3},{3,4},{4,5},{5,6},{6,7},{7,8},{8,9},{9,10},{10,1... | collective-permute-start | bytes 1376264 | tf_op jit(solution)/shard_map/ppermute | solution.py:21
  6.8 3.8 %collective-permute-start.1 = (f32[7,16,4,256]{3,2,1,0:T(4,128)S(1)}, f32[7,16,4,256]{3,2,1,0:T(4,128)S(1)}, u32[]{:S(2)}, u32[]{:S(2)}) collective-permute-start(f32[7,16,4,256]{3,2,1,0:T(4,128)S(1)} %get-tuple-element.25), channel_id=1, source_target_pairs={{0,15},{1,0},{2,1},{3,2},{4,3},{5,4},{6,5},{7,6},{8,7},{9,8},{10,9... | collective-permute-start | bytes 1376264 | tf_op jit(solution)/shard_map/ppermute | solution.py:21
  10.7 10.3 %collective-permute-done.ylo = f32[7,16,4,256]{3,2,1,0:T(4,128)S(1)} collective-permute-done((f32[7,16,4,256]{3,2,1,0:T(4,128)S(1)}, f32[7,16,4,256]{3,2,1,0:T(4,128)S(1)}, u32[]{:S(2)}, u32[]{:S(2)}) %collective-permute-start) | collective-permute-done | bytes 458784 | tf_op jit(solution)/shard_map/ppermute | solution.py:21
  21.2 0.9 pad_maximum_fusion
  22.1 0.9 pad_maximum_fusion.1
  23.0 1.7 %collective-permute-start.3 = (f32[25,24,256]{2,1,0:T(8,128)}, f32[25,24,256]{2,1,0:T(8,128)}, u32[]{:S(2)}, u32[]{:S(2)}) collective-permute-start(f32[25,24,256]{2,1,0:T(8,128)} %pad_maximum_fusion.1), channel_id=1, source_target_pairs={{0,240},{16,0},{32,16},{48,32},{64,48},{80,64},{96,80},{112,96},{1... | collective-permute-start | bytes 1843208 | tf_op jit(solution)/shard_map/ppermute | solution.py:21
  24.7 0.1 pad_add_fusion.place
  24.8 7.2 %shard_map.92 = (f32[3,10,16,256]{3,2,1,0:T(8,128)S(1)}, f32[16,8,128]{2,1,0:T(8,128)S(1)}, f32[4,2,3,2,24,256]{5,4,3,2,1,0:T(8,128)S(1)}, f32[2,3,4,24,256]{4,3,2,1,0:T(8,128)S(1)}, f32[2,5,24,256]{3,2,1,0:T(8,128)S(1)}) custom-call(s32[4]{0:T(128)S(1)} %pad_add_fusion.place, f32[3,16,16,256]{3,2,1,0:T(8,128)S(1)} %copy-done.1, ...), custom_call_target="tpu_custom_call" | custom-call | flops 60000000 | bytes 6000000 | tf_op jit(solution)/shard_map/pallas_call | solution.py:453
  32.0 0.7 collective-permute-done.3.xhi
  32.7 7.1 %shard_map.93 = (f32[3,16,16,256]{3,2,1,0:T(8,128)}, f32[32,8,128]{2,1,0:T(8,128)S(1)}) custom-call(s32[4]{0:T(128)S(1)} %pad_add_fusion.place, f32[3,10,16,256]{3,2,1,0:T(8,128)S(1)} %get-tuple-element.26.u_mid, f32[16,8,128]{2,1,0:T(8,128)S(1)} %get-tuple-element.27.packet_mid, f32[4,2,3,2,24,256]{5,4,3,2,1,0:T(8,128)S(1)} %get-tuple-element.28.u_edge, ...), custom_call_target="tpu_custom_call" | custom-call | tf_op jit(solution)/shard_map/pallas_call | solution.py:462
  39.8 0.1 collective-permute-start.4
  39.9 5.3 %collective-permute-start.5 = (f32[4,8,4,128]{3,2,1,0:T(4,128)S(1)}, f32[4,8,4,128]{3,2,1,0:T(4,128)S(1)}, u32[]{:S(2)}, u32[]{:S(2)}) collective-permute-start(f32[4,8,4,128]{3,2,1,0:T(4,128)S(1)} %get-tuple-element.60), channel_id=1, source_target_pairs={{0,15},{1,0},{2,1},{3,2},{4,3},{5,4},{6,5},{7,6},{8,7},{9,8},{10,9... | collective-permute-start | bytes 196616 | tf_op jit(solution)/shard_map/ppermute | solution.py:21
  45.2 2.2 %collective-permute-done.4.ylo = f32[4,8,4,128]{3,2,1,0:T(4,128)S(1)} collective-permute-done((f32[4,8,4,128]{3,2,1,0:T(4,128)S(1)}, f32[4,8,4,128]{3,2,1,0:T(4,128)S(1)}, u32[]{:S(2)}, u32[]{:S(2)}) %collective-permute-start.4) | collective-permute-done | bytes 65568 | tf_op jit(solution)/shard_map/ppermute | solution.py:21
  47.5 1.1 %collective-permute-start.6 = (f32[4,4,16,128]{3,2,1,0:T(8,128)S(1)}, f32[4,4,16,128]{3,2,1,0:T(8,128)S(1)}, u32[]{:S(2)}, u32[]{:S(2)}) collective-permute-start(f32[4,4,16,128]{3,2,1,0:T(8,128)S(1)} %get-tuple-element.57), channel_id=1, source_target_pairs={{0,16},{16,32},{32,48},{48,64},{64,80},{80,96},{96,112},{112,128},... | collective-permute-start | bytes 393224 | tf_op jit(solution)/shard_map/ppermute | solution.py:21
  48.7 0.6 collective-permute-start.7
  49.3 2.6 %collective-permute-done.6.xlo = f32[4,4,16,128]{3,2,1,0:T(8,128)S(1)} collective-permute-done((f32[4,4,16,128]{3,2,1,0:T(8,128)S(1)}, f32[4,4,16,128]{3,2,1,0:T(8,128)S(1)}, u32[]{:S(2)}, u32[]{:S(2)}) %collective-permute-start.6) | collective-permute-done | bytes 131104 | tf_op jit(solution)/shard_map/ppermute | solution.py:21
  51.9 1.7 %shard_map.94 = (f32[3,8,8,128]{3,2,1,0:T(8,128)}, f32[16,4,128]{2,1,0:T(4,128)S(1)}) custom-call(s32[4]{0:T(128)S(1)} %pad_add_fusion.place, f32[4,8,8,128]{3,2,1,0:T(8,128)S(1)} %bitcast.16, f32[4,8,4,128]{3,2,1,0:T(4,128)S(1)} %collective-permute-done.4.ylo, f32[4,8,4,128]{3,2,1,0:T(4,128)S(1)} %collective-permute-done.5.yhi, ...), custom_call_target="tpu_custom_call" | custom-call | tf_op jit(solution)/shard_map/pallas_call | solution.py:492
  53.6 5.3 %collective-permute-start.9 = (f32[4,4,4,128]{3,2,1,0:T(4,128)S(1)}, f32[4,4,4,128]{3,2,1,0:T(4,128)S(1)}, u32[]{:S(2)}, u32[]{:S(2)}) collective-permute-start(f32[4,4,4,128]{3,2,1,0:T(4,128)S(1)} %bitcast.19), channel_id=1, source_target_pairs={{0,15},{1,0},{2,1},{3,2},{4,3},{5,4},{6,5},{7,6},{8,7},{9,8},{10,9... | collective-permute-start | bytes 98312 | tf_op jit(solution)/shard_map/ppermute | solution.py:21
  59.0 1.8 %collective-permute-done.8.ylo = f32[4,4,4,128]{3,2,1,0:T(4,128)S(1)} collective-permute-done((f32[4,4,4,128]{3,2,1,0:T(4,128)S(1)}, f32[4,4,4,128]{3,2,1,0:T(4,128)S(1)}, u32[]{:S(2)}, u32[]{:S(2)}) %collective-permute-start.8) | collective-permute-done | bytes 32800 | tf_op jit(solution)/shard_map/ppermute | solution.py:21
  60.9 0.1 pad_maximum_fusion.7
  60.9 1.2 %collective-permute-start.10 = (f32[4,4,16,128]{3,2,1,0:T(8,128)S(1)}, f32[4,4,16,128]{3,2,1,0:T(8,128)S(1)}, u32[]{:S(2)}, u32[]{:S(2)}) collective-permute-start(f32[4,4,16,128]{3,2,1,0:T(8,128)S(1)} %pad_maximum_fusion.7), channel_id=1, source_target_pairs={{0,16},{16,32},{32,48},{48,64},{64,80},{80,96},{96,112},{112,128},... | collective-permute-start | bytes 393224 | tf_op jit(solution)/shard_map/ppermute | solution.py:21
  62.1 0.6 collective-permute-start.11
  62.7 2.6 %collective-permute-done.10.xlo = f32[4,4,16,128]{3,2,1,0:T(8,128)S(1)} collective-permute-done((f32[4,4,16,128]{3,2,1,0:T(8,128)S(1)}, f32[4,4,16,128]{3,2,1,0:T(8,128)S(1)}, u32[]{:S(2)}, u32[]{:S(2)}) %collective-permute-start.10) | collective-permute-done | bytes 131104 | tf_op jit(solution)/shard_map/ppermute | solution.py:21
  65.3 1.7 %shard_map.95 = (f32[3,4,4,64]{3,2,1,0:T(4,128)}, f32[4,128]{1,0:T(4,128)S(1)}) custom-call(s32[4]{0:T(128)S(1)} %pad_add_fusion.place, f32[4,4,4,128]{3,2,1,0:T(4,128)S(1)} %bitcast.21, f32[4,4,4,128]{3,2,1,0:T(4,128)S(1)} %collective-permute-done.8.ylo, f32[4,4,4,128]{3,2,1,0:T(4,128)S(1)} %collective-permute-done.9.yhi, ...), custom_call_target="tpu_custom_call" | custom-call | tf_op jit(solution)/shard_map/pallas_call | solution.py:492
  67.0 18.6 %all_to_all.10 = f32[16,4,128]{2,1,0:T(4,128)S(1)} all-to-all(f32[16,4,128]{2,1,0:T(4,128)S(1)} %broadcast_in_dim.10), channel_id=1, replica_groups=mesh['gx'=16,'gy'=16] {'gx'}, dimensions={0} | all-to-all | bytes 65536 | tf_op jit(solution)/shard_map/all_to_all | solution.py:504
  85.6 18.3 %all_to_all.11.g = f32[16,4,16,128]{3,2,1,0:T(8,128)S(1)} all-to-all(f32[16,4,16,128]{3,2,1,0:T(8,128)S(1)} %broadcast_in_dim.22), channel_id=1, replica_groups=mesh['gx'=16,'gy'=16] {'gy'}, dimensions={0} | all-to-all | bytes 1048576 | tf_op jit(solution)/shard_map/all_to_all | solution.py:506
  103.9 5.5 %shard_map.96 = (f32[3,2,2,32]{3,2,1,0:T(2,128)}, f32[3,1,1,16]{3,2,1,0:T(1,128)}, f32[3,1,1,16]{3,2,1,0:T(1,128)}) custom-call(s32[4]{0:T(128)S(1)} %pad_add_fusion.place, f32[16,4,16,128]{3,2,1,0:T(8,128)S(1)} %all_to_all.11.g), custom_call_target="tpu_custom_call" | custom-call | tf_op jit(solution)/shard_map/pallas_call | solution.py:511
  (38 shorter events, 0.5 us)
Async XLA Ops:
  0.6 1.1 %copy-start = (f32[3,16,16,256]{3,2,1,0:T(8,128)S(1)}, f32[3,16,16,256]{3,2,1,0:T(8,128)}, u32[]{:S(2)}) copy-start(f32[3,16,16,256]{3,2,1,0:T(8,128)} %u_in.3) | copy-start | bytes 2359300
  1.8 1.1 %copy-start.2 = (f32[3,16,16,256]{3,2,1,0:T(8,128)S(1)}, f32[3,16,16,256]{3,2,1,0:T(8,128)}, u32[]{:S(2)}) copy-start(f32[3,16,16,256]{3,2,1,0:T(8,128)} %f_in.3) | copy-start | bytes 2359300
  2.9 0.9 copy-start.4
  3.9 0.7 copy-start.5
  5.2 15.8 %collective-permute-start = (f32[7,16,4,256]{3,2,1,0:T(4,128)S(1)}, f32[7,16,4,256]{3,2,1,0:T(4,128)S(1)}, u32[]{:S(2)}, u32[]{:S(2)}) collective-permute-start(f32[7,16,4,256]{3,2,1,0:T(4,128)S(1)} %get-tuple-element.24), channel_id=1, source_target_pairs={{0,1},{1,2},{2,3},{3,4},{4,5},{5,6},{6,7},{7,8},{8,9},{9,10},{10,1... | collective-permute-start | bytes 1376264 | tf_op jit(solution)/shard_map/ppermute | solution.py:21
  6.8 14.2 %collective-permute-start.1 = (f32[7,16,4,256]{3,2,1,0:T(4,128)S(1)}, f32[7,16,4,256]{3,2,1,0:T(4,128)S(1)}, u32[]{:S(2)}, u32[]{:S(2)}) collective-permute-start(f32[7,16,4,256]{3,2,1,0:T(4,128)S(1)} %get-tuple-element.25), channel_id=1, source_target_pairs={{0,15},{1,0},{2,1},{3,2},{4,3},{5,4},{6,5},{7,6},{8,7},{9,8},{10,9... | collective-permute-start | bytes 1376264 | tf_op jit(solution)/shard_map/ppermute | solution.py:21
  21.2 3.6 %copy-start.1 = (f32[3,16,16,256]{3,2,1,0:T(8,128)S(1)}, f32[3,16,16,256]{3,2,1,0:T(8,128)}, u32[]{:S(2)}) copy-start(f32[3,16,16,256]{3,2,1,0:T(8,128)} %u_in.3) | copy-start | bytes 2359300
  21.2 3.6 %copy-start.3 = (f32[3,16,16,256]{3,2,1,0:T(8,128)S(1)}, f32[3,16,16,256]{3,2,1,0:T(8,128)}, u32[]{:S(2)}) copy-start(f32[3,16,16,256]{3,2,1,0:T(8,128)} %f_in.3) | copy-start | bytes 2359300
  22.1 10.0 %collective-permute-start.2 = (f32[25,24,256]{2,1,0:T(8,128)}, f32[25,24,256]{2,1,0:T(8,128)S(1)}, u32[]{:S(2)}, u32[]{:S(2)}) collective-permute-start(f32[25,24,256]{2,1,0:T(8,128)} %pad_maximum_fusion), channel_id=1, source_target_pairs={{0,16},{16,32},{32,48},{48,64},{64,80},{80,96},{96,112},{112,128},... | collective-permute-start | bytes 1843208 | tf_op jit(solution)/shard_map/ppermute | solution.py:21
  23.0 9.7 %collective-permute-start.3 = (f32[25,24,256]{2,1,0:T(8,128)}, f32[25,24,256]{2,1,0:T(8,128)}, u32[]{:S(2)}, u32[]{:S(2)}) collective-permute-start(f32[25,24,256]{2,1,0:T(8,128)} %pad_maximum_fusion.1), channel_id=1, source_target_pairs={{0,240},{16,0},{32,16},{48,32},{64,48},{80,64},{96,80},{112,96},{1... | collective-permute-start | bytes 1843208 | tf_op jit(solution)/shard_map/ppermute | solution.py:21
  39.8 7.7 %collective-permute-start.4 = (f32[4,8,4,128]{3,2,1,0:T(4,128)S(1)}, f32[4,8,4,128]{3,2,1,0:T(4,128)S(1)}, u32[]{:S(2)}, u32[]{:S(2)}) collective-permute-start(f32[4,8,4,128]{3,2,1,0:T(4,128)S(1)} %get-tuple-element.61), channel_id=1, source_target_pairs={{0,1},{1,2},{2,3},{3,4},{4,5},{5,6},{6,7},{7,8},{8,9},{9,10},{10,1... | collective-permute-start | bytes 196616 | tf_op jit(solution)/shard_map/ppermute | solution.py:21
  39.9 7.6 %collective-permute-start.5 = (f32[4,8,4,128]{3,2,1,0:T(4,128)S(1)}, f32[4,8,4,128]{3,2,1,0:T(4,128)S(1)}, u32[]{:S(2)}, u32[]{:S(2)}) collective-permute-start(f32[4,8,4,128]{3,2,1,0:T(4,128)S(1)} %get-tuple-element.60), channel_id=1, source_target_pairs={{0,15},{1,0},{2,1},{3,2},{4,3},{5,4},{6,5},{7,6},{8,7},{9,8},{10,9... | collective-permute-start | bytes 196616 | tf_op jit(solution)/shard_map/ppermute | solution.py:21
  47.5 4.4 %collective-permute-start.6 = (f32[4,4,16,128]{3,2,1,0:T(8,128)S(1)}, f32[4,4,16,128]{3,2,1,0:T(8,128)S(1)}, u32[]{:S(2)}, u32[]{:S(2)}) collective-permute-start(f32[4,4,16,128]{3,2,1,0:T(8,128)S(1)} %get-tuple-element.57), channel_id=1, source_target_pairs={{0,16},{16,32},{32,48},{48,64},{64,80},{80,96},{96,112},{112,128},... | collective-permute-start | bytes 393224 | tf_op jit(solution)/shard_map/ppermute | solution.py:21
  48.7 3.3 %collective-permute-start.7 = (f32[4,4,16,128]{3,2,1,0:T(8,128)S(1)}, f32[4,4,16,128]{3,2,1,0:T(8,128)S(1)}, u32[]{:S(2)}, u32[]{:S(2)}) collective-permute-start(f32[4,4,16,128]{3,2,1,0:T(8,128)S(1)} %get-tuple-element.56), channel_id=1, source_target_pairs={{0,240},{16,0},{32,16},{48,32},{64,48},{80,64},{96,80},{112,96},{1... | collective-permute-start | bytes 393224 | tf_op jit(solution)/shard_map/ppermute | solution.py:21
  53.6 7.2 %collective-permute-start.8 = (f32[4,4,4,128]{3,2,1,0:T(4,128)S(1)}, f32[4,4,4,128]{3,2,1,0:T(4,128)S(1)}, u32[]{:S(2)}, u32[]{:S(2)}) collective-permute-start(f32[4,4,4,128]{3,2,1,0:T(4,128)S(1)} %bitcast.18), channel_id=1, source_target_pairs={{0,1},{1,2},{2,3},{3,4},{4,5},{5,6},{6,7},{7,8},{8,9},{9,10},{10,1... | collective-permute-start | bytes 98312 | tf_op jit(solution)/shard_map/ppermute | solution.py:21
  53.6 7.2 %collective-permute-start.9 = (f32[4,4,4,128]{3,2,1,0:T(4,128)S(1)}, f32[4,4,4,128]{3,2,1,0:T(4,128)S(1)}, u32[]{:S(2)}, u32[]{:S(2)}) collective-permute-start(f32[4,4,4,128]{3,2,1,0:T(4,128)S(1)} %bitcast.19), channel_id=1, source_target_pairs={{0,15},{1,0},{2,1},{3,2},{4,3},{5,4},{6,5},{7,6},{8,7},{9,8},{10,9... | collective-permute-start | bytes 98312 | tf_op jit(solution)/shard_map/ppermute | solution.py:21
  60.9 4.4 %collective-permute-start.10 = (f32[4,4,16,128]{3,2,1,0:T(8,128)S(1)}, f32[4,4,16,128]{3,2,1,0:T(8,128)S(1)}, u32[]{:S(2)}, u32[]{:S(2)}) collective-permute-start(f32[4,4,16,128]{3,2,1,0:T(8,128)S(1)} %pad_maximum_fusion.7), channel_id=1, source_target_pairs={{0,16},{16,32},{32,48},{48,64},{64,80},{80,96},{96,112},{112,128},... | collective-permute-start | bytes 393224 | tf_op jit(solution)/shard_map/ppermute | solution.py:21
  62.1 3.2 %collective-permute-start.11 = (f32[4,4,16,128]{3,2,1,0:T(8,128)S(1)}, f32[4,4,16,128]{3,2,1,0:T(8,128)S(1)}, u32[]{:S(2)}, u32[]{:S(2)}) collective-permute-start(f32[4,4,16,128]{3,2,1,0:T(8,128)S(1)} %pad_maximum_fusion.7), channel_id=1, source_target_pairs={{0,240},{16,0},{32,16},{48,32},{64,48},{80,64},{96,80},{112,96},{1... | collective-permute-start | bytes 393224 | tf_op jit(solution)/shard_map/ppermute | solution.py:21

commit v3 on v2

--- a/solution.py
+++ b/solution.py
@@ -127,7 +127,7 @@
     return pooled[:, pl.ds(0, rows // 2, 2), :] + pooled[:, pl.ds(1, rows // 2, 2), :]
 
 
-def inner_kernel(place, u_in, f_in, m_in, ylo, yhi, u_mid, packet_mid, u_edge, f_edge, m_edge,
+def inner_kernel(place, viscosities, u_in, f_in, types, ylo, yhi, u_mid, packet_mid, u_edge, f_edge, m_edge,
                  ua, ub, f, m, cx, cym, cyp, czm, czp, weight, diag, pairs, pooled):
     own, rows = u_in.shape[1:3]
     body = pl.ds(HALO, own)
@@ -140,7 +140,7 @@
         f[c, body, :rows] = f_in[c]
         f[c, body, rows:rows + HALO] = yhi[3 + c]
         f[c, body, rows + HALO:] = ylo[3 + c]
-    m[body, :rows] = m_in[...]
+    m[body, :rows] = viscosity_of(types[...], viscosities)
     m[body, rows:rows + HALO] = jnp.where(has_upper, yhi[6], 0.0)
     m[body, rows + HALO:] = jnp.where(has_lower, ylo[6], 0.0)
 
@@ -151,52 +151,67 @@
     edges(0, ua, 0)
     f_edge[0], f_edge[1] = f[:, HALO:2 * HALO], f[:, last - HALO:last]
     m_edge[0], m_edge[1] = m[HALO:2 * HALO + 1], m[last - HALO - 1:last]
-    make_coefficients(1.0, HALO + 1, last - 1, m, cx, cym, cyp, czm, czp, weight, diag)
+    make_coefficients(1.0, HALO + 1, last - 1, m, cx, cym, cyp, czm, czp, weight, diag, True)
     faces = (cx, cym, cyp, czm, czp)
-    relax(HALO + 1, last - 1, ua, ub, f, weight, faces)
+    relax(HALO + 1, last - 1, ua, ub, f, weight, faces, True)
     edges(1, ub, 1)
-    relax(HALO + 2, last - 2, ub, ua, f, weight, faces)
+    relax(HALO + 2, last - 2, ub, ua, f, weight, faces, True)
     edges(2, ua, 2)
-    relax(HALO + 3, last - 3, ua, ub, f, weight, faces)
+    relax(HALO + 3, last - 3, ua, ub, f, weight, faces, True)
     edges(3, ub, 3)
     u_mid[...] = ub[:, HALO + 3:last - 3, :rows]
-    residual_pairs(2 * HALO, own // 2 - HALO, 0, rows, ub, f, m, diag, faces, pairs)
+    residual_pairs(2 * HALO, own // 2 - HALO, 0, rows, ub, f, m, diag, faces, pairs, True)
     packet_mid[...] = pool_pairs(pairs, pooled)
 
 
-def outer_kernel(place, u_mid, packet_mid, u_edge, f_edge, m_edge, xlo, xhi, u_out, packet,
+def outer_kernel(place, u_mid, packet_mid, u_edge, f_edge, m_edge, xlo, xhi, clo, chi, u_out, packet,
                  ua, ub, f, m, cx, cym, cyp, czm, czp, weight, diag, pairs, pooled):
     own, rows = u_out.shape[1:3]
     planes = m.shape[1]
     count_f = HALO - 1
     at_f, at_m = 3 * HALO, 3 * HALO + 3 * count_f
     half = own // 2
-    for end, halo in ((0, xlo), (1, xhi)):
+    corner_shape = clo.shape[1:]
+    for end, halo, corner in ((0, xlo, clo), (1, xhi, chi)):
         outer = 0 if end == 0 else planes - HALO
         inner = HALO if end == 0 else 0
         present = place[0] > 0 if end == 0 else place[0] < place[2] - 1
-        inside = inside_rows(place, rows, m.shape[2], m.shape[2:], present)
+        inside = inside_rows(place, 0, 2 * HALO, corner_shape, present)
+
+        def put_corner(field, channel, masked):
+            at, deep = corner_layers(channel)
+            value = corner[at:at + deep]
+            if masked:
+                value = jnp.where(inside, value, 0.0)
+            first = HALO - deep if end == 0 else planes - HALO
+            field[first:first + deep, rows:] = value
+            far = first - 1 if end == 0 else first + deep
+            field[far, rows:] = jnp.zeros(corner_shape, jnp.float32)
+
         for c in range(3):
-            ua[end, c, outer:outer + HALO] = jnp.where(inside, halo[HALO * c:HALO * (c + 1)], 0.0)
+            ua[end, c, outer:outer + HALO, :rows] = jnp.where(present, halo[HALO * c:HALO * (c + 1)], 0.0)
+            put_corner(ua.at[end, c], c, True)
             nearest = HALO if end == 0 else planes - HALO - 2
             ua[end, c, nearest:nearest + 2] = u_edge[0, end, c]
             beyond = 1 if end == 0 else planes - HALO
-            f[end, c, beyond:beyond + count_f] = halo[at_f + count_f * c:at_f + count_f * (c + 1)]
+            f[end, c, beyond:beyond + count_f, :rows] = halo[at_f + count_f * c:at_f + count_f * (c + 1)]
+            put_corner(f.at[end, c], 3 + c, False)
             own_f = HALO if end == 0 else planes - 2 * HALO
             f[end, c, own_f:own_f + HALO] = f_edge[end, c]
-        m[end, outer:outer + HALO] = jnp.where(inside, halo[at_m:], 0.0)
+        m[end, outer:outer + HALO, :rows] = jnp.where(present, halo[at_m:], 0.0)
+        put_corner(m.at[end], 6, True)
         m[end, inner:inner + HALO + 1] = m_edge[end]
         parts = (cx.at[end], cym.at[end], cyp.at[end], czm.at[end], czp.at[end])
         u_a, u_b, f_e, w_e, d_e = ua.at[end], ub.at[end], f.at[end], weight.at[end], diag.at[end]
-        make_coefficients(1.0, 1, planes - 1, m.at[end], *parts, w_e, d_e)
+        make_coefficients(1.0, 1, planes - 1, m.at[end], *parts, w_e, d_e, True)
         for stage, (source, target) in enumerate(((u_a, u_b), (u_b, u_a), (u_a, u_b))):
             first = 1 + stage if end == 0 else planes - 1 - HALO - stage
-            relax(first, first + HALO, source, target, f_e, w_e, parts)
+            relax(first, first + HALO, source, target, f_e, w_e, parts, True)
             known = first + HALO if end == 0 else first - 2
             for c in range(3):
                 target[c, known:known + 2] = u_edge[stage + 1, end, c]
         at = HALO if end == 0 else 1
-        residual_pairs(at, HALO // 2, HALO // 2 * end, rows, u_b, f_e, m.at[end], d_e, parts, pairs)
+        residual_pairs(at, HALO // 2, HALO // 2 * end, rows, u_b, f_e, m.at[end], d_e, parts, pairs, True)
         for c in range(3):
             if end == 0:
                 u_out[c, :HALO - 1] = ub[end, c, HALO:2 * HALO - 1, :rows]
@@ -377,19 +392,56 @@
         r4_out[c, 0] = ends[3 + c:4 + c, :16]
 
 
-def pack_kernel(viscosities, u_in, f_in, types, up, down, viscosity):
-    rows = u_in.shape[2]
-    kind = types[...]
-    value = jnp.where(
+def viscosity_of(kind, viscosities):
+    return jnp.where(
         kind < 2,
         jnp.where(kind == 0, viscosities[0], viscosities[1]),
         jnp.where(kind == 2, viscosities[2], viscosities[3]),
     )
-    viscosity[...] = value
+
+
+def pack_kernel(viscosities, u_in, f_in, types, y_up, y_down, x_up, x_down, kinds, done):
+    own, rows = types.shape[:2]
+    pairs = [(types, kinds)]
+    at = 3 * HALO
     for c in range(3):
-        up[c], down[c] = u_in[c, :, rows - HALO:], u_in[c, :, :HALO]
-        up[3 + c], down[3 + c] = f_in[c, :, rows - HALO:], f_in[c, :, :HALO]
-    up[6], down[6] = value[:, rows - HALO:], value[:, :HALO]
+        for k, field in ((0, u_in), (3, f_in)):
+            pairs.append((field.at[c, :, pl.ds(rows - HALO, HALO)], y_up.at[k + c]))
+            pairs.append((field.at[c, :, pl.ds(0, HALO)], y_down.at[k + c]))
+        pairs.append((u_in.at[c, pl.ds(own - HALO, HALO)], x_up.at[pl.ds(HALO * c, HALO)]))
+        pairs.append((u_in.at[c, pl.ds(0, HALO)], x_down.at[pl.ds(HALO * c, HALO)]))
+        pairs.append((f_in.at[c, pl.ds(own - HALO + 1, HALO - 1)], x_up.at[pl.ds(at, HALO - 1)]))
+        pairs.append((f_in.at[c, pl.ds(0, HALO - 1)], x_down.at[pl.ds(at, HALO - 1)]))
+        at += HALO - 1
+    copies = [pltpu.make_async_copy(*pair, done.at[i]) for i, pair in enumerate(pairs)]
+    for copy in copies:
+        copy.start()
+    copies[0].wait()
+    y_up[6] = viscosity_of(kinds[:, rows - HALO:], viscosities)
+    y_down[6] = viscosity_of(kinds[:, :HALO], viscosities)
+    x_up[at:] = viscosity_of(kinds[own - HALO:], viscosities)
+    x_down[at:] = viscosity_of(kinds[:HALO], viscosities)
+    for copy in copies[1:]:
+        copy.wait()
+
+
+def corner_layers(count):
+    at = 0
+    for channel in range(7):
+        deep = HALO - 2 if 3 <= channel < 6 else HALO - 1
+        if channel == count:
+            return at, deep
+        at += deep
+    return at, 0
+
+
+def corner_kernel(ylo, yhi, up, down):
+    own = ylo.shape[1]
+    for channel in range(7):
+        at, deep = corner_layers(channel)
+        for target, first in ((up, own - deep), (down, 0)):
+            target[at:at + deep, :HALO] = yhi[channel, first:first + deep]
+            target[at:at + deep, HALO:] = ylo[channel, first:first + deep]
 
 
 def on_chip(count):
@@ -405,6 +457,7 @@
     )
 
 
+PACK_LIMIT = 62 * 1024 * 1024
 LIMIT = pltpu.CompilerParams(vmem_limit_bytes=20 * 1024 * 1024)
 
 
@@ -414,33 +467,30 @@
     place = jnp.stack([lax.axis_index("gx"), lax.axis_index("gy"), count_x, count_y]).astype(jnp.int32)
     in_smem = [pl.BlockSpec(memory_space=pltpu.SMEM)]
     own, rows, lanes = cell_type.shape
-    edge = jax.ShapeDtypeStruct((7, own, HALO, lanes), f32)
-    up, down, viscosity = pl.pallas_call(
+    y_edge = jax.ShapeDtypeStruct((7, own, HALO, lanes), f32)
+    x_edge = jax.ShapeDtypeStruct((7 * HALO - 3, rows, lanes), f32)
+    y_up, y_down, x_up, x_down = pl.pallas_call(
         pack_kernel,
-        out_shape=(edge, edge, jax.ShapeDtypeStruct(cell_type.shape, f32)),
-        in_specs=in_smem + on_chip(3),
-        out_specs=tuple(on_chip(3)),
+        out_shape=(y_edge, y_edge, x_edge, x_edge),
+        in_specs=in_smem + [pl.BlockSpec(memory_space=pl.ANY)] * 3,
+        out_specs=tuple(on_chip(4)),
+        scratch_shapes=[pltpu.VMEM(cell_type.shape, jnp.int32), pltpu.SemaphoreType.DMA((25,))],
+        compiler_params=pltpu.CompilerParams(vmem_limit_bytes=PACK_LIMIT),
+    )(viscosities, velocity_guess, forcing, cell_type)
+    ylo = passed_round(y_up, "gy", 1)
+    yhi = passed_round(y_down, "gy", -1)
+    xlo = passed_round(x_up, "gx", 1)
+    xhi = passed_round(x_down, "gx", -1)
+    corner = jax.ShapeDtypeStruct((corner_layers(7)[0], 2 * HALO, lanes), f32)
+    up, down = pl.pallas_call(
+        corner_kernel,
+        out_shape=(corner, corner),
+        in_specs=on_chip(2),
+        out_specs=tuple(on_chip(2)),
         compiler_params=LIMIT,
-    )(viscosities, velocity_guess, forcing, cell_type)
-    ylo = passed_round(up, "gy", 1)
-    yhi = passed_round(down, "gy", -1)
-
-    def wide(first, *inner):
-        def layers(own_part, at, layer):
-            part = jnp.concatenate([own_part[:, layer], yhi[at, layer], ylo[at, layer]], axis=2)
-            return part.reshape(-1, rows + 2 * HALO, lanes)
-
-        return jnp.concatenate(
-            [
-                layers(velocity_guess, slice(0, 3), slice(first, first + HALO)),
-                layers(forcing, slice(3, 6), slice(*inner)),
-                layers(viscosity[None], slice(6, 7), slice(first, first + HALO)),
-            ],
-            axis=0,
-        )
-
-    xlo = passed_round(wide(own - HALO, own - HALO + 1, own), "gx", 1)
-    xhi = passed_round(wide(0, 0, HALO - 1), "gx", -1)
+    )(ylo, yhi)
+    clo = passed_round(up, "gx", 1)
+    chi = passed_round(down, "gx", -1)
     tall = rows + 2 * HALO
     middle = own // 2 - HALO
     state = (
@@ -453,23 +503,23 @@
     known = pl.pallas_call(
         inner_kernel,
         out_shape=tuple(jax.ShapeDtypeStruct(shape, f32) for shape in state),
-        in_specs=in_smem + on_chip(5),
+        in_specs=in_smem * 2 + on_chip(5),
         out_specs=tuple(on_chip(5)),
         scratch_shapes=planes_scratch(own + 2 * HALO, tall, lanes, middle, rows, (4 * middle, rows, 128)),
         compiler_params=LIMIT,
         cost_estimate=pl.CostEstimate(flops=60_000_000, bytes_accessed=6_000_000, transcendentals=0),
-    )(place, velocity_guess, forcing, viscosity, ylo, yhi)
+    )(place, viscosities, velocity_guess, forcing, cell_type, ylo, yhi)
     u0, packet = pl.pallas_call(
         outer_kernel,
         out_shape=(
             jax.ShapeDtypeStruct(velocity_guess.shape, f32),
             jax.ShapeDtypeStruct((4 * own // 2, rows // 2, lanes // 2), f32),
         ),
-        in_specs=in_smem + on_chip(7),
+        in_specs=in_smem + on_chip(9),
         out_specs=tuple(on_chip(2)),
         scratch_shapes=planes_scratch(2 * HALO + 1, tall, lanes, HALO, rows, (4 * HALO, rows, 128), (2,)),
         compiler_params=LIMIT,
-    )(place, *known, xlo, xhi)
+    )(place, *known, xlo, xhi, clo, chi)
     results = [u0]
     for grid_level in (1, 2):
         own, rows = own // 2, rows // 2

time: 111 us -> 102 us (0.919)
  local copies, waits for them, and re-layouts: 4.15 us -> 0.19 us
  other arithmetic: 2.09 us -> 0.19 us
  Pallas kernels: 23.8 us -> 22 us
  starting transfers between devices: 21.4 us -> 23.2 us
  waiting for transfers between devices: 20.3 us -> 18.8 us
    unnamed x12 -> x8, local copies, waits for them, and re-layouts: 3.88 us -> 0.02 us
    pallas_call x1 -> x2, Pallas kernels: 0.64 us -> 4.32 us  [the longest x1 3.58 us: on_device(): pl.pallas_call(pack_kernel, out_shape=(y_edge, y_edge, x_edge, x_edge), i...]
    pallas_call x1, Pallas kernels: 7.22 us -> 4.29 us  [on_device(): pl.pallas_call(inner_kernel, out_shape=tuple((jax.ShapeDtypeStruct(shape,...]
    pallas_call x1, Pallas kernels: 7.06 us -> 4.53 us  [on_device(): pl.pallas_call(outer_kernel, out_shape=(jax.ShapeDtypeStruct(velocity_gue...]
    concatenate x4 -> x0, other arithmetic: 1.86 us -> none  [the longest x2 1.74 us: wide(): jnp.concatenate([layers(velocity_guess, slice(0, 3), slice(first, first +...]
    ppermute x12 -> x14, starting transfers between devices: 21.4 us -> 23.2 us  [passed_round(): lax.ppermute(value, axis, [(source, (source + steps) % count) for source...]
    ppermute x12 -> x14, waiting for transfers between devices: 20.3 us -> 18.8 us  [passed_round(): lax.ppermute(value, axis, [(source, (source + steps) % count) for source...]
  transfers between devices with their start and end apart: 12 -> 14, of which waited for: 6 -> 5; matrix products, arithmetic and copies ran while one was open for 1% -> 0% of each run, Pallas kernels for 7% -> 5%
where the time goes in v3:
time: 102 us; the launch traced here: 101 us
  blocking collectives  36.3 us (36%)
  starting transfers between devices  23.2 us (23%)
  Pallas kernels  22 us (22%)
  waiting for transfers between devices  18.8 us (18%)
    ppermute x14, starting transfers between devices, passed_round(): lax.ppermute(value, axis, [(source, (source + steps) % count) for source...  23.2 us
    ppermute x14, waiting for transfers between devices, passed_round(): lax.ppermute(value, axis, [(source, (source + steps) % count) for source...  18.8 us
    all_to_all x1, blocking collectives, on_device(): lax.all_to_all(jnp.broadcast_to(column[None], (count_y, 4, count_x, 128))...  18.3 us
    all_to_all x1, blocking collectives, on_device(): lax.all_to_all(jnp.broadcast_to(packet[None], (count_x, 4, 128)), 'gx', 0...  18 us
    pallas_call x1, Pallas kernels, on_device(): pl.pallas_call(last_kernel, out_shape=tuple((jax.ShapeDtypeStruct(shape,...  5.48 us
    pallas_call x1, Pallas kernels, on_device(): pl.pallas_call(outer_kernel, out_shape=(jax.ShapeDtypeStruct(velocity_gue...  4.53 us
    pallas_call x1, Pallas kernels, on_device(): pl.pallas_call(inner_kernel, out_shape=tuple((jax.ShapeDtypeStruct(shape,...  4.29 us
    pallas_call x1, Pallas kernels, on_device(): pl.pallas_call(pack_kernel, out_shape=(y_edge, y_edge, x_edge, x_edge), i...  3.58 us
  transfers between devices with their start and end apart: 14, of which 5 were waited for; matrix products, arithmetic and copies ran while one was open for 0% of the time, Pallas kernels for 5%

profile of v3, /device:TPU:32, one launch (start us, length us, event | category | flops | bytes accessed | tf_op | source)
XLA Modules:
  0.0 101.4 jit_solution(3379501949559158068)
XLA Ops:
  0.7 3.6 %shard_map.91 = (f32[7,16,4,256]{3,2,1,0:T(4,128)}, f32[7,16,4,256]{3,2,1,0:T(4,128)}, f32[25,16,256]{2,1,0:T(8,128)}, f32[25,16,256]{2,1,0:T(8,128)}) custom-call(f32[4]{0:T(128)} %viscosities.3, f32[3,16,16,256]{3,2,1,0:T(8,128)} %u_in.3, f32[3,16,16,256]{3,2,1,0:T(8,128)} %f_in.3, s32[16,16,256]{2,1,0:T(8,128)} %types.3), custom_call_target="tpu_custom_call" | custom-call | tf_op jit(solution)/shard_map/pallas_call | solution.py:472
  4.3 1.7 %collective-permute-start = (f32[7,16,4,256]{3,2,1,0:T(4,128)}, f32[7,16,4,256]{3,2,1,0:T(4,128)S(1)}, u32[]{:S(2)}, u32[]{:S(2)}) collective-permute-start(f32[7,16,4,256]{3,2,1,0:T(4,128)} %get-tuple-element.26), channel_id=1, source_target_pairs={{0,1},{1,2},{2,3},{3,4},{4,5},{5,6},{6,7},{7,8},{8,9},{9,10},{10,1... | collective-permute-start | bytes 1376264 | tf_op jit(solution)/shard_map/ppermute | solution.py:21
  5.9 3.8 %collective-permute-start.1 = (f32[7,16,4,256]{3,2,1,0:T(4,128)}, f32[7,16,4,256]{3,2,1,0:T(4,128)S(1)}, u32[]{:S(2)}, u32[]{:S(2)}) collective-permute-start(f32[7,16,4,256]{3,2,1,0:T(4,128)} %get-tuple-element.27), channel_id=1, source_target_pairs={{0,15},{1,0},{2,1},{3,2},{4,3},{5,4},{6,5},{7,6},{8,7},{9,8},{10,9... | collective-permute-start | bytes 1376264 | tf_op jit(solution)/shard_map/ppermute | solution.py:21
  9.7 0.0 collective-permute-start.2
  9.7 1.7 %collective-permute-start.3 = (f32[25,16,256]{2,1,0:T(8,128)}, f32[25,16,256]{2,1,0:T(8,128)}, u32[]{:S(2)}, u32[]{:S(2)}) collective-permute-start(f32[25,16,256]{2,1,0:T(8,128)} %get-tuple-element.34), channel_id=1, source_target_pairs={{0,240},{16,0},{32,16},{48,32},{64,48},{80,64},{96,80},{112,96},{1... | collective-permute-start | bytes 1228808 | tf_op jit(solution)/shard_map/ppermute | solution.py:21
  11.4 8.8 %collective-permute-done.ylo = f32[7,16,4,256]{3,2,1,0:T(4,128)S(1)} collective-permute-done((f32[7,16,4,256]{3,2,1,0:T(4,128)}, f32[7,16,4,256]{3,2,1,0:T(4,128)S(1)}, u32[]{:S(2)}, u32[]{:S(2)}) %collective-permute-start) | collective-permute-done | bytes 458784 | tf_op jit(solution)/shard_map/ppermute | solution.py:21
  20.3 0.7 shard_map.93
  21.0 0.0 collective-permute-start.4
  21.0 1.7 %collective-permute-start.5 = (f32[18,8,256]{2,1,0:T(8,128)}, f32[18,8,256]{2,1,0:T(8,128)}, u32[]{:S(2)}, u32[]{:S(2)}) collective-permute-start(f32[18,8,256]{2,1,0:T(8,128)} %get-tuple-element.36), channel_id=1, source_target_pairs={{0,240},{16,0},{32,16},{48,32},{64,48},{80,64},{96,80},{112,96},{1... | collective-permute-start | bytes 442376 | tf_op jit(solution)/shard_map/ppermute | solution.py:21
  22.8 0.1 pad_add_fusion.place
  22.9 4.3 %shard_map.92 = (f32[3,10,16,256]{3,2,1,0:T(8,128)S(1)}, f32[16,8,128]{2,1,0:T(8,128)S(1)}, f32[4,2,3,2,24,256]{5,4,3,2,1,0:T(8,128)S(1)}, f32[2,3,4,24,256]{4,3,2,1,0:T(8,128)S(1)}, f32[2,5,24,256]{3,2,1,0:T(8,128)S(1)}) custom-call(s32[4]{0:T(128)S(1)} %pad_add_fusion.place, f32[4]{0:T(128)S(1)} %copy-done.3, f32[3,16,16,256]{3,2,1,0:T(8,128)S(1)} %copy-done, ...), custom_call_target="tpu_custom_call" | custom-call | flops 60000000 | bytes 6000000 | tf_op jit(solution)/shard_map/pallas_call | solution.py:503
  27.2 0.0 collective-permute-done.2.xlo
  27.2 0.0 collective-permute-done.4.clo
  27.2 4.5 %shard_map.94 = (f32[3,16,16,256]{3,2,1,0:T(8,128)}, f32[32,8,128]{2,1,0:T(8,128)S(1)}) custom-call(s32[4]{0:T(128)S(1)} %pad_add_fusion.place, f32[3,10,16,256]{3,2,1,0:T(8,128)S(1)} %get-tuple-element.28.u_mid, f32[16,8,128]{2,1,0:T(8,128)S(1)} %get-tuple-element.29.packet_mid, f32[4,2,3,2,24,256]{5,4,3,2,1,0:T(8,128)S(1)} %get-tuple-element.30.u_edge, ...), custom_call_target="tpu_custom_call" | custom-call | tf_op jit(solution)/shard_map/pallas_call | solution.py:512
  31.8 0.1 collective-permute-start.6
  31.8 5.3 %collective-permute-start.7 = (f32[4,8,4,128]{3,2,1,0:T(4,128)S(1)}, f32[4,8,4,128]{3,2,1,0:T(4,128)S(1)}, u32[]{:S(2)}, u32[]{:S(2)}) collective-permute-start(f32[4,8,4,128]{3,2,1,0:T(4,128)S(1)} %get-tuple-element.48), channel_id=1, source_target_pairs={{0,15},{1,0},{2,1},{3,2},{4,3},{5,4},{6,5},{7,6},{8,7},{9,8},{10,9... | collective-permute-start | bytes 196616 | tf_op jit(solution)/shard_map/ppermute | solution.py:21
  37.2 2.8 %collective-permute-done.6.ylo = f32[4,8,4,128]{3,2,1,0:T(4,128)S(1)} collective-permute-done((f32[4,8,4,128]{3,2,1,0:T(4,128)S(1)}, f32[4,8,4,128]{3,2,1,0:T(4,128)S(1)}, u32[]{:S(2)}, u32[]{:S(2)}) %collective-permute-start.6) | collective-permute-done | bytes 65568 | tf_op jit(solution)/shard_map/ppermute | solution.py:21
  40.0 0.0 collective-permute-start.8
  40.1 1.7 %collective-permute-start.9 = (f32[4,4,16,128]{3,2,1,0:T(8,128)S(1)}, f32[4,4,16,128]{3,2,1,0:T(8,128)S(1)}, u32[]{:S(2)}, u32[]{:S(2)}) collective-permute-start(f32[4,4,16,128]{3,2,1,0:T(8,128)S(1)} %get-tuple-element.46), channel_id=1, source_target_pairs={{0,240},{16,0},{32,16},{48,32},{64,48},{80,64},{96,80},{112,96},{1... | collective-permute-start | bytes 393224 | tf_op jit(solution)/shard_map/ppermute | solution.py:21
  41.8 2.6 %collective-permute-done.8.xlo = f32[4,4,16,128]{3,2,1,0:T(8,128)S(1)} collective-permute-done((f32[4,4,16,128]{3,2,1,0:T(8,128)S(1)}, f32[4,4,16,128]{3,2,1,0:T(8,128)S(1)}, u32[]{:S(2)}, u32[]{:S(2)}) %collective-permute-start.8) | collective-permute-done | bytes 131104 | tf_op jit(solution)/shard_map/ppermute | solution.py:21
  44.4 1.7 %shard_map.95 = (f32[3,8,8,128]{3,2,1,0:T(8,128)}, f32[16,4,128]{2,1,0:T(4,128)S(1)}) custom-call(s32[4]{0:T(128)S(1)} %pad_add_fusion.place, f32[4,8,8,128]{3,2,1,0:T(8,128)S(1)} %bitcast.7, f32[4,8,4,128]{3,2,1,0:T(4,128)S(1)} %collective-permute-done.6.ylo, f32[4,8,4,128]{3,2,1,0:T(4,128)S(1)} %collective-permute-done.7.yhi, ...), custom_call_target="tpu_custom_call" | custom-call | tf_op jit(solution)/shard_map/pallas_call | solution.py:542
  46.1 5.3 %collective-permute-start.11 = (f32[4,4,4,128]{3,2,1,0:T(4,128)S(1)}, f32[4,4,4,128]{3,2,1,0:T(4,128)S(1)}, u32[]{:S(2)}, u32[]{:S(2)}) collective-permute-start(f32[4,4,4,128]{3,2,1,0:T(4,128)S(1)} %bitcast.9), channel_id=1, source_target_pairs={{0,15},{1,0},{2,1},{3,2},{4,3},{5,4},{6,5},{7,6},{8,7},{9,8},{10,9... | collective-permute-start | bytes 98312 | tf_op jit(solution)/shard_map/ppermute | solution.py:21
  51.5 0.1 pad.2.clone
  51.6 1.8 %collective-permute-done.10.ylo = f32[4,4,4,128]{3,2,1,0:T(4,128)S(1)} collective-permute-done((f32[4,4,4,128]{3,2,1,0:T(4,128)S(1)}, f32[4,4,4,128]{3,2,1,0:T(4,128)S(1)}, u32[]{:S(2)}, u32[]{:S(2)}) %collective-permute-start.10) | collective-permute-done | bytes 32800 | tf_op jit(solution)/shard_map/ppermute | solution.py:21
  53.4 0.1 pad_maximum_fusion.1
  53.5 1.0 collective-permute-start.12
  54.4 0.8 collective-permute-start.13
  55.2 2.6 %collective-permute-done.12.xlo = f32[4,4,16,128]{3,2,1,0:T(8,128)S(1)} collective-permute-done((f32[4,4,16,128]{3,2,1,0:T(8,128)S(1)}, f32[4,4,16,128]{3,2,1,0:T(8,128)S(1)}, u32[]{:S(2)}, u32[]{:S(2)}) %collective-permute-start.12) | collective-permute-done | bytes 131104 | tf_op jit(solution)/shard_map/ppermute | solution.py:21
  57.9 1.7 %shard_map.96 = (f32[3,4,4,64]{3,2,1,0:T(4,128)}, f32[4,128]{1,0:T(4,128)S(1)}) custom-call(s32[4]{0:T(128)S(1)} %pad_add_fusion.place, f32[4,4,4,128]{3,2,1,0:T(4,128)S(1)} %bitcast.11, f32[4,4,4,128]{3,2,1,0:T(4,128)S(1)} %collective-permute-done.10.ylo, f32[4,4,4,128]{3,2,1,0:T(4,128)S(1)} %collective-permute-done.11.yhi, ...), custom_call_target="tpu_custom_call" | custom-call | tf_op jit(solution)/shard_map/pallas_call | solution.py:542
  59.5 18.0 %all_to_all.10 = f32[16,4,128]{2,1,0:T(4,128)S(1)} all-to-all(f32[16,4,128]{2,1,0:T(4,128)S(1)} %broadcast_in_dim.7), channel_id=1, replica_groups=mesh['gx'=16,'gy'=16] {'gx'}, dimensions={0} | all-to-all | bytes 65536 | tf_op jit(solution)/shard_map/all_to_all | solution.py:554
  77.6 18.3 %all_to_all.11.g = f32[16,4,16,128]{3,2,1,0:T(8,128)S(1)} all-to-all(f32[16,4,16,128]{3,2,1,0:T(8,128)S(1)} %broadcast_in_dim.8), channel_id=1, replica_groups=mesh['gx'=16,'gy'=16] {'gy'}, dimensions={0} | all-to-all | bytes 1048576 | tf_op jit(solution)/shard_map/all_to_all | solution.py:556
  95.9 5.5 %shard_map.97 = (f32[3,2,2,32]{3,2,1,0:T(2,128)}, f32[3,1,1,16]{3,2,1,0:T(1,128)}, f32[3,1,1,16]{3,2,1,0:T(1,128)}) custom-call(s32[4]{0:T(128)S(1)} %pad_add_fusion.place, f32[16,4,16,128]{3,2,1,0:T(8,128)S(1)} %all_to_all.11.g), custom_call_target="tpu_custom_call" | custom-call | tf_op jit(solution)/shard_map/pallas_call | solution.py:561
  (24 shorter events, 0.2 us)
Async XLA Ops:
  0.6 22.2 %copy-start = (f32[3,16,16,256]{3,2,1,0:T(8,128)S(1)}, f32[3,16,16,256]{3,2,1,0:T(8,128)}, u32[]{:S(2)}) copy-start(f32[3,16,16,256]{3,2,1,0:T(8,128)} %u_in.3) | copy-start | bytes 2359300
  0.6 22.2 %copy-start.1 = (f32[3,16,16,256]{3,2,1,0:T(8,128)S(1)}, f32[3,16,16,256]{3,2,1,0:T(8,128)}, u32[]{:S(2)}) copy-start(f32[3,16,16,256]{3,2,1,0:T(8,128)} %f_in.3) | copy-start | bytes 2359300
  0.7 22.2 %copy-start.2 = (s32[16,16,256]{2,1,0:T(8,128)S(1)}, s32[16,16,256]{2,1,0:T(8,128)}, u32[]{:S(2)}) copy-start(s32[16,16,256]{2,1,0:T(8,128)} %types.3) | copy-start | bytes 786436
  0.7 22.2 %copy-start.3 = (f32[4]{0:T(128)S(1)}, f32[4]{0:T(128)}, u32[]{:S(2)}) copy-start(f32[4]{0:T(128)} %viscosities.3) | copy-start | bytes 52
  4.3 16.0 %collective-permute-start = (f32[7,16,4,256]{3,2,1,0:T(4,128)}, f32[7,16,4,256]{3,2,1,0:T(4,128)S(1)}, u32[]{:S(2)}, u32[]{:S(2)}) collective-permute-start(f32[7,16,4,256]{3,2,1,0:T(4,128)} %get-tuple-element.26), channel_id=1, source_target_pairs={{0,1},{1,2},{2,3},{3,4},{4,5},{5,6},{6,7},{7,8},{8,9},{9,10},{10,1... | collective-permute-start | bytes 1376264 | tf_op jit(solution)/shard_map/ppermute | solution.py:21
  5.9 14.4 %collective-permute-start.1 = (f32[7,16,4,256]{3,2,1,0:T(4,128)}, f32[7,16,4,256]{3,2,1,0:T(4,128)S(1)}, u32[]{:S(2)}, u32[]{:S(2)}) collective-permute-start(f32[7,16,4,256]{3,2,1,0:T(4,128)} %get-tuple-element.27), channel_id=1, source_target_pairs={{0,15},{1,0},{2,1},{3,2},{4,3},{5,4},{6,5},{7,6},{8,7},{9,8},{10,9... | collective-permute-start | bytes 1376264 | tf_op jit(solution)/shard_map/ppermute | solution.py:21
  9.7 17.5 %collective-permute-start.2 = (f32[25,16,256]{2,1,0:T(8,128)}, f32[25,16,256]{2,1,0:T(8,128)}, u32[]{:S(2)}, u32[]{:S(2)}) collective-permute-start(f32[25,16,256]{2,1,0:T(8,128)} %get-tuple-element.33), channel_id=1, source_target_pairs={{0,16},{16,32},{32,48},{48,64},{64,80},{80,96},{96,112},{112,128},... | collective-permute-start | bytes 1228808 | tf_op jit(solution)/shard_map/ppermute | solution.py:21
  9.7 17.5 %collective-permute-start.3 = (f32[25,16,256]{2,1,0:T(8,128)}, f32[25,16,256]{2,1,0:T(8,128)}, u32[]{:S(2)}, u32[]{:S(2)}) collective-permute-start(f32[25,16,256]{2,1,0:T(8,128)} %get-tuple-element.34), channel_id=1, source_target_pairs={{0,240},{16,0},{32,16},{48,32},{64,48},{80,64},{96,80},{112,96},{1... | collective-permute-start | bytes 1228808 | tf_op jit(solution)/shard_map/ppermute | solution.py:21
  21.0 6.2 %collective-permute-start.4 = (f32[18,8,256]{2,1,0:T(8,128)}, f32[18,8,256]{2,1,0:T(8,128)S(1)}, u32[]{:S(2)}, u32[]{:S(2)}) collective-permute-start(f32[18,8,256]{2,1,0:T(8,128)} %get-tuple-element.35), channel_id=1, source_target_pairs={{0,16},{16,32},{32,48},{48,64},{64,80},{80,96},{96,112},{112,128},... | collective-permute-start | bytes 442376 | tf_op jit(solution)/shard_map/ppermute | solution.py:21
  21.0 6.2 %collective-permute-start.5 = (f32[18,8,256]{2,1,0:T(8,128)}, f32[18,8,256]{2,1,0:T(8,128)}, u32[]{:S(2)}, u32[]{:S(2)}) collective-permute-start(f32[18,8,256]{2,1,0:T(8,128)} %get-tuple-element.36), channel_id=1, source_target_pairs={{0,240},{16,0},{32,16},{48,32},{64,48},{80,64},{96,80},{112,96},{1... | collective-permute-start | bytes 442376 | tf_op jit(solution)/shard_map/ppermute | solution.py:21
  31.8 8.2 %collective-permute-start.6 = (f32[4,8,4,128]{3,2,1,0:T(4,128)S(1)}, f32[4,8,4,128]{3,2,1,0:T(4,128)S(1)}, u32[]{:S(2)}, u32[]{:S(2)}) collective-permute-start(f32[4,8,4,128]{3,2,1,0:T(4,128)S(1)} %get-tuple-element.49), channel_id=1, source_target_pairs={{0,1},{1,2},{2,3},{3,4},{4,5},{5,6},{6,7},{7,8},{8,9},{9,10},{10,1... | collective-permute-start | bytes 196616 | tf_op jit(solution)/shard_map/ppermute | solution.py:21
  31.8 8.1 %collective-permute-start.7 = (f32[4,8,4,128]{3,2,1,0:T(4,128)S(1)}, f32[4,8,4,128]{3,2,1,0:T(4,128)S(1)}, u32[]{:S(2)}, u32[]{:S(2)}) collective-permute-start(f32[4,8,4,128]{3,2,1,0:T(4,128)S(1)} %get-tuple-element.48), channel_id=1, source_target_pairs={{0,15},{1,0},{2,1},{3,2},{4,3},{5,4},{6,5},{7,6},{8,7},{9,8},{10,9... | collective-permute-start | bytes 196616 | tf_op jit(solution)/shard_map/ppermute | solution.py:21
  40.0 4.4 %collective-permute-start.8 = (f32[4,4,16,128]{3,2,1,0:T(8,128)S(1)}, f32[4,4,16,128]{3,2,1,0:T(8,128)S(1)}, u32[]{:S(2)}, u32[]{:S(2)}) collective-permute-start(f32[4,4,16,128]{3,2,1,0:T(8,128)S(1)} %get-tuple-element.47), channel_id=1, source_target_pairs={{0,16},{16,32},{32,48},{48,64},{64,80},{80,96},{96,112},{112,128},... | collective-permute-start | bytes 393224 | tf_op jit(solution)/shard_map/ppermute | solution.py:21
  40.1 4.4 %collective-permute-start.9 = (f32[4,4,16,128]{3,2,1,0:T(8,128)S(1)}, f32[4,4,16,128]{3,2,1,0:T(8,128)S(1)}, u32[]{:S(2)}, u32[]{:S(2)}) collective-permute-start(f32[4,4,16,128]{3,2,1,0:T(8,128)S(1)} %get-tuple-element.46), channel_id=1, source_target_pairs={{0,240},{16,0},{32,16},{48,32},{64,48},{80,64},{96,80},{112,96},{1... | collective-permute-start | bytes 393224 | tf_op jit(solution)/shard_map/ppermute | solution.py:21
  46.1 7.2 %collective-permute-start.10 = (f32[4,4,4,128]{3,2,1,0:T(4,128)S(1)}, f32[4,4,4,128]{3,2,1,0:T(4,128)S(1)}, u32[]{:S(2)}, u32[]{:S(2)}) collective-permute-start(f32[4,4,4,128]{3,2,1,0:T(4,128)S(1)} %bitcast.8), channel_id=1, source_target_pairs={{0,1},{1,2},{2,3},{3,4},{4,5},{5,6},{6,7},{7,8},{8,9},{9,10},{10,1... | collective-permute-start | bytes 98312 | tf_op jit(solution)/shard_map/ppermute | solution.py:21
  46.1 7.2 %collective-permute-start.11 = (f32[4,4,4,128]{3,2,1,0:T(4,128)S(1)}, f32[4,4,4,128]{3,2,1,0:T(4,128)S(1)}, u32[]{:S(2)}, u32[]{:S(2)}) collective-permute-start(f32[4,4,4,128]{3,2,1,0:T(4,128)S(1)} %bitcast.9), channel_id=1, source_target_pairs={{0,15},{1,0},{2,1},{3,2},{4,3},{5,4},{6,5},{7,6},{8,7},{9,8},{10,9... | collective-permute-start | bytes 98312 | tf_op jit(solution)/shard_map/ppermute | solution.py:21
  53.5 4.4 %collective-permute-start.12 = (f32[4,4,16,128]{3,2,1,0:T(8,128)S(1)}, f32[4,4,16,128]{3,2,1,0:T(8,128)S(1)}, u32[]{:S(2)}, u32[]{:S(2)}) collective-permute-start(f32[4,4,16,128]{3,2,1,0:T(8,128)S(1)} %pad_maximum_fusion.1), channel_id=1, source_target_pairs={{0,16},{16,32},{32,48},{48,64},{64,80},{80,96},{96,112},{112,128},... | collective-permute-start | bytes 393224 | tf_op jit(solution)/shard_map/ppermute | solution.py:21
  54.4 3.4 %collective-permute-start.13 = (f32[4,4,16,128]{3,2,1,0:T(8,128)S(1)}, f32[4,4,16,128]{3,2,1,0:T(8,128)S(1)}, u32[]{:S(2)}, u32[]{:S(2)}) collective-permute-start(f32[4,4,16,128]{3,2,1,0:T(8,128)S(1)} %pad_maximum_fusion.1), channel_id=1, source_target_pairs={{0,240},{16,0},{32,16},{48,32},{64,48},{80,64},{96,80},{112,96},{1... | collective-permute-start | bytes 393224 | tf_op jit(solution)/shard_map/ppermute | solution.py:21

commit v4 on v3

--- a/solution.py
+++ b/solution.py
@@ -16,9 +16,32 @@
 mass_term = 0.05
 
 
-def passed_round(value, axis, steps):
-    count = lax.axis_size(axis)
-    return lax.ppermute(value, axis, [(source, (source + steps) % count) for source in range(count)])
+def pair_swap(value, axis, odd):
+    sizes = {name: lax.axis_size(name) for name in ("gx", "gy")}
+    route = []
+    for x in range(sizes["gx"]):
+        for y in range(sizes["gy"]):
+            place = {"gx": x, "gy": y}
+            other = ((place[axis] + odd) ^ 1) - odd
+            if 0 <= other < sizes[axis]:
+                place[axis] = other
+            else:
+                across = "gy" if axis == "gx" else "gx"
+                place[across] ^= 1
+            route.append((x * sizes["gy"] + y, place["gx"] * sizes["gy"] + place["gy"]))
+    return lax.ppermute(value, ("gx", "gy"), route)
+
+
+def swapped(to_even, to_odd, axis):
+    return pair_swap(to_even, axis, 0), pair_swap(to_odd, axis, 1)
+
+
+def own_place():
+    return lax.axis_index("gx"), lax.axis_index("gy"), lax.axis_size("gx"), lax.axis_size("gy")
+
+
+def is_even(position):
+    return position % 2 == 0
 
 
 def split_dot(rows, pool):
@@ -127,22 +150,28 @@
     return pooled[:, pl.ds(0, rows // 2, 2), :] + pooled[:, pl.ds(1, rows // 2, 2), :]
 
 
-def inner_kernel(place, viscosities, u_in, f_in, types, ylo, yhi, u_mid, packet_mid, u_edge, f_edge, m_edge,
+def inner_kernel(viscosities, u_in, f_in, types, y_first, y_second, u_mid, packet_mid, u_edge, f_edge, m_edge,
                  ua, ub, f, m, cx, cym, cyp, czm, czp, weight, diag, pairs, pooled):
+    place = own_place()
     own, rows = u_in.shape[1:3]
     body = pl.ds(HALO, own)
     last = HALO + own
     has_lower, has_upper = place[1] > 0, place[1] < place[3] - 1
+    even = is_even(place[1])
+
+    def put_rows(field, channel, masked):
+        first, second = y_first[channel], y_second[channel]
+        upper, lower = jnp.where(even, first, second), jnp.where(even, second, first)
+        field[body, rows:rows + HALO] = jnp.where(has_upper, upper, 0.0) if masked else upper
+        field[body, rows + HALO:] = jnp.where(has_lower, lower, 0.0) if masked else lower
+
     for c in range(3):
         ua[c, body, :rows] = u_in[c]
-        ua[c, body, rows:rows + HALO] = jnp.where(has_upper, yhi[c], 0.0)
-        ua[c, body, rows + HALO:] = jnp.where(has_lower, ylo[c], 0.0)
+        put_rows(ua.at[c], c, True)
         f[c, body, :rows] = f_in[c]
-        f[c, body, rows:rows + HALO] = yhi[3 + c]
-        f[c, body, rows + HALO:] = ylo[3 + c]
+        put_rows(f.at[c], 3 + c, False)
     m[body, :rows] = viscosity_of(types[...], viscosities)
-    m[body, rows:rows + HALO] = jnp.where(has_upper, yhi[6], 0.0)
-    m[body, rows + HALO:] = jnp.where(has_lower, ylo[6], 0.0)
+    put_rows(m, 6, True)
 
     def edges(stage, u, depth):
         u_edge[stage, 0] = u[:, HALO + depth:HALO + depth + 2]
@@ -164,15 +193,28 @@
     packet_mid[...] = pool_pairs(pairs, pooled)
 
 
-def outer_kernel(place, u_mid, packet_mid, u_edge, f_edge, m_edge, xlo, xhi, clo, chi, u_out, packet,
+def outer_kernel(u_mid, packet_mid, u_edge, f_edge, m_edge, x_first, x_second, corner_first, corner_second, u_out, packet,
                  ua, ub, f, m, cx, cym, cyp, czm, czp, weight, diag, pairs, pooled):
+    place = own_place()
     own, rows = u_out.shape[1:3]
     planes = m.shape[1]
     count_f = HALO - 1
     at_f, at_m = 3 * HALO, 3 * HALO + 3 * count_f
     half = own // 2
-    corner_shape = clo.shape[1:]
-    for end, halo, corner in ((0, xlo, clo), (1, xhi, chi)):
+    corner_shape = corner_first.shape[1:]
+    even, even_y = is_even(place[0]), is_even(place[1])
+
+    for end in range(2):
+        take_first = even if end == 1 else jnp.logical_not(even)
+
+        def halo(at, count):
+            return jnp.where(take_first, x_first[at:at + count], x_second[at:at + count])
+
+        def corner(at, count):
+            rows_of = [corner_first[at + i] for i in range(count)], [corner_second[at + i] for i in range(count)]
+            chosen = [jnp.where(take_first, one, two) for one, two in zip(*rows_of)]
+            return jnp.stack([jnp.where(even_y, one, pltpu.roll(one, HALO, 0)) for one in chosen])
+
         outer = 0 if end == 0 else planes - HALO
         inner = HALO if end == 0 else 0
         present = place[0] > 0 if end == 0 else place[0] < place[2] - 1
@@ -180,7 +222,7 @@
 
         def put_corner(field, channel, masked):
             at, deep = corner_layers(channel)
-            value = corner[at:at + deep]
+            value = corner(at, deep)
             if masked:
                 value = jnp.where(inside, value, 0.0)
             first = HALO - deep if end == 0 else planes - HALO
@@ -189,16 +231,16 @@
             field[far, rows:] = jnp.zeros(corner_shape, jnp.float32)
 
         for c in range(3):
-            ua[end, c, outer:outer + HALO, :rows] = jnp.where(present, halo[HALO * c:HALO * (c + 1)], 0.0)
+            ua[end, c, outer:outer + HALO, :rows] = jnp.where(present, halo(HALO * c, HALO), 0.0)
             put_corner(ua.at[end, c], c, True)
             nearest = HALO if end == 0 else planes - HALO - 2
             ua[end, c, nearest:nearest + 2] = u_edge[0, end, c]
             beyond = 1 if end == 0 else planes - HALO
-            f[end, c, beyond:beyond + count_f, :rows] = halo[at_f + count_f * c:at_f + count_f * (c + 1)]
+            f[end, c, beyond:beyond + count_f, :rows] = halo(at_f + count_f * c, count_f)
             put_corner(f.at[end, c], 3 + c, False)
             own_f = HALO if end == 0 else planes - 2 * HALO
             f[end, c, own_f:own_f + HALO] = f_edge[end, c]
-        m[end, outer:outer + HALO, :rows] = jnp.where(present, halo[at_m:], 0.0)
+        m[end, outer:outer + HALO, :rows] = jnp.where(present, halo(at_m, HALO), 0.0)
         put_corner(m.at[end], 6, True)
         m[end, inner:inner + HALO + 1] = m_edge[end]
         parts = (cx.at[end], cym.at[end], cyp.at[end], czm.at[end], czp.at[end])
@@ -226,12 +268,14 @@
         packet[half * (c + 1) - 2:half * (c + 1)] = ends[at + 2:at + 4]
 
 
-def middle_kernel(scale, place, p_in, ylo, yhi, xlo, xhi, u_out, packet,
+def middle_kernel(scale, p_in, y_first, y_second, x_first, x_second, u_out, packet,
                   ua, ub, f, m, cx, cym, cyp, czm, czp, weight, diag, pairs, pooled):
+    place = own_place()
     own, rows = p_in.shape[1:3]
     body = pl.ds(HALO, own)
     planes = own + 2 * HALO
     total_rows = m.shape[1]
+    even_x, even_y = is_even(place[0]), is_even(place[1])
     for c in range(4):
         if c < 3:
             field = f.at[c]
@@ -240,10 +284,10 @@
         if total_rows > rows + 2 * HALO:
             field[body] = jnp.zeros((own,) + m.shape[1:], jnp.float32)
         field[body, :rows] = p_in[c]
-        field[body, rows:rows + HALO] = yhi[c]
-        field[body, total_rows - HALO:] = ylo[c]
-        field[:HALO] = xlo[c]
-        field[HALO + own:] = xhi[c]
+        field[body, rows:rows + HALO] = jnp.where(even_y, y_first[c], y_second[c])
+        field[body, total_rows - HALO:] = jnp.where(even_y, y_second[c], y_first[c])
+        field[:HALO] = jnp.where(even_x, x_second[c], x_first[c])
+        field[HALO + own:] = jnp.where(even_x, x_first[c], x_second[c])
     shape = m.shape[1:]
     in_rows = inside_rows(place, rows, total_rows, shape)
     in_lower = inside_rows(place, rows, total_rows, shape, place[0] > 0)
@@ -278,7 +322,7 @@
         packet[...] = split_dot(pooled[...], pool)[:4]
 
 
-def last_kernel(place, g, u3_out, u4_out, r4_out, fw, mw, ua, ub, faces, weight, diag,
+def last_kernel(g, u3_out, u4_out, r4_out, fw, mw, ua, ub, faces, weight, diag,
                 f4, m4, faces4, weight4, diag4, va, vb, rows_out):
     count = g.shape[0]
     rows, lanes = g.shape[2:]
@@ -288,7 +332,7 @@
     x_one, y_one, z = lane // 64 == 1, lane // 32 % 2 == 1, lane % 32
     first_row, last_row = row == 0, row == rows - 1
     zero = jnp.zeros(shape, jnp.float32)
-    x_at, y_at = place[0], place[1]
+    x_at, y_at = lax.axis_index("gx"), lax.axis_index("gy")
     window = 2 * REACH + 1
     for w in range(window):
         i = y_at + (w - REACH)
@@ -400,28 +444,46 @@
     )
 
 
-def pack_kernel(viscosities, u_in, f_in, types, y_up, y_down, x_up, x_down, kinds, done):
+def pack_kernel(viscosities, u_in, f_in, types, y_first, y_second, x_first, x_second, kinds, done):
+    place = own_place()
     own, rows = types.shape[:2]
-    pairs = [(types, kinds)]
+    even_x, even_y = is_even(place[0]), is_even(place[1])
+    upper, upper_f, lower = own - HALO, own - HALO + 1, 0
+    at_first, at_second = jnp.where(even_x, upper, lower), jnp.where(even_x, lower, upper)
+    f_first, f_second = jnp.where(even_x, upper_f, lower), jnp.where(even_x, lower, upper_f)
+    always, if_even, if_odd = [(types, kinds)], [], []
     at = 3 * HALO
     for c in range(3):
         for k, field in ((0, u_in), (3, f_in)):
-            pairs.append((field.at[c, :, pl.ds(rows - HALO, HALO)], y_up.at[k + c]))
-            pairs.append((field.at[c, :, pl.ds(0, HALO)], y_down.at[k + c]))
-        pairs.append((u_in.at[c, pl.ds(own - HALO, HALO)], x_up.at[pl.ds(HALO * c, HALO)]))
-        pairs.append((u_in.at[c, pl.ds(0, HALO)], x_down.at[pl.ds(HALO * c, HALO)]))
-        pairs.append((f_in.at[c, pl.ds(own - HALO + 1, HALO - 1)], x_up.at[pl.ds(at, HALO - 1)]))
-        pairs.append((f_in.at[c, pl.ds(0, HALO - 1)], x_down.at[pl.ds(at, HALO - 1)]))
+            top, bottom = field.at[c, :, pl.ds(rows - HALO, HALO)], field.at[c, :, pl.ds(0, HALO)]
+            if_even += [(top, y_first.at[k + c]), (bottom, y_second.at[k + c])]
+            if_odd += [(bottom, y_first.at[k + c]), (top, y_second.at[k + c])]
+        here = pl.ds(HALO * c, HALO)
+        always.append((u_in.at[c, pl.ds(at_first, HALO)], x_first.at[here]))
+        always.append((u_in.at[c, pl.ds(at_second, HALO)], x_second.at[here]))
+        here = pl.ds(at, HALO - 1)
+        always.append((f_in.at[c, pl.ds(f_first, HALO - 1)], x_first.at[here]))
+        always.append((f_in.at[c, pl.ds(f_second, HALO - 1)], x_second.at[here]))
         at += HALO - 1
-    copies = [pltpu.make_async_copy(*pair, done.at[i]) for i, pair in enumerate(pairs)]
-    for copy in copies:
-        copy.start()
-    copies[0].wait()
-    y_up[6] = viscosity_of(kinds[:, rows - HALO:], viscosities)
-    y_down[6] = viscosity_of(kinds[:, :HALO], viscosities)
-    x_up[at:] = viscosity_of(kinds[own - HALO:], viscosities)
-    x_down[at:] = viscosity_of(kinds[:HALO], viscosities)
-    for copy in copies[1:]:
+
+    def copies(pairs, first):
+        return [pltpu.make_async_copy(*pair, done.at[first + i]) for i, pair in enumerate(pairs)]
+
+    def start(pairs, first):
+        for copy in copies(pairs, first):
+            copy.start()
+
+    start(always[:1], 0)
+    pl.when(even_y)(lambda: start(if_even, len(always)))
+    pl.when(jnp.logical_not(even_y))(lambda: start(if_odd, len(always)))
+    start(always[1:], 1)
+    copies(always[:1], 0)[0].wait()
+    top = viscosity_of(kinds[:, rows - HALO:], viscosities)
+    bottom = viscosity_of(kinds[:, :HALO], viscosities)
+    y_first[6], y_second[6] = jnp.where(even_y, top, bottom), jnp.where(even_y, bottom, top)
+    x_first[at:] = viscosity_of(kinds[pl.ds(at_first, HALO)], viscosities)
+    x_second[at:] = viscosity_of(kinds[pl.ds(at_second, HALO)], viscosities)
+    for copy in copies(always[1:], 1) + copies(if_even, len(always)):
         copy.wait()
 
 
@@ -435,13 +497,15 @@
     return at, 0
 
 
-def corner_kernel(ylo, yhi, up, down):
-    own = ylo.shape[1]
+def corner_kernel(y_first, y_second, first, second):
+    own = y_first.shape[1]
+    even = is_even(lax.axis_index("gx"))
     for channel in range(7):
         at, deep = corner_layers(channel)
-        for target, first in ((up, own - deep), (down, 0)):
-            target[at:at + deep, :HALO] = yhi[channel, first:first + deep]
-            target[at:at + deep, HALO:] = ylo[channel, first:first + deep]
+        for target, upper in ((first, even), (second, jnp.logical_not(even))):
+            planes = pl.ds(jnp.where(upper, own - deep, 0), deep)
+            target[at:at + deep, :HALO] = y_first[channel, planes]
+            target[at:at + deep, HALO:] = y_second[channel, planes]
 
 
 def on_chip(count):
@@ -464,12 +528,12 @@
 def on_device(velocity_guess, forcing, cell_type, viscosities):
     f32 = jnp.float32
     count_x, count_y = lax.axis_size("gx"), lax.axis_size("gy")
-    place = jnp.stack([lax.axis_index("gx"), lax.axis_index("gy"), count_x, count_y]).astype(jnp.int32)
+    even_x, even_y = is_even(lax.axis_index("gx")), is_even(lax.axis_index("gy"))
     in_smem = [pl.BlockSpec(memory_space=pltpu.SMEM)]
     own, rows, lanes = cell_type.shape
     y_edge = jax.ShapeDtypeStruct((7, own, HALO, lanes), f32)
     x_edge = jax.ShapeDtypeStruct((7 * HALO - 3, rows, lanes), f32)
-    y_up, y_down, x_up, x_down = pl.pallas_call(
+    y_out, y_out_odd, x_out, x_out_odd = pl.pallas_call(
         pack_kernel,
         out_shape=(y_edge, y_edge, x_edge, x_edge),
         in_specs=in_smem + [pl.BlockSpec(memory_space=pl.ANY)] * 3,
@@ -477,20 +541,17 @@
         scratch_shapes=[pltpu.VMEM(cell_type.shape, jnp.int32), pltpu.SemaphoreType.DMA((25,))],
         compiler_params=pltpu.CompilerParams(vmem_limit_bytes=PACK_LIMIT),
     )(viscosities, velocity_guess, forcing, cell_type)
-    ylo = passed_round(y_up, "gy", 1)
-    yhi = passed_round(y_down, "gy", -1)
-    xlo = passed_round(x_up, "gx", 1)
-    xhi = passed_round(x_down, "gx", -1)
+    y_halo = swapped(y_out, y_out_odd, "gy")
+    x_halo = swapped(x_out, x_out_odd, "gx")
     corner = jax.ShapeDtypeStruct((corner_layers(7)[0], 2 * HALO, lanes), f32)
-    up, down = pl.pallas_call(
+    corners = pl.pallas_call(
         corner_kernel,
         out_shape=(corner, corner),
         in_specs=on_chip(2),
         out_specs=tuple(on_chip(2)),
         compiler_params=LIMIT,
-    )(ylo, yhi)
-    clo = passed_round(up, "gx", 1)
-    chi = passed_round(down, "gx", -1)
+    )(*y_halo)
+    corner_halo = swapped(*corners, "gx")
     tall = rows + 2 * HALO
     middle = own // 2 - HALO
     state = (
@@ -503,38 +564,40 @@
     known = pl.pallas_call(
         inner_kernel,
         out_shape=tuple(jax.ShapeDtypeStruct(shape, f32) for shape in state),
-        in_specs=in_smem * 2 + on_chip(5),
+        in_specs=in_smem + on_chip(5),
         out_specs=tuple(on_chip(5)),
         scratch_shapes=planes_scratch(own + 2 * HALO, tall, lanes, middle, rows, (4 * middle, rows, 128)),
         compiler_params=LIMIT,
         cost_estimate=pl.CostEstimate(flops=60_000_000, bytes_accessed=6_000_000, transcendentals=0),
-    )(place, viscosities, velocity_guess, forcing, cell_type, ylo, yhi)
+    )(viscosities, velocity_guess, forcing, cell_type, *y_halo)
     u0, packet = pl.pallas_call(
         outer_kernel,
         out_shape=(
             jax.ShapeDtypeStruct(velocity_guess.shape, f32),
             jax.ShapeDtypeStruct((4 * own // 2, rows // 2, lanes // 2), f32),
         ),
-        in_specs=in_smem + on_chip(9),
+        in_specs=on_chip(9),
         out_specs=tuple(on_chip(2)),
         scratch_shapes=planes_scratch(2 * HALO + 1, tall, lanes, HALO, rows, (4 * HALO, rows, 128), (2,)),
         compiler_params=LIMIT,
-    )(place, *known, xlo, xhi, clo, chi)
+    )(*known, *x_halo, *corner_halo)
     results = [u0]
     for grid_level in (1, 2):
         own, rows = own // 2, rows // 2
         packet = packet.reshape(4, own, rows, 128)
         valid = 256 >> grid_level
-        ylo = passed_round(packet[:, :, rows - HALO:], "gy", 1)
-        yhi = passed_round(packet[:, :, :HALO], "gy", -1)
-        parts = [packet, yhi, ylo]
+        top, bottom = packet[:, :, rows - HALO:], packet[:, :, :HALO]
+        y_halo = swapped(jnp.where(even_y, top, bottom), jnp.where(even_y, bottom, top), "gy")
+        upper, lower = jnp.where(even_y, y_halo[0], y_halo[1]), jnp.where(even_y, y_halo[1], y_halo[0])
+        parts = [packet, upper, lower]
         total_rows = rows + 2 * HALO
         if total_rows % 8:
-            parts = [packet, yhi, jnp.zeros_like(yhi), ylo]
+            parts = [packet, upper, jnp.zeros_like(upper), lower]
             total_rows += HALO
-        tall = jnp.concatenate(parts, axis=2)
-        xlo = passed_round(tall[:, own - HALO:], "gx", 1)
-        xhi = passed_round(tall[:, :HALO], "gx", -1)
+        top, bottom = (
+            jnp.concatenate([part[:, at:at + HALO] for part in parts], axis=2) for at in (own - HALO, 0)
+        )
+        x_halo = swapped(jnp.where(even_x, top, bottom), jnp.where(even_x, bottom, top), "gx")
         if grid_level == 1:
             packet_shape, pooled_shape = (4 * own // 2, rows // 2, 128), (4 * own // 2, rows, 128)
         else:
@@ -545,11 +608,11 @@
                 jax.ShapeDtypeStruct((3, own, rows, valid), f32),
                 jax.ShapeDtypeStruct(packet_shape, f32),
             ),
-            in_specs=in_smem + on_chip(5),
+            in_specs=on_chip(5),
             out_specs=tuple(on_chip(2)),
             scratch_shapes=planes_scratch(own + 2 * HALO, total_rows, 128, own // 2, rows, pooled_shape),
             compiler_params=LIMIT,
-        )(place, packet, ylo, yhi, xlo, xhi)
+        )(packet, *y_halo, *x_halo)
         results.append(u_own)
     column = lax.all_to_all(jnp.broadcast_to(packet[None], (count_x, 4, 128)), "gx", 0, 0)
     column = column.transpose(1, 0, 2)
@@ -561,12 +624,12 @@
     last = pl.pallas_call(
         last_kernel,
         out_shape=tuple(jax.ShapeDtypeStruct(shape, f32) for shape in ((3, 2, 2, 32), (3, 1, 1, 16), (3, 1, 1, 16))),
-        in_specs=in_smem + on_chip(1),
+        in_specs=on_chip(1),
         out_specs=tuple(on_chip(3)),
         scratch_shapes=[vector, field, vector, vector, six, field, field,
                         vector, field, six, field, field, vector, vector, pltpu.VMEM((8, 128), f32)],
         compiler_params=LIMIT,
-    )(place, gathered)
+    )(gathered)
     return (*results, *last)
 
 

time: 102 us -> 96.7 us (0.948)
  starting transfers between devices: 23.2 us -> 14.2 us
  blocking collectives: 36.3 us -> 40.4 us
  Pallas kernels: 22 us -> 20.3 us
    ppermute x14, starting transfers between devices: 23.2 us -> 14.2 us  [pair_swap(): return lax.ppermute(value, ('gx', 'gy'), route)]
    all_to_all x1, blocking collectives: 18.3 us -> 22.4 us  [on_device(): lax.all_to_all(jnp.broadcast_to(column[None], (count_y, 4, count_x, 128))...]
    pallas_call x2, Pallas kernels: 3.34 us -> 2.24 us  [on_device(): pl.pallas_call(functools.partial(middle_kernel, 0.25 ** grid_level), out_...]
  transfers between devices with their start and end apart: 14 -> 14, of which waited for: 5 -> 6; matrix products, arithmetic and copies ran while one was open for 0% -> 0% of each run, Pallas kernels for 5% -> 5%
where the time goes in v4:
time: 96.7 us; the launch traced here: 95.7 us
  blocking collectives  40.4 us (42%)
  Pallas kernels  20.3 us (21%)
  waiting for transfers between devices  19.7 us (20%)
  starting transfers between devices  14.2 us (15%)
    all_to_all x1, blocking collectives, on_device(): lax.all_to_all(jnp.broadcast_to(column[None], (count_y, 4, count_x, 128))...  22.4 us
    ppermute x14, waiting for transfers between devices, pair_swap(): return lax.ppermute(value, ('gx', 'gy'), route)  19.7 us
    all_to_all x1, blocking collectives, on_device(): lax.all_to_all(jnp.broadcast_to(packet[None], (count_x, 4, 128)), 'gx', 0...  18 us
    ppermute x14, starting transfers between devices, pair_swap(): return lax.ppermute(value, ('gx', 'gy'), route)  14.2 us
    pallas_call x1, Pallas kernels, on_device(): pl.pallas_call(last_kernel, out_shape=tuple((jax.ShapeDtypeStruct(shape,...  4.93 us
    pallas_call x1, Pallas kernels, on_device(): pl.pallas_call(outer_kernel, out_shape=(jax.ShapeDtypeStruct(velocity_gue...  4.52 us
    pallas_call x1, Pallas kernels, on_device(): pl.pallas_call(inner_kernel, out_shape=tuple((jax.ShapeDtypeStruct(shape,...  4.28 us
    pallas_call x1, Pallas kernels, on_device(): pl.pallas_call(pack_kernel, out_shape=(y_edge, y_edge, x_edge, x_edge), i...  3.63 us
  transfers between devices with their start and end apart: 14, of which 6 were waited for; matrix products, arithmetic and copies ran while one was open for 0% of the time, Pallas kernels for 5%

profile of v4, /device:TPU:32, one launch (start us, length us, event | category | flops | bytes accessed | tf_op | source)
XLA Modules:
  0.0 95.7 jit_solution(14877472523711048453)
XLA Ops:
  0.7 3.6 %shard_map.91 = (f32[7,16,4,256]{3,2,1,0:T(4,128)}, f32[7,16,4,256]{3,2,1,0:T(4,128)}, f32[25,16,256]{2,1,0:T(8,128)}, f32[25,16,256]{2,1,0:T(8,128)}) custom-call(f32[4]{0:T(128)} %viscosities.3, f32[3,16,16,256]{3,2,1,0:T(8,128)} %u_in.3, f32[3,16,16,256]{3,2,1,0:T(8,128)} %f_in.3, s32[16,16,256]{2,1,0:T(8,128)} %types.3), custom_call_target="tpu_custom_call" | custom-call | tf_op jit(solution)/shard_map/pallas_call | solution.py:536
  4.3 1.7 %collective-permute-start = (f32[7,16,4,256]{3,2,1,0:T(4,128)}, f32[7,16,4,256]{3,2,1,0:T(4,128)S(1)}, u32[]{:S(2)}, u32[]{:S(2)}) collective-permute-start(f32[7,16,4,256]{3,2,1,0:T(4,128)} %get-tuple-element.26), channel_id=1, source_target_pairs={{0,1},{1,0},{2,3},{3,2},{4,5},{5,4},{6,7},{7,6},{8,9},{9,8},{10,11... | collective-permute-start | bytes 1376264 | tf_op jit(solution)/shard_map/ppermute | solution.py:32
  6.0 0.5 collective-permute-start.2
  6.5 0.1 collective-permute-start.3
  6.6 10.3 %collective-permute-done.y_first = f32[7,16,4,256]{3,2,1,0:T(4,128)S(1)} collective-permute-done((f32[7,16,4,256]{3,2,1,0:T(4,128)}, f32[7,16,4,256]{3,2,1,0:T(4,128)S(1)}, u32[]{:S(2)}, u32[]{:S(2)}) %collective-permute-start) | collective-permute-done | bytes 458784 | tf_op jit(solution)/shard_map/ppermute | solution.py:32
  16.9 0.7 shard_map.93
  17.6 0.0 collective-permute-start.4
  17.6 0.1 collective-permute-start.5
  17.7 4.3 %shard_map.92 = (f32[3,10,16,256]{3,2,1,0:T(8,128)S(1)}, f32[16,8,128]{2,1,0:T(8,128)S(1)}, f32[4,2,3,2,24,256]{5,4,3,2,1,0:T(8,128)S(1)}, f32[2,3,4,24,256]{4,3,2,1,0:T(8,128)S(1)}, f32[2,5,24,256]{3,2,1,0:T(8,128)S(1)}) custom-call(f32[4]{0:T(128)S(1)} %copy-done.3, f32[3,16,16,256]{3,2,1,0:T(8,128)S(1)} %copy-done, f32[3,16,16,256]{3,2,1,0:T(8,128)S(1)} %copy-done.1, ...), custom_call_target="tpu_custom_call" | custom-call | flops 60000000 | bytes 6000000 | tf_op jit(solution)/shard_map/pallas_call | solution.py:564
  22.0 0.0 collective-permute-done.2.x_first
  22.0 0.0 collective-permute-done.4.corner_first
  22.0 0.5 collective-permute-done.5.corner_second
  22.5 4.5 %shard_map.94 = (f32[3,16,16,256]{3,2,1,0:T(8,128)}, f32[32,8,128]{2,1,0:T(8,128)S(1)}) custom-call(f32[3,10,16,256]{3,2,1,0:T(8,128)S(1)} %get-tuple-element.28.u_mid, f32[16,8,128]{2,1,0:T(8,128)S(1)} %get-tuple-element.29.packet_mid, f32[4,2,3,2,24,256]{5,4,3,2,1,0:T(8,128)S(1)} %get-tuple-element.30.u_edge, ...), custom_call_target="tpu_custom_call" | custom-call | tf_op jit(solution)/shard_map/pallas_call | solution.py:573
  27.0 2.5 %collective-permute-start.6 = (f32[4,8,4,128]{3,2,1,0:T(4,128)S(1)}, f32[4,8,4,128]{3,2,1,0:T(4,128)S(1)}, u32[]{:S(2)}, u32[]{:S(2)}) collective-permute-start(f32[4,8,4,128]{3,2,1,0:T(4,128)S(1)} %get-tuple-element.53), channel_id=1, source_target_pairs={{0,1},{1,0},{2,3},{3,2},{4,5},{5,4},{6,7},{7,6},{8,9},{9,8},{10,11... | collective-permute-start | bytes 196616 | tf_op jit(solution)/shard_map/ppermute | solution.py:32
  29.5 1.2 %collective-permute-start.7 = (f32[4,8,4,128]{3,2,1,0:T(4,128)S(1)}, f32[4,8,4,128]{3,2,1,0:T(4,128)S(1)}, u32[]{:S(2)}, u32[]{:S(2)}) collective-permute-start(f32[4,8,4,128]{3,2,1,0:T(4,128)S(1)} %get-tuple-element.52), channel_id=1, source_target_pairs={{0,16},{1,2},{2,1},{3,4},{4,3},{5,6},{6,5},{7,8},{8,7},{9,10},{10,... | collective-permute-start | bytes 196616 | tf_op jit(solution)/shard_map/ppermute | solution.py:32
  30.8 1.0 %collective-permute-done.6.y_first = f32[4,8,4,128]{3,2,1,0:T(4,128)S(1)} collective-permute-done((f32[4,8,4,128]{3,2,1,0:T(4,128)S(1)}, f32[4,8,4,128]{3,2,1,0:T(4,128)S(1)}, u32[]{:S(2)}, u32[]{:S(2)}) %collective-permute-start.6) | collective-permute-done | bytes 65568 | tf_op jit(solution)/shard_map/ppermute | solution.py:32
  31.9 0.7 collective-permute-start.8
  32.6 1.1 %collective-permute-start.9 = (f32[4,4,16,128]{3,2,1,0:T(8,128)S(1)}, f32[4,4,16,128]{3,2,1,0:T(8,128)S(1)}, u32[]{:S(2)}, u32[]{:S(2)}) collective-permute-start(f32[4,4,16,128]{3,2,1,0:T(8,128)S(1)} %get-tuple-element.46), channel_id=1, source_target_pairs={{0,1},{1,0},{2,3},{3,2},{4,5},{5,4},{6,7},{7,6},{8,9},{9,8},{10,11... | collective-permute-start | bytes 393224 | tf_op jit(solution)/shard_map/ppermute | solution.py:32
  33.7 3.3 %collective-permute-done.9.x_second = f32[4,4,16,128]{3,2,1,0:T(8,128)S(1)} collective-permute-done((f32[4,4,16,128]{3,2,1,0:T(8,128)S(1)}, f32[4,4,16,128]{3,2,1,0:T(8,128)S(1)}, u32[]{:S(2)}, u32[]{:S(2)}) %collective-permute-start.9) | collective-permute-done | bytes 131104 | tf_op jit(solution)/shard_map/ppermute | solution.py:32
  37.0 1.2 %shard_map.95 = (f32[3,8,8,128]{3,2,1,0:T(8,128)}, f32[16,4,128]{2,1,0:T(4,128)S(1)}) custom-call(f32[4,8,8,128]{3,2,1,0:T(8,128)S(1)} %bitcast.13, f32[4,8,4,128]{3,2,1,0:T(4,128)S(1)} %collective-permute-done.6.y_first, f32[4,8,4,128]{3,2,1,0:T(4,128)S(1)} %collective-permute-done.7.y_second, f32[4,4,16,128]{3,2,1,0:T(8,128)S(1)} %collective-permute-done.8.x_first, ...), custom_call_target="tpu_custom_call" | custom-call | tf_op jit(solution)/shard_map/pallas_call | solution.py:605
  38.1 4.5 %collective-permute-start.10 = (f32[4,4,4,128]{3,2,1,0:T(4,128)S(1)}, f32[4,4,4,128]{3,2,1,0:T(4,128)S(1)}, u32[]{:S(2)}, u32[]{:S(2)}) collective-permute-start(f32[4,4,4,128]{3,2,1,0:T(4,128)S(1)} %bitcast.16), channel_id=1, source_target_pairs={{0,1},{1,0},{2,3},{3,2},{4,5},{5,4},{6,7},{7,6},{8,9},{9,8},{10,11... | collective-permute-start | bytes 98312 | tf_op jit(solution)/shard_map/ppermute | solution.py:32
  42.6 0.0 collective-permute-start.11
  42.7 0.1 pad.2.clone
  42.7 1.8 %collective-permute-done.10.y_first = f32[4,4,4,128]{3,2,1,0:T(4,128)S(1)} collective-permute-done((f32[4,4,4,128]{3,2,1,0:T(4,128)S(1)}, f32[4,4,4,128]{3,2,1,0:T(4,128)S(1)}, u32[]{:S(2)}, u32[]{:S(2)}) %collective-permute-start.10) | collective-permute-done | bytes 32800 | tf_op jit(solution)/shard_map/ppermute | solution.py:32
  44.6 0.1 pad_maximum_fusion.2
  44.6 0.1 collective-permute-start.12
  44.7 1.8 %collective-permute-start.13 = (f32[4,4,16,128]{3,2,1,0:T(8,128)S(1)}, f32[4,4,16,128]{3,2,1,0:T(8,128)S(1)}, u32[]{:S(2)}, u32[]{:S(2)}) collective-permute-start(f32[4,4,16,128]{3,2,1,0:T(8,128)S(1)} %pad_maximum_fusion.2), channel_id=1, source_target_pairs={{0,1},{1,0},{2,3},{3,2},{4,5},{5,4},{6,7},{7,6},{8,9},{9,8},{10,11... | collective-permute-start | bytes 393224 | tf_op jit(solution)/shard_map/ppermute | solution.py:32
  46.5 2.7 %collective-permute-done.13.x_second = f32[4,4,16,128]{3,2,1,0:T(8,128)S(1)} collective-permute-done((f32[4,4,16,128]{3,2,1,0:T(8,128)S(1)}, f32[4,4,16,128]{3,2,1,0:T(8,128)S(1)}, u32[]{:S(2)}, u32[]{:S(2)}) %collective-permute-start.13) | collective-permute-done | bytes 131104 | tf_op jit(solution)/shard_map/ppermute | solution.py:32
  49.2 1.1 %shard_map.96 = (f32[3,4,4,64]{3,2,1,0:T(4,128)}, f32[4,128]{1,0:T(4,128)S(1)}) custom-call(f32[4,4,4,128]{3,2,1,0:T(4,128)S(1)} %bitcast.19, f32[4,4,4,128]{3,2,1,0:T(4,128)S(1)} %collective-permute-done.10.y_first, f32[4,4,4,128]{3,2,1,0:T(4,128)S(1)} %collective-permute-done.11.y_second, f32[4,4,16,128]{3,2,1,0:T(8,128)S(1)} %collective-permute-done.12.x_first, ...), custom_call_target="tpu_custom_call" | custom-call | tf_op jit(solution)/shard_map/pallas_call | solution.py:605
  50.3 18.0 %all_to_all.10 = f32[16,4,128]{2,1,0:T(4,128)S(1)} all-to-all(f32[16,4,128]{2,1,0:T(4,128)S(1)} %broadcast_in_dim.7), channel_id=1, replica_groups=mesh['gx'=16,'gy'=16] {'gx'}, dimensions={0} | all-to-all | bytes 65536 | tf_op jit(solution)/shard_map/all_to_all | solution.py:617
  68.4 22.4 %all_to_all.11.g = f32[16,4,16,128]{3,2,1,0:T(8,128)S(1)} all-to-all(f32[16,4,16,128]{3,2,1,0:T(8,128)S(1)} %broadcast_in_dim.8), channel_id=1, replica_groups=mesh['gx'=16,'gy'=16] {'gy'}, dimensions={0} | all-to-all | bytes 1048576 | tf_op jit(solution)/shard_map/all_to_all | solution.py:619
  90.7 4.9 %shard_map.97 = (f32[3,2,2,32]{3,2,1,0:T(2,128)}, f32[3,1,1,16]{3,2,1,0:T(1,128)}, f32[3,1,1,16]{3,2,1,0:T(1,128)}) custom-call(f32[16,4,16,128]{3,2,1,0:T(8,128)S(1)} %all_to_all.11.g), custom_call_target="tpu_custom_call" | custom-call | tf_op jit(solution)/shard_map/pallas_call | solution.py:624
  (25 shorter events, 0.2 us)
Async XLA Ops:
  0.6 17.0 %copy-start = (f32[3,16,16,256]{3,2,1,0:T(8,128)S(1)}, f32[3,16,16,256]{3,2,1,0:T(8,128)}, u32[]{:S(2)}) copy-start(f32[3,16,16,256]{3,2,1,0:T(8,128)} %u_in.3) | copy-start | bytes 2359300
  0.6 17.0 %copy-start.1 = (f32[3,16,16,256]{3,2,1,0:T(8,128)S(1)}, f32[3,16,16,256]{3,2,1,0:T(8,128)}, u32[]{:S(2)}) copy-start(f32[3,16,16,256]{3,2,1,0:T(8,128)} %f_in.3) | copy-start | bytes 2359300
  0.7 17.0 %copy-start.2 = (s32[16,16,256]{2,1,0:T(8,128)S(1)}, s32[16,16,256]{2,1,0:T(8,128)}, u32[]{:S(2)}) copy-start(s32[16,16,256]{2,1,0:T(8,128)} %types.3) | copy-start | bytes 786436
  0.7 17.0 %copy-start.3 = (f32[4]{0:T(128)S(1)}, f32[4]{0:T(128)}, u32[]{:S(2)}) copy-start(f32[4]{0:T(128)} %viscosities.3) | copy-start | bytes 52
  4.3 12.6 %collective-permute-start = (f32[7,16,4,256]{3,2,1,0:T(4,128)}, f32[7,16,4,256]{3,2,1,0:T(4,128)S(1)}, u32[]{:S(2)}, u32[]{:S(2)}) collective-permute-start(f32[7,16,4,256]{3,2,1,0:T(4,128)} %get-tuple-element.26), channel_id=1, source_target_pairs={{0,1},{1,0},{2,3},{3,2},{4,5},{5,4},{6,7},{7,6},{8,9},{9,8},{10,11... | collective-permute-start | bytes 1376264 | tf_op jit(solution)/shard_map/ppermute | solution.py:32
  6.0 10.9 %collective-permute-start.1 = (f32[7,16,4,256]{3,2,1,0:T(4,128)}, f32[7,16,4,256]{3,2,1,0:T(4,128)S(1)}, u32[]{:S(2)}, u32[]{:S(2)}) collective-permute-start(f32[7,16,4,256]{3,2,1,0:T(4,128)} %get-tuple-element.27), channel_id=1, source_target_pairs={{0,16},{1,2},{2,1},{3,4},{4,3},{5,6},{6,5},{7,8},{8,7},{9,10},{10,... | collective-permute-start | bytes 1376264 | tf_op jit(solution)/shard_map/ppermute | solution.py:32
  6.0 16.0 %collective-permute-start.2 = (f32[25,16,256]{2,1,0:T(8,128)}, f32[25,16,256]{2,1,0:T(8,128)}, u32[]{:S(2)}, u32[]{:S(2)}) collective-permute-start(f32[25,16,256]{2,1,0:T(8,128)} %get-tuple-element.33), channel_id=1, source_target_pairs={{0,16},{1,17},{2,18},{3,19},{4,20},{5,21},{6,22},{7,23},{8,24},{9,... | collective-permute-start | bytes 1228808 | tf_op jit(solution)/shard_map/ppermute | solution.py:32
  6.5 15.5 %collective-permute-start.3 = (f32[25,16,256]{2,1,0:T(8,128)}, f32[25,16,256]{2,1,0:T(8,128)}, u32[]{:S(2)}, u32[]{:S(2)}) collective-permute-start(f32[25,16,256]{2,1,0:T(8,128)} %get-tuple-element.34), channel_id=1, source_target_pairs={{0,1},{1,0},{2,3},{3,2},{4,5},{5,4},{6,7},{7,6},{8,9},{9,8},{10,11... | collective-permute-start | bytes 1228808 | tf_op jit(solution)/shard_map/ppermute | solution.py:32
  17.6 4.4 %collective-permute-start.4 = (f32[18,8,256]{2,1,0:T(8,128)}, f32[18,8,256]{2,1,0:T(8,128)S(1)}, u32[]{:S(2)}, u32[]{:S(2)}) collective-permute-start(f32[18,8,256]{2,1,0:T(8,128)} %get-tuple-element.35), channel_id=1, source_target_pairs={{0,16},{1,17},{2,18},{3,19},{4,20},{5,21},{6,22},{7,23},{8,24},{9,... | collective-permute-start | bytes 442376 | tf_op jit(solution)/shard_map/ppermute | solution.py:32
  17.6 4.9 %collective-permute-start.5 = (f32[18,8,256]{2,1,0:T(8,128)}, f32[18,8,256]{2,1,0:T(8,128)}, u32[]{:S(2)}, u32[]{:S(2)}) collective-permute-start(f32[18,8,256]{2,1,0:T(8,128)} %get-tuple-element.36), channel_id=1, source_target_pairs={{0,1},{1,0},{2,3},{3,2},{4,5},{5,4},{6,7},{7,6},{8,9},{9,8},{10,11... | collective-permute-start | bytes 442376 | tf_op jit(solution)/shard_map/ppermute | solution.py:32
  27.0 4.7 %collective-permute-start.6 = (f32[4,8,4,128]{3,2,1,0:T(4,128)S(1)}, f32[4,8,4,128]{3,2,1,0:T(4,128)S(1)}, u32[]{:S(2)}, u32[]{:S(2)}) collective-permute-start(f32[4,8,4,128]{3,2,1,0:T(4,128)S(1)} %get-tuple-element.53), channel_id=1, source_target_pairs={{0,1},{1,0},{2,3},{3,2},{4,5},{5,4},{6,7},{7,6},{8,9},{9,8},{10,11... | collective-permute-start | bytes 196616 | tf_op jit(solution)/shard_map/ppermute | solution.py:32
  29.5 2.2 %collective-permute-start.7 = (f32[4,8,4,128]{3,2,1,0:T(4,128)S(1)}, f32[4,8,4,128]{3,2,1,0:T(4,128)S(1)}, u32[]{:S(2)}, u32[]{:S(2)}) collective-permute-start(f32[4,8,4,128]{3,2,1,0:T(4,128)S(1)} %get-tuple-element.52), channel_id=1, source_target_pairs={{0,16},{1,2},{2,1},{3,4},{4,3},{5,6},{6,5},{7,8},{8,7},{9,10},{10,... | collective-permute-start | bytes 196616 | tf_op jit(solution)/shard_map/ppermute | solution.py:32
  31.9 1.8 %collective-permute-start.8 = (f32[4,4,16,128]{3,2,1,0:T(8,128)S(1)}, f32[4,4,16,128]{3,2,1,0:T(8,128)S(1)}, u32[]{:S(2)}, u32[]{:S(2)}) collective-permute-start(f32[4,4,16,128]{3,2,1,0:T(8,128)S(1)} %get-tuple-element.47), channel_id=1, source_target_pairs={{0,16},{1,17},{2,18},{3,19},{4,20},{5,21},{6,22},{7,23},{8,24},{9,... | collective-permute-start | bytes 393224 | tf_op jit(solution)/shard_map/ppermute | solution.py:32
  32.6 4.4 %collective-permute-start.9 = (f32[4,4,16,128]{3,2,1,0:T(8,128)S(1)}, f32[4,4,16,128]{3,2,1,0:T(8,128)S(1)}, u32[]{:S(2)}, u32[]{:S(2)}) collective-permute-start(f32[4,4,16,128]{3,2,1,0:T(8,128)S(1)} %get-tuple-element.46), channel_id=1, source_target_pairs={{0,1},{1,0},{2,3},{3,2},{4,5},{5,4},{6,7},{7,6},{8,9},{9,8},{10,11... | collective-permute-start | bytes 393224 | tf_op jit(solution)/shard_map/ppermute | solution.py:32
  38.1 6.4 %collective-permute-start.10 = (f32[4,4,4,128]{3,2,1,0:T(4,128)S(1)}, f32[4,4,4,128]{3,2,1,0:T(4,128)S(1)}, u32[]{:S(2)}, u32[]{:S(2)}) collective-permute-start(f32[4,4,4,128]{3,2,1,0:T(4,128)S(1)} %bitcast.16), channel_id=1, source_target_pairs={{0,1},{1,0},{2,3},{3,2},{4,5},{5,4},{6,7},{7,6},{8,9},{9,8},{10,11... | collective-permute-start | bytes 98312 | tf_op jit(solution)/shard_map/ppermute | solution.py:32
  42.6 1.9 %collective-permute-start.11 = (f32[4,4,4,128]{3,2,1,0:T(4,128)S(1)}, f32[4,4,4,128]{3,2,1,0:T(4,128)S(1)}, u32[]{:S(2)}, u32[]{:S(2)}) collective-permute-start(f32[4,4,4,128]{3,2,1,0:T(4,128)S(1)} %bitcast.17), channel_id=1, source_target_pairs={{0,16},{1,2},{2,1},{3,4},{4,3},{5,6},{6,5},{7,8},{8,7},{9,10},{10,... | collective-permute-start | bytes 98312 | tf_op jit(solution)/shard_map/ppermute | solution.py:32
  44.6 1.9 %collective-permute-start.12 = (f32[4,4,16,128]{3,2,1,0:T(8,128)S(1)}, f32[4,4,16,128]{3,2,1,0:T(8,128)S(1)}, u32[]{:S(2)}, u32[]{:S(2)}) collective-permute-start(f32[4,4,16,128]{3,2,1,0:T(8,128)S(1)} %pad_maximum_fusion.2), channel_id=1, source_target_pairs={{0,16},{1,17},{2,18},{3,19},{4,20},{5,21},{6,22},{7,23},{8,24},{9,... | collective-permute-start | bytes 393224 | tf_op jit(solution)/shard_map/ppermute | solution.py:32
  44.7 4.5 %collective-permute-start.13 = (f32[4,4,16,128]{3,2,1,0:T(8,128)S(1)}, f32[4,4,16,128]{3,2,1,0:T(8,128)S(1)}, u32[]{:S(2)}, u32[]{:S(2)}) collective-permute-start(f32[4,4,16,128]{3,2,1,0:T(8,128)S(1)} %pad_maximum_fusion.2), channel_id=1, source_target_pairs={{0,1},{1,0},{2,3},{3,2},{4,5},{5,4},{6,7},{7,6},{8,9},{9,8},{10,11... | collective-permute-start | bytes 393224 | tf_op jit(solution)/shard_map/ppermute | solution.py:32

commit v5 on v4

--- a/solution.py
+++ b/solution.py
@@ -322,55 +322,68 @@
         packet[...] = split_dot(pooled[...], pool)[:4]
 
 
+def window_kernel(column, out, rows_of):
+    count = column.shape[0]
+    width = rows_of.shape[0] // 4
+    x_at = lax.axis_index("gx")
+    for r in range(width):
+        i = x_at + (r - REACH)
+        value = jnp.where((i >= 0) & (i < count), column[jnp.clip(i, 0, count - 1)], 0.0)
+        for c in range(4):
+            rows_of[width * c + r:width * c + r + 1] = value[c:c + 1]
+    out[...] = jnp.broadcast_to(rows_of[...][None], out.shape)
+
+
 def last_kernel(g, u3_out, u4_out, r4_out, fw, mw, ua, ub, faces, weight, diag,
                 f4, m4, faces4, weight4, diag4, va, vb, rows_out):
-    count = g.shape[0]
-    rows, lanes = g.shape[2:]
+    count, width = g.shape[0], g.shape[1] // 4
+    rows, lanes = mw.shape[1:]
     shape = (rows, lanes)
     lane = lax.broadcasted_iota(jnp.int32, shape, 1)
-    row = lax.broadcasted_iota(jnp.int32, shape, 0)
     x_one, y_one, z = lane // 64 == 1, lane // 32 % 2 == 1, lane % 32
-    first_row, last_row = row == 0, row == rows - 1
     zero = jnp.zeros(shape, jnp.float32)
-    x_at, y_at = lax.axis_index("gx"), lax.axis_index("gy")
+    y_at = lax.axis_index("gy")
     window = 2 * REACH + 1
     for w in range(window):
         i = y_at + (w - REACH)
         inside = (i >= 0) & (i < count)
         i = jnp.clip(i, 0, count - 1)
-        for c in range(3):
-            fw[c, w] = jnp.where(inside, g[i, c], 0.0)
-        mw[w] = jnp.where(inside, g[i, 3], 0.0)
+        for c in range(4):
+            place = fw.at[c, w] if c < 3 else mw.at[w]
+            place[:width] = jnp.where(inside, g[i, width * c:width * (c + 1)], 0.0)
+            place[width:] = zero[width:]
 
     def shifted_rows(value):
         return pltpu.roll(value, 1, 0), pltpu.roll(value, rows - 1, 0)
 
-    def near3(get, w):
+    def near3(get, w, turned):
+        for j in (w - 1, w, w + 1):
+            if j not in turned:
+                inside = 0 <= j < window
+                turned[j] = (pltpu.roll(get(j), 32, 1), pltpu.roll(get(j), lanes - 32, 1)) if inside else (zero, zero)
         centre = get(w)
         other = pltpu.roll(centre, 64, 1)
         lower, upper = shifted_rows(other)
         x_out = jnp.where(x_one, upper, lower)
-        y_in = jnp.where(y_one, pltpu.roll(centre, 32, 1), pltpu.roll(centre, lanes - 32, 1))
-        below = pltpu.roll(get(w - 1), lanes - 32, 1) if w > 0 else zero
-        above = pltpu.roll(get(w + 1), 32, 1) if w < window - 1 else zero
-        y_out = jnp.where(y_one, above, below)
+        y_in = jnp.where(y_one, turned[w][0], turned[w][1])
+        y_out = jnp.where(y_one, turned[w + 1][0], turned[w - 1][1])
         return centre, (other, x_out, y_in, y_out, pltpu.roll(centre, 1, 1), pltpu.roll(centre, lanes - 1, 1))
 
-    x_edge = (x_one & last_row) | (jnp.logical_not(x_one) & first_row)
-    outside3 = (None, x_edge, None, None, z == 0, z == 31)
-
-    def near4(get, w):
+    outside3 = (None, None, None, None, z == 0, z == 31)
+
+    def near4(get, w, turned):
         centre = get(w)
         lower, upper = shifted_rows(centre)
         return centre, (lower, upper, get(w - 1), get(w + 1),
                         pltpu.roll(centre, 2, 1), pltpu.roll(centre, lanes - 2, 1))
 
-    outside4 = (first_row, last_row, None, None, z < 2, z >= 30)
+    outside4 = (None, None, None, None, z < 2, z >= 30)
 
     def level(scale, near, outside, f, m, faces, weight, diag, ua, ub, spans, residual):
         half = 0.5 * scale
+        turned = {}
         for w in spans[0]:
-            centre, sides = near(lambda j: m[j], w)
+            centre, sides = near(lambda j: m[j], w, turned)
             total = jnp.full(shape, mass_term, jnp.float32)
             for k in range(6):
                 side = sides[k] if outside[k] is None else jnp.where(outside[k], 0.0, sides[k])
@@ -382,21 +395,23 @@
             for c in range(3):
                 ua[c, w] = weight[w] * f[c, w]
 
-        def flux_at(u, c, w):
-            centre, sides = near(lambda j: u[c, j], w)
+        def flux_at(u, c, w, turned):
+            centre, sides = near(lambda j: u[c, j], w, turned)
             flux = faces[0, w] * sides[0]
             for k in range(1, 6):
                 flux = flux + faces[k, w] * sides[k]
             return centre, flux
 
         for source, target, span in ((ua, ub, spans[1]), (ub, ua, spans[2])):
-            for w in span:
-                for c in range(3):
-                    centre, flux = flux_at(source, c, w)
+            for c in range(3):
+                turned = {}
+                for w in span:
+                    centre, flux = flux_at(source, c, w, turned)
                     target[c, w] = (1.0 - damping) * centre + weight[w] * (f[c, w] + flux)
-        for w in spans[3]:
-            for c in range(3):
-                centre, flux = flux_at(ua, c, w)
+        for c in range(3):
+            turned = {}
+            for w in spans[3]:
+                centre, flux = flux_at(ua, c, w, turned)
                 residual(c, w, f[c, w] + flux - diag[w] * centre)
 
     def pool(value):
@@ -411,10 +426,9 @@
     level(0.25**3, near3, outside3, fw, mw, faces, weight, diag, ua, ub, spans, to_level4)
     for w in range(1, window - 1):
         m4[w] = pool(mw[w])
-    mine = row == x_at
 
     def own_row(value):
-        return jnp.sum(jnp.where(mine, value, 0.0), axis=0, keepdims=True)
+        return value[REACH:REACH + 1]
 
     def keep(c, w, value):
         rows_out[3 + c:4 + c] = own_row(value)
@@ -615,11 +629,17 @@
         )(packet, *y_halo, *x_halo)
         results.append(u_own)
     column = lax.all_to_all(jnp.broadcast_to(packet[None], (count_x, 4, 128)), "gx", 0, 0)
-    column = column.transpose(1, 0, 2)
-    gathered = lax.all_to_all(
-        jnp.broadcast_to(column[None], (count_y, 4, count_x, 128)), "gy", 0, 0
-    )
-    block = (2 * REACH + 1, count_x, 128)
+    width = 2 * REACH + 2
+    window = pl.pallas_call(
+        window_kernel,
+        out_shape=jax.ShapeDtypeStruct((count_y, 4 * width, 128), f32),
+        in_specs=on_chip(1),
+        out_specs=on_chip(1)[0],
+        scratch_shapes=[pltpu.VMEM((4 * width, 128), f32)],
+        compiler_params=LIMIT,
+    )(column)
+    gathered = lax.all_to_all(window, "gy", 0, 0)
+    block = (2 * REACH + 1, 16, 128)
     field, vector, six = (pltpu.VMEM(lead + block, f32) for lead in ((), (3,), (6,)))
     last = pl.pallas_call(
         last_kernel,

time: 96.7 us -> 93.8 us (0.970)
  Pallas kernels: 20.3 us -> 18.6 us
  blocking collectives: 40.4 us -> 38.7 us
    pallas_call x1, Pallas kernels: 4.93 us -> 3.12 us  [on_device(): pl.pallas_call(last_kernel, out_shape=tuple((jax.ShapeDtypeStruct(shape,...]
    all_to_all x1, blocking collectives: 22.4 us -> 20.7 us  [on_device(): gathered = lax.all_to_all(window, 'gy', 0, 0)]
where the time goes in v5:
time: 93.8 us; the launch traced here: 92.2 us
  blocking collectives  38.7 us (41%)
  waiting for transfers between devices  19.7 us (21%)
  Pallas kernels  18.6 us (20%)
  starting transfers between devices  14.2 us (15%)
    all_to_all x1, blocking collectives, on_device(): gathered = lax.all_to_all(window, 'gy', 0, 0)  20.7 us
    ppermute x14, waiting for transfers between devices, pair_swap(): return lax.ppermute(value, ('gx', 'gy'), route)  19.7 us
    all_to_all x1, blocking collectives, on_device(): lax.all_to_all(jnp.broadcast_to(packet[None], (count_x, 4, 128)), 'gx', 0...  18 us
    ppermute x14, starting transfers between devices, pair_swap(): return lax.ppermute(value, ('gx', 'gy'), route)  14.2 us
    pallas_call x1, Pallas kernels, on_device(): pl.pallas_call(outer_kernel, out_shape=(jax.ShapeDtypeStruct(velocity_gue...  4.52 us
    pallas_call x1, Pallas kernels, on_device(): pl.pallas_call(inner_kernel, out_shape=tuple((jax.ShapeDtypeStruct(shape,...  4.28 us
    pallas_call x1, Pallas kernels, on_device(): pl.pallas_call(pack_kernel, out_shape=(y_edge, y_edge, x_edge, x_edge), i...  3.63 us
    pallas_call x1, Pallas kernels, on_device(): pl.pallas_call(last_kernel, out_shape=tuple((jax.ShapeDtypeStruct(shape,...  3.12 us
  transfers between devices with their start and end apart: 14, of which 6 were waited for; matrix products, arithmetic and copies ran while one was open for 0% of the time, Pallas kernels for 5%

profile of v5, /device:TPU:32, one launch (start us, length us, event | category | flops | bytes accessed | tf_op | source)
XLA Modules:
  0.0 92.2 jit_solution(10950402537391462060)
XLA Ops:
  0.7 3.6 %shard_map.91 = (f32[7,16,4,256]{3,2,1,0:T(4,128)}, f32[7,16,4,256]{3,2,1,0:T(4,128)}, f32[25,16,256]{2,1,0:T(8,128)}, f32[25,16,256]{2,1,0:T(8,128)}) custom-call(f32[4]{0:T(128)} %viscosities.3, f32[3,16,16,256]{3,2,1,0:T(8,128)} %u_in.3, f32[3,16,16,256]{3,2,1,0:T(8,128)} %f_in.3, s32[16,16,256]{2,1,0:T(8,128)} %types.3), custom_call_target="tpu_custom_call" | custom-call | tf_op jit(solution)/shard_map/pallas_call | solution.py:550
  4.3 1.7 %collective-permute-start = (f32[7,16,4,256]{3,2,1,0:T(4,128)}, f32[7,16,4,256]{3,2,1,0:T(4,128)S(1)}, u32[]{:S(2)}, u32[]{:S(2)}) collective-permute-start(f32[7,16,4,256]{3,2,1,0:T(4,128)} %get-tuple-element.26), channel_id=1, source_target_pairs={{0,1},{1,0},{2,3},{3,2},{4,5},{5,4},{6,7},{7,6},{8,9},{9,8},{10,11... | collective-permute-start | bytes 1376264 | tf_op jit(solution)/shard_map/ppermute | solution.py:32
  6.0 0.5 collective-permute-start.2
  6.5 0.1 collective-permute-start.3
  6.6 10.3 %collective-permute-done.y_first = f32[7,16,4,256]{3,2,1,0:T(4,128)S(1)} collective-permute-done((f32[7,16,4,256]{3,2,1,0:T(4,128)}, f32[7,16,4,256]{3,2,1,0:T(4,128)S(1)}, u32[]{:S(2)}, u32[]{:S(2)}) %collective-permute-start) | collective-permute-done | bytes 458784 | tf_op jit(solution)/shard_map/ppermute | solution.py:32
  16.9 0.7 shard_map.93
  17.6 0.0 collective-permute-start.4
  17.6 0.1 collective-permute-start.5
  17.7 4.3 %shard_map.92 = (f32[3,10,16,256]{3,2,1,0:T(8,128)S(1)}, f32[16,8,128]{2,1,0:T(8,128)S(1)}, f32[4,2,3,2,24,256]{5,4,3,2,1,0:T(8,128)S(1)}, f32[2,3,4,24,256]{4,3,2,1,0:T(8,128)S(1)}, f32[2,5,24,256]{3,2,1,0:T(8,128)S(1)}) custom-call(f32[4]{0:T(128)S(1)} %copy-done.3, f32[3,16,16,256]{3,2,1,0:T(8,128)S(1)} %copy-done, f32[3,16,16,256]{3,2,1,0:T(8,128)S(1)} %copy-done.1, ...), custom_call_target="tpu_custom_call" | custom-call | flops 60000000 | bytes 6000000 | tf_op jit(solution)/shard_map/pallas_call | solution.py:578
  22.0 0.0 collective-permute-done.2.x_first
  22.0 0.5 collective-permute-done.5.corner_second
  22.5 4.5 %shard_map.94 = (f32[3,16,16,256]{3,2,1,0:T(8,128)}, f32[32,8,128]{2,1,0:T(8,128)S(1)}) custom-call(f32[3,10,16,256]{3,2,1,0:T(8,128)S(1)} %get-tuple-element.28.u_mid, f32[16,8,128]{2,1,0:T(8,128)S(1)} %get-tuple-element.29.packet_mid, f32[4,2,3,2,24,256]{5,4,3,2,1,0:T(8,128)S(1)} %get-tuple-element.30.u_edge, ...), custom_call_target="tpu_custom_call" | custom-call | tf_op jit(solution)/shard_map/pallas_call | solution.py:587
  27.0 2.5 %collective-permute-start.6 = (f32[4,8,4,128]{3,2,1,0:T(4,128)S(1)}, f32[4,8,4,128]{3,2,1,0:T(4,128)S(1)}, u32[]{:S(2)}, u32[]{:S(2)}) collective-permute-start(f32[4,8,4,128]{3,2,1,0:T(4,128)S(1)} %get-tuple-element.53), channel_id=1, source_target_pairs={{0,1},{1,0},{2,3},{3,2},{4,5},{5,4},{6,7},{7,6},{8,9},{9,8},{10,11... | collective-permute-start | bytes 196616 | tf_op jit(solution)/shard_map/ppermute | solution.py:32
  29.5 1.2 %collective-permute-start.7 = (f32[4,8,4,128]{3,2,1,0:T(4,128)S(1)}, f32[4,8,4,128]{3,2,1,0:T(4,128)S(1)}, u32[]{:S(2)}, u32[]{:S(2)}) collective-permute-start(f32[4,8,4,128]{3,2,1,0:T(4,128)S(1)} %get-tuple-element.52), channel_id=1, source_target_pairs={{0,16},{1,2},{2,1},{3,4},{4,3},{5,6},{6,5},{7,8},{8,7},{9,10},{10,... | collective-permute-start | bytes 196616 | tf_op jit(solution)/shard_map/ppermute | solution.py:32
  30.8 1.0 %collective-permute-done.6.y_first = f32[4,8,4,128]{3,2,1,0:T(4,128)S(1)} collective-permute-done((f32[4,8,4,128]{3,2,1,0:T(4,128)S(1)}, f32[4,8,4,128]{3,2,1,0:T(4,128)S(1)}, u32[]{:S(2)}, u32[]{:S(2)}) %collective-permute-start.6) | collective-permute-done | bytes 65568 | tf_op jit(solution)/shard_map/ppermute | solution.py:32
  31.9 0.7 collective-permute-start.8
  32.6 1.1 %collective-permute-start.9 = (f32[4,4,16,128]{3,2,1,0:T(8,128)S(1)}, f32[4,4,16,128]{3,2,1,0:T(8,128)S(1)}, u32[]{:S(2)}, u32[]{:S(2)}) collective-permute-start(f32[4,4,16,128]{3,2,1,0:T(8,128)S(1)} %get-tuple-element.46), channel_id=1, source_target_pairs={{0,1},{1,0},{2,3},{3,2},{4,5},{5,4},{6,7},{7,6},{8,9},{9,8},{10,11... | collective-permute-start | bytes 393224 | tf_op jit(solution)/shard_map/ppermute | solution.py:32
  33.7 3.3 %collective-permute-done.9.x_second = f32[4,4,16,128]{3,2,1,0:T(8,128)S(1)} collective-permute-done((f32[4,4,16,128]{3,2,1,0:T(8,128)S(1)}, f32[4,4,16,128]{3,2,1,0:T(8,128)S(1)}, u32[]{:S(2)}, u32[]{:S(2)}) %collective-permute-start.9) | collective-permute-done | bytes 131104 | tf_op jit(solution)/shard_map/ppermute | solution.py:32
  37.0 1.2 %shard_map.95 = (f32[3,8,8,128]{3,2,1,0:T(8,128)}, f32[16,4,128]{2,1,0:T(4,128)S(1)}) custom-call(f32[4,8,8,128]{3,2,1,0:T(8,128)S(1)} %bitcast.12, f32[4,8,4,128]{3,2,1,0:T(4,128)S(1)} %collective-permute-done.6.y_first, f32[4,8,4,128]{3,2,1,0:T(4,128)S(1)} %collective-permute-done.7.y_second, f32[4,4,16,128]{3,2,1,0:T(8,128)S(1)} %collective-permute-done.8.x_first, ...), custom_call_target="tpu_custom_call" | custom-call | tf_op jit(solution)/shard_map/pallas_call | solution.py:619
  38.1 4.5 %collective-permute-start.10 = (f32[4,4,4,128]{3,2,1,0:T(4,128)S(1)}, f32[4,4,4,128]{3,2,1,0:T(4,128)S(1)}, u32[]{:S(2)}, u32[]{:S(2)}) collective-permute-start(f32[4,4,4,128]{3,2,1,0:T(4,128)S(1)} %bitcast.15), channel_id=1, source_target_pairs={{0,1},{1,0},{2,3},{3,2},{4,5},{5,4},{6,7},{7,6},{8,9},{9,8},{10,11... | collective-permute-start | bytes 98312 | tf_op jit(solution)/shard_map/ppermute | solution.py:32
  42.6 0.0 collective-permute-start.11
  42.7 0.1 pad.2.clone
  42.7 1.8 %collective-permute-done.10.y_first = f32[4,4,4,128]{3,2,1,0:T(4,128)S(1)} collective-permute-done((f32[4,4,4,128]{3,2,1,0:T(4,128)S(1)}, f32[4,4,4,128]{3,2,1,0:T(4,128)S(1)}, u32[]{:S(2)}, u32[]{:S(2)}) %collective-permute-start.10) | collective-permute-done | bytes 32800 | tf_op jit(solution)/shard_map/ppermute | solution.py:32
  44.6 0.1 pad_maximum_fusion.2
  44.6 0.1 collective-permute-start.12
  44.7 1.8 %collective-permute-start.13 = (f32[4,4,16,128]{3,2,1,0:T(8,128)S(1)}, f32[4,4,16,128]{3,2,1,0:T(8,128)S(1)}, u32[]{:S(2)}, u32[]{:S(2)}) collective-permute-start(f32[4,4,16,128]{3,2,1,0:T(8,128)S(1)} %pad_maximum_fusion.2), channel_id=1, source_target_pairs={{0,1},{1,0},{2,3},{3,2},{4,5},{5,4},{6,7},{7,6},{8,9},{9,8},{10,11... | collective-permute-start | bytes 393224 | tf_op jit(solution)/shard_map/ppermute | solution.py:32
  46.5 2.7 %collective-permute-done.13.x_second = f32[4,4,16,128]{3,2,1,0:T(8,128)S(1)} collective-permute-done((f32[4,4,16,128]{3,2,1,0:T(8,128)S(1)}, f32[4,4,16,128]{3,2,1,0:T(8,128)S(1)}, u32[]{:S(2)}, u32[]{:S(2)}) %collective-permute-start.13) | collective-permute-done | bytes 131104 | tf_op jit(solution)/shard_map/ppermute | solution.py:32
  49.2 1.1 %shard_map.96 = (f32[3,4,4,64]{3,2,1,0:T(4,128)}, f32[4,128]{1,0:T(4,128)S(1)}) custom-call(f32[4,4,4,128]{3,2,1,0:T(4,128)S(1)} %bitcast.18, f32[4,4,4,128]{3,2,1,0:T(4,128)S(1)} %collective-permute-done.10.y_first, f32[4,4,4,128]{3,2,1,0:T(4,128)S(1)} %collective-permute-done.11.y_second, f32[4,4,16,128]{3,2,1,0:T(8,128)S(1)} %collective-permute-done.12.x_first, ...), custom_call_target="tpu_custom_call" | custom-call | tf_op jit(solution)/shard_map/pallas_call | solution.py:619
  50.3 18.0 %all_to_all.10.column = f32[16,4,128]{2,1,0:T(4,128)S(1)} all-to-all(f32[16,4,128]{2,1,0:T(4,128)S(1)} %broadcast_in_dim.10), channel_id=1, replica_groups=mesh['gx'=16,'gy'=16] {'gx'}, dimensions={0} | all-to-all | bytes 65536 | tf_op jit(solution)/shard_map/all_to_all | solution.py:631
  68.3 0.1 shard_map.97
  68.4 20.7 %all_to_all.11.g = f32[16,48,128]{2,1,0:T(8,128)S(1)} all-to-all(f32[16,48,128]{2,1,0:T(8,128)S(1)} %shard_map.97), channel_id=1, replica_groups=mesh['gx'=16,'gy'=16] {'gy'}, dimensions={0} | all-to-all | bytes 786432 | tf_op jit(solution)/shard_map/all_to_all | solution.py:641
  89.1 3.1 %shard_map.98 = (f32[3,2,2,32]{3,2,1,0:T(2,128)}, f32[3,1,1,16]{3,2,1,0:T(1,128)}, f32[3,1,1,16]{3,2,1,0:T(1,128)}) custom-call(f32[16,48,128]{2,1,0:T(8,128)S(1)} %all_to_all.11.g), custom_call_target="tpu_custom_call" | custom-call | tf_op jit(solution)/shard_map/pallas_call | solution.py:644
  (24 shorter events, 0.1 us)
Async XLA Ops:
  0.6 17.0 %copy-start = (f32[3,16,16,256]{3,2,1,0:T(8,128)S(1)}, f32[3,16,16,256]{3,2,1,0:T(8,128)}, u32[]{:S(2)}) copy-start(f32[3,16,16,256]{3,2,1,0:T(8,128)} %u_in.3) | copy-start | bytes 2359300
  0.6 17.0 %copy-start.1 = (f32[3,16,16,256]{3,2,1,0:T(8,128)S(1)}, f32[3,16,16,256]{3,2,1,0:T(8,128)}, u32[]{:S(2)}) copy-start(f32[3,16,16,256]{3,2,1,0:T(8,128)} %f_in.3) | copy-start | bytes 2359300
  0.7 17.0 %copy-start.2 = (s32[16,16,256]{2,1,0:T(8,128)S(1)}, s32[16,16,256]{2,1,0:T(8,128)}, u32[]{:S(2)}) copy-start(s32[16,16,256]{2,1,0:T(8,128)} %types.3) | copy-start | bytes 786436
  0.7 17.0 %copy-start.3 = (f32[4]{0:T(128)S(1)}, f32[4]{0:T(128)}, u32[]{:S(2)}) copy-start(f32[4]{0:T(128)} %viscosities.3) | copy-start | bytes 52
  4.3 12.6 %collective-permute-start = (f32[7,16,4,256]{3,2,1,0:T(4,128)}, f32[7,16,4,256]{3,2,1,0:T(4,128)S(1)}, u32[]{:S(2)}, u32[]{:S(2)}) collective-permute-start(f32[7,16,4,256]{3,2,1,0:T(4,128)} %get-tuple-element.26), channel_id=1, source_target_pairs={{0,1},{1,0},{2,3},{3,2},{4,5},{5,4},{6,7},{7,6},{8,9},{9,8},{10,11... | collective-permute-start | bytes 1376264 | tf_op jit(solution)/shard_map/ppermute | solution.py:32
  6.0 10.9 %collective-permute-start.1 = (f32[7,16,4,256]{3,2,1,0:T(4,128)}, f32[7,16,4,256]{3,2,1,0:T(4,128)S(1)}, u32[]{:S(2)}, u32[]{:S(2)}) collective-permute-start(f32[7,16,4,256]{3,2,1,0:T(4,128)} %get-tuple-element.27), channel_id=1, source_target_pairs={{0,16},{1,2},{2,1},{3,4},{4,3},{5,6},{6,5},{7,8},{8,7},{9,10},{10,... | collective-permute-start | bytes 1376264 | tf_op jit(solution)/shard_map/ppermute | solution.py:32
  6.0 16.0 %collective-permute-start.2 = (f32[25,16,256]{2,1,0:T(8,128)}, f32[25,16,256]{2,1,0:T(8,128)}, u32[]{:S(2)}, u32[]{:S(2)}) collective-permute-start(f32[25,16,256]{2,1,0:T(8,128)} %get-tuple-element.33), channel_id=1, source_target_pairs={{0,16},{1,17},{2,18},{3,19},{4,20},{5,21},{6,22},{7,23},{8,24},{9,... | collective-permute-start | bytes 1228808 | tf_op jit(solution)/shard_map/ppermute | solution.py:32
  6.5 15.5 %collective-permute-start.3 = (f32[25,16,256]{2,1,0:T(8,128)}, f32[25,16,256]{2,1,0:T(8,128)}, u32[]{:S(2)}, u32[]{:S(2)}) collective-permute-start(f32[25,16,256]{2,1,0:T(8,128)} %get-tuple-element.34), channel_id=1, source_target_pairs={{0,1},{1,0},{2,3},{3,2},{4,5},{5,4},{6,7},{7,6},{8,9},{9,8},{10,11... | collective-permute-start | bytes 1228808 | tf_op jit(solution)/shard_map/ppermute | solution.py:32
  17.6 4.4 %collective-permute-start.4 = (f32[18,8,256]{2,1,0:T(8,128)}, f32[18,8,256]{2,1,0:T(8,128)S(1)}, u32[]{:S(2)}, u32[]{:S(2)}) collective-permute-start(f32[18,8,256]{2,1,0:T(8,128)} %get-tuple-element.35), channel_id=1, source_target_pairs={{0,16},{1,17},{2,18},{3,19},{4,20},{5,21},{6,22},{7,23},{8,24},{9,... | collective-permute-start | bytes 442376 | tf_op jit(solution)/shard_map/ppermute | solution.py:32
  17.6 4.9 %collective-permute-start.5 = (f32[18,8,256]{2,1,0:T(8,128)}, f32[18,8,256]{2,1,0:T(8,128)}, u32[]{:S(2)}, u32[]{:S(2)}) collective-permute-start(f32[18,8,256]{2,1,0:T(8,128)} %get-tuple-element.36), channel_id=1, source_target_pairs={{0,1},{1,0},{2,3},{3,2},{4,5},{5,4},{6,7},{7,6},{8,9},{9,8},{10,11... | collective-permute-start | bytes 442376 | tf_op jit(solution)/shard_map/ppermute | solution.py:32
  27.0 4.7 %collective-permute-start.6 = (f32[4,8,4,128]{3,2,1,0:T(4,128)S(1)}, f32[4,8,4,128]{3,2,1,0:T(4,128)S(1)}, u32[]{:S(2)}, u32[]{:S(2)}) collective-permute-start(f32[4,8,4,128]{3,2,1,0:T(4,128)S(1)} %get-tuple-element.53), channel_id=1, source_target_pairs={{0,1},{1,0},{2,3},{3,2},{4,5},{5,4},{6,7},{7,6},{8,9},{9,8},{10,11... | collective-permute-start | bytes 196616 | tf_op jit(solution)/shard_map/ppermute | solution.py:32
  29.5 2.2 %collective-permute-start.7 = (f32[4,8,4,128]{3,2,1,0:T(4,128)S(1)}, f32[4,8,4,128]{3,2,1,0:T(4,128)S(1)}, u32[]{:S(2)}, u32[]{:S(2)}) collective-permute-start(f32[4,8,4,128]{3,2,1,0:T(4,128)S(1)} %get-tuple-element.52), channel_id=1, source_target_pairs={{0,16},{1,2},{2,1},{3,4},{4,3},{5,6},{6,5},{7,8},{8,7},{9,10},{10,... | collective-permute-start | bytes 196616 | tf_op jit(solution)/shard_map/ppermute | solution.py:32
  31.9 1.8 %collective-permute-start.8 = (f32[4,4,16,128]{3,2,1,0:T(8,128)S(1)}, f32[4,4,16,128]{3,2,1,0:T(8,128)S(1)}, u32[]{:S(2)}, u32[]{:S(2)}) collective-permute-start(f32[4,4,16,128]{3,2,1,0:T(8,128)S(1)} %get-tuple-element.47), channel_id=1, source_target_pairs={{0,16},{1,17},{2,18},{3,19},{4,20},{5,21},{6,22},{7,23},{8,24},{9,... | collective-permute-start | bytes 393224 | tf_op jit(solution)/shard_map/ppermute | solution.py:32
  32.6 4.4 %collective-permute-start.9 = (f32[4,4,16,128]{3,2,1,0:T(8,128)S(1)}, f32[4,4,16,128]{3,2,1,0:T(8,128)S(1)}, u32[]{:S(2)}, u32[]{:S(2)}) collective-permute-start(f32[4,4,16,128]{3,2,1,0:T(8,128)S(1)} %get-tuple-element.46), channel_id=1, source_target_pairs={{0,1},{1,0},{2,3},{3,2},{4,5},{5,4},{6,7},{7,6},{8,9},{9,8},{10,11... | collective-permute-start | bytes 393224 | tf_op jit(solution)/shard_map/ppermute | solution.py:32
  38.1 6.4 %collective-permute-start.10 = (f32[4,4,4,128]{3,2,1,0:T(4,128)S(1)}, f32[4,4,4,128]{3,2,1,0:T(4,128)S(1)}, u32[]{:S(2)}, u32[]{:S(2)}) collective-permute-start(f32[4,4,4,128]{3,2,1,0:T(4,128)S(1)} %bitcast.15), channel_id=1, source_target_pairs={{0,1},{1,0},{2,3},{3,2},{4,5},{5,4},{6,7},{7,6},{8,9},{9,8},{10,11... | collective-permute-start | bytes 98312 | tf_op jit(solution)/shard_map/ppermute | solution.py:32
  42.6 1.9 %collective-permute-start.11 = (f32[4,4,4,128]{3,2,1,0:T(4,128)S(1)}, f32[4,4,4,128]{3,2,1,0:T(4,128)S(1)}, u32[]{:S(2)}, u32[]{:S(2)}) collective-permute-start(f32[4,4,4,128]{3,2,1,0:T(4,128)S(1)} %bitcast.16), channel_id=1, source_target_pairs={{0,16},{1,2},{2,1},{3,4},{4,3},{5,6},{6,5},{7,8},{8,7},{9,10},{10,... | collective-permute-start | bytes 98312 | tf_op jit(solution)/shard_map/ppermute | solution.py:32
  44.6 1.9 %collective-permute-start.12 = (f32[4,4,16,128]{3,2,1,0:T(8,128)S(1)}, f32[4,4,16,128]{3,2,1,0:T(8,128)S(1)}, u32[]{:S(2)}, u32[]{:S(2)}) collective-permute-start(f32[4,4,16,128]{3,2,1,0:T(8,128)S(1)} %pad_maximum_fusion.2), channel_id=1, source_target_pairs={{0,16},{1,17},{2,18},{3,19},{4,20},{5,21},{6,22},{7,23},{8,24},{9,... | collective-permute-start | bytes 393224 | tf_op jit(solution)/shard_map/ppermute | solution.py:32
  44.7 4.5 %collective-permute-start.13 = (f32[4,4,16,128]{3,2,1,0:T(8,128)S(1)}, f32[4,4,16,128]{3,2,1,0:T(8,128)S(1)}, u32[]{:S(2)}, u32[]{:S(2)}) collective-permute-start(f32[4,4,16,128]{3,2,1,0:T(8,128)S(1)} %pad_maximum_fusion.2), channel_id=1, source_target_pairs={{0,1},{1,0},{2,3},{3,2},{4,5},{5,4},{6,7},{7,6},{8,9},{9,8},{10,11... | collective-permute-start | bytes 393224 | tf_op jit(solution)/shard_map/ppermute | solution.py:32

commit v6 on v5

--- a/solution.py
+++ b/solution.py
@@ -286,8 +286,17 @@
         field[body, :rows] = p_in[c]
         field[body, rows:rows + HALO] = jnp.where(even_y, y_first[c], y_second[c])
         field[body, total_rows - HALO:] = jnp.where(even_y, y_second[c], y_first[c])
-        field[:HALO] = jnp.where(even_x, x_second[c], x_first[c])
-        field[HALO + own:] = jnp.where(even_x, x_first[c], x_second[c])
+        below = jnp.where(even_x, x_second[c], x_first[c])
+        above = jnp.where(even_x, x_first[c], x_second[c])
+        for start, value in ((0, below), (HALO + own, above)):
+            if value.shape[1] == total_rows:
+                field[start:start + HALO] = value
+                continue
+            half = value.shape[1]
+            left = lax.broadcasted_iota(jnp.int32, value.shape[1:], 1) < 64
+            for i in range(HALO):
+                field[start + i, :half] = jnp.where(left, value[i], 0.0)
+                field[start + i, half:] = jnp.where(left, pltpu.roll(value[i], 64, 1), 0.0)
     shape = m.shape[1:]
     in_rows = inside_rows(place, rows, total_rows, shape)
     in_lower = inside_rows(place, rows, total_rows, shape, place[0] > 0)
@@ -458,46 +467,53 @@
     )
 
 
-def pack_kernel(viscosities, u_in, f_in, types, y_first, y_second, x_first, x_second, kinds, done):
-    place = own_place()
+def start_all(pairs, done):
+    copies = [pltpu.make_async_copy(*pair, done.at[i]) for i, pair in enumerate(pairs)]
+    for copy in copies:
+        copy.start()
+    return copies
+
+
+def pack_rows_kernel(viscosities, u_in, f_in, types, first, second, turn, kinds, done):
     own, rows = types.shape[:2]
-    even_x, even_y = is_even(place[0]), is_even(place[1])
-    upper, upper_f, lower = own - HALO, own - HALO + 1, 0
-    at_first, at_second = jnp.where(even_x, upper, lower), jnp.where(even_x, lower, upper)
-    f_first, f_second = jnp.where(even_x, upper_f, lower), jnp.where(even_x, lower, upper_f)
-    always, if_even, if_odd = [(types, kinds)], [], []
+    even = is_even(lax.axis_index("gy"))
+    if_even, if_odd = [(types, kinds)], [(types, kinds)]
+    for c in range(6):
+        field = u_in.at[c] if c < 3 else f_in.at[c - 3]
+        top, bottom = field.at[:, pl.ds(rows - HALO, HALO)], field.at[:, pl.ds(0, HALO)]
+        if_even += [(top, first.at[c]), (bottom, second.at[c])]
+        if_odd += [(bottom, first.at[c]), (top, second.at[c])]
+    pl.when(even)(lambda: start_all(if_even, done) and None)
+    pl.when(jnp.logical_not(even))(lambda: start_all(if_odd, done) and None)
+    turn[...] = jnp.zeros(turn.shape, jnp.float32)
+    waits = [pltpu.make_async_copy(*pair, done.at[i]) for i, pair in enumerate(if_even)]
+    waits[0].wait()
+    top = viscosity_of(kinds[:, rows - HALO:], viscosities)
+    bottom = viscosity_of(kinds[:, :HALO], viscosities)
+    first[6], second[6] = jnp.where(even, top, bottom), jnp.where(even, bottom, top)
+    for copy in waits[1:]:
+        copy.wait()
+
+
+def pack_planes_kernel(viscosities, turn, u_in, f_in, types, first, second, kinds, done):
+    own = types.shape[0]
+    even = is_even(lax.axis_index("gx"))
+    starts = [
+        (jnp.where(upper, own - HALO, 0), jnp.where(upper, own - HALO + 1, 0))
+        for upper in (even, jnp.logical_not(even))
+    ]
+    pairs = [(types.at[pl.ds(starts[k][0], HALO)], kinds.at[k]) for k in range(2)]
     at = 3 * HALO
     for c in range(3):
-        for k, field in ((0, u_in), (3, f_in)):
-            top, bottom = field.at[c, :, pl.ds(rows - HALO, HALO)], field.at[c, :, pl.ds(0, HALO)]
-            if_even += [(top, y_first.at[k + c]), (bottom, y_second.at[k + c])]
-            if_odd += [(bottom, y_first.at[k + c]), (top, y_second.at[k + c])]
-        here = pl.ds(HALO * c, HALO)
-        always.append((u_in.at[c, pl.ds(at_first, HALO)], x_first.at[here]))
-        always.append((u_in.at[c, pl.ds(at_second, HALO)], x_second.at[here]))
-        here = pl.ds(at, HALO - 1)
-        always.append((f_in.at[c, pl.ds(f_first, HALO - 1)], x_first.at[here]))
-        always.append((f_in.at[c, pl.ds(f_second, HALO - 1)], x_second.at[here]))
+        for target, (start, start_f) in zip((first, second), starts):
+            pairs.append((u_in.at[c, pl.ds(start, HALO)], target.at[pl.ds(HALO * c, HALO)]))
+            pairs.append((f_in.at[c, pl.ds(start_f, HALO - 1)], target.at[pl.ds(at, HALO - 1)]))
         at += HALO - 1
-
-    def copies(pairs, first):
-        return [pltpu.make_async_copy(*pair, done.at[first + i]) for i, pair in enumerate(pairs)]
-
-    def start(pairs, first):
-        for copy in copies(pairs, first):
-            copy.start()
-
-    start(always[:1], 0)
-    pl.when(even_y)(lambda: start(if_even, len(always)))
-    pl.when(jnp.logical_not(even_y))(lambda: start(if_odd, len(always)))
-    start(always[1:], 1)
-    copies(always[:1], 0)[0].wait()
-    top = viscosity_of(kinds[:, rows - HALO:], viscosities)
-    bottom = viscosity_of(kinds[:, :HALO], viscosities)
-    y_first[6], y_second[6] = jnp.where(even_y, top, bottom), jnp.where(even_y, bottom, top)
-    x_first[at:] = viscosity_of(kinds[pl.ds(at_first, HALO)], viscosities)
-    x_second[at:] = viscosity_of(kinds[pl.ds(at_second, HALO)], viscosities)
-    for copy in copies(always[1:], 1) + copies(if_even, len(always)):
+    copies = start_all(pairs, done)
+    for k, target in enumerate((first, second)):
+        copies[k].wait()
+        target[at:] = viscosity_of(kinds[k], viscosities)
+    for copy in copies[2:]:
         copy.wait()
 
 
@@ -547,15 +563,25 @@
     own, rows, lanes = cell_type.shape
     y_edge = jax.ShapeDtypeStruct((7, own, HALO, lanes), f32)
     x_edge = jax.ShapeDtypeStruct((7 * HALO - 3, rows, lanes), f32)
-    y_out, y_out_odd, x_out, x_out_odd = pl.pallas_call(
-        pack_kernel,
-        out_shape=(y_edge, y_edge, x_edge, x_edge),
-        in_specs=in_smem + [pl.BlockSpec(memory_space=pl.ANY)] * 3,
-        out_specs=tuple(on_chip(4)),
-        scratch_shapes=[pltpu.VMEM(cell_type.shape, jnp.int32), pltpu.SemaphoreType.DMA((25,))],
-        compiler_params=pltpu.CompilerParams(vmem_limit_bytes=PACK_LIMIT),
+    anywhere = [pl.BlockSpec(memory_space=pl.ANY)]
+    pack_params = pltpu.CompilerParams(vmem_limit_bytes=PACK_LIMIT)
+    y_out, y_out_odd, turn = pl.pallas_call(
+        pack_rows_kernel,
+        out_shape=(y_edge, y_edge, jax.ShapeDtypeStruct((8, 128), f32)),
+        in_specs=in_smem + anywhere * 3,
+        out_specs=tuple(on_chip(3)),
+        scratch_shapes=[pltpu.VMEM(cell_type.shape, jnp.int32), pltpu.SemaphoreType.DMA((13,))],
+        compiler_params=pack_params,
     )(viscosities, velocity_guess, forcing, cell_type)
     y_halo = swapped(y_out, y_out_odd, "gy")
+    x_out, x_out_odd = pl.pallas_call(
+        pack_planes_kernel,
+        out_shape=(x_edge, x_edge),
+        in_specs=in_smem + on_chip(1) + anywhere * 3,
+        out_specs=tuple(on_chip(2)),
+        scratch_shapes=[pltpu.VMEM((2, HALO, rows, lanes), jnp.int32), pltpu.SemaphoreType.DMA((14,))],
+        compiler_params=pack_params,
+    )(viscosities, turn, velocity_guess, forcing, cell_type)
     x_halo = swapped(x_out, x_out_odd, "gx")
     corner = jax.ShapeDtypeStruct((corner_layers(7)[0], 2 * HALO, lanes), f32)
     corners = pl.pallas_call(
@@ -611,6 +637,11 @@
         top, bottom = (
             jnp.concatenate([part[:, at:at + HALO] for part in parts], axis=2) for at in (own - HALO, 0)
         )
+        if valid <= 64:
+            top, bottom = (
+                jnp.concatenate([tall[:, :, :2 * HALO, :64], tall[:, :, 2 * HALO:, :64]], axis=3)
+                for tall in (top, bottom)
+            )
         x_halo = swapped(jnp.where(even_x, top, bottom), jnp.where(even_x, bottom, top), "gx")
         if grid_level == 1:
             packet_shape, pooled_shape = (4 * own // 2, rows // 2, 128), (4 * own // 2, rows, 128)

time: 93.8 us -> 91.4 us (0.974)
  waiting for transfers between devices: 19.7 us -> 15.6 us
  blocking collectives: 38.7 us -> 36.2 us
  Pallas kernels: 18.6 us -> 20.9 us
  starting transfers between devices: 14.2 us -> 15.9 us
    ppermute x14, waiting for transfers between devices: 19.7 us -> 15.6 us  [pair_swap(): return lax.ppermute(value, ('gx', 'gy'), route)]
    pallas_call x1 -> x2, Pallas kernels: 3.63 us -> 5.92 us  [the longest x1 3.02 us: on_device(): pl.pallas_call(pack_planes_kernel, out_shape=(x_edge, x_edge), in_specs=i...]
    all_to_all x1, blocking collectives: 20.7 us -> 18.6 us  [on_device(): gathered = lax.all_to_all(window, 'gy', 0, 0)]
    ppermute x14, starting transfers between devices: 14.2 us -> 15.9 us  [pair_swap(): return lax.ppermute(value, ('gx', 'gy'), route)]
    pallas_call x1, Pallas kernels: 4.52 us -> 3.37 us  [on_device(): pl.pallas_call(outer_kernel, out_shape=(jax.ShapeDtypeStruct(velocity_gue...]
  transfers between devices with their start and end apart: 14 -> 14, of which waited for: 6 -> 5; matrix products, arithmetic and copies ran while one was open for 0% -> 0% of each run, Pallas kernels for 5% -> 10%
where the time goes in v6:
time: 91.4 us; the launch traced here: 89.7 us
  blocking collectives  36.2 us (40%)
  Pallas kernels  20.9 us (23%)
  starting transfers between devices  15.9 us (17%)
  waiting for transfers between devices  15.6 us (17%)
    all_to_all x1, blocking collectives, on_device(): gathered = lax.all_to_all(window, 'gy', 0, 0)  18.6 us
    all_to_all x1, blocking collectives, on_device(): lax.all_to_all(jnp.broadcast_to(packet[None], (count_x, 4, 128)), 'gx', 0...  17.7 us
    ppermute x14, starting transfers between devices, pair_swap(): return lax.ppermute(value, ('gx', 'gy'), route)  15.9 us
    ppermute x14, waiting for transfers between devices, pair_swap(): return lax.ppermute(value, ('gx', 'gy'), route)  15.6 us
    pallas_call x1, Pallas kernels, on_device(): pl.pallas_call(inner_kernel, out_shape=tuple((jax.ShapeDtypeStruct(shape,...  4.91 us
    pallas_call x1, Pallas kernels, on_device(): pl.pallas_call(outer_kernel, out_shape=(jax.ShapeDtypeStruct(velocity_gue...  3.37 us
    pallas_call x1, Pallas kernels, on_device(): pl.pallas_call(last_kernel, out_shape=tuple((jax.ShapeDtypeStruct(shape,...  3.12 us
    pallas_call x1, Pallas kernels, on_device(): pl.pallas_call(pack_planes_kernel, out_shape=(x_edge, x_edge), in_specs=i...  3.02 us
  transfers between devices with their start and end apart: 14, of which 5 were waited for; matrix products, arithmetic and copies ran while one was open for 0% of the time, Pallas kernels for 10%

profile of v6, /device:TPU:32, one launch (start us, length us, event | category | flops | bytes accessed | tf_op | source)
XLA Modules:
  0.0 89.7 jit_solution(9369931096800457651)
XLA Ops:
  0.6 2.9 %shard_map.91 = (f32[7,16,4,256]{3,2,1,0:T(4,128)}, f32[7,16,4,256]{3,2,1,0:T(4,128)}, f32[8,128]{1,0:T(8,128)}) custom-call(f32[4]{0:T(128)} %viscosities.5, f32[3,16,16,256]{3,2,1,0:T(8,128)} %u_in.5, f32[3,16,16,256]{3,2,1,0:T(8,128)} %f_in.5, s32[16,16,256]{2,1,0:T(8,128)} %types.5), custom_call_target="tpu_custom_call" | custom-call | tf_op jit(solution)/shard_map/pallas_call | solution.py:568
  3.5 1.7 %collective-permute-start = (f32[7,16,4,256]{3,2,1,0:T(4,128)}, f32[7,16,4,256]{3,2,1,0:T(4,128)}, u32[]{:S(2)}, u32[]{:S(2)}) collective-permute-start(f32[7,16,4,256]{3,2,1,0:T(4,128)} %get-tuple-element.27), channel_id=1, source_target_pairs={{0,1},{1,0},{2,3},{3,2},{4,5},{5,4},{6,7},{7,6},{8,9},{9,8},{10,11... | collective-permute-start | bytes 1376264 | tf_op jit(solution)/shard_map/ppermute | solution.py:32
  5.3 0.0 copy-start.3
  5.3 3.0 %shard_map.93 = (f32[25,16,256]{2,1,0:T(8,128)}, f32[25,16,256]{2,1,0:T(8,128)}) custom-call(f32[4]{0:T(128)} %viscosities.5, f32[8,128]{1,0:T(8,128)} %get-tuple-element.34.turn, f32[3,16,16,256]{3,2,1,0:T(8,128)} %u_in.5, f32[3,16,16,256]{3,2,1,0:T(8,128)} %f_in.5, s32[16,16,256]{2,1,0:T(8,128)} %types.5), custom_call_target="tpu_custom_call" | custom-call | tf_op jit(solution)/shard_map/pallas_call | solution.py:577
  8.3 0.6 collective-permute-start.2
  8.9 0.0 collective-permute-start.3
  8.9 7.3 %collective-permute-done.y_first = f32[7,16,4,256]{3,2,1,0:T(4,128)} collective-permute-done((f32[7,16,4,256]{3,2,1,0:T(4,128)}, f32[7,16,4,256]{3,2,1,0:T(4,128)}, u32[]{:S(2)}, u32[]{:S(2)}) %collective-permute-start) | collective-permute-done | bytes 458784 | tf_op jit(solution)/shard_map/ppermute | solution.py:32
  16.2 1.2 %shard_map.94 = (f32[18,8,256]{2,1,0:T(8,128)S(1)}, f32[18,8,256]{2,1,0:T(8,128)S(1)}) custom-call(f32[7,16,4,256]{3,2,1,0:T(4,128)} %collective-permute-done.y_first, f32[7,16,4,256]{3,2,1,0:T(4,128)} %collective-permute-done.1.y_second), custom_call_target="tpu_custom_call" | custom-call | tf_op jit(solution)/shard_map/pallas_call | solution.py:587
  17.4 0.1 collective-permute-start.4
  17.5 0.1 collective-permute-start.5
  17.7 4.9 %shard_map.92 = (f32[3,10,16,256]{3,2,1,0:T(8,128)S(1)}, f32[16,8,128]{2,1,0:T(8,128)S(1)}, f32[4,2,3,2,24,256]{5,4,3,2,1,0:T(8,128)S(1)}, f32[2,3,4,24,256]{4,3,2,1,0:T(8,128)S(1)}, f32[2,5,24,256]{3,2,1,0:T(8,128)S(1)}) custom-call(f32[4]{0:T(128)S(1)} %copy-done.3, f32[3,16,16,256]{3,2,1,0:T(8,128)S(1)} %copy-done, f32[3,16,16,256]{3,2,1,0:T(8,128)S(1)} %copy-done.1, ...), custom_call_target="tpu_custom_call" | custom-call | flops 60000000 | bytes 6000000 | tf_op jit(solution)/shard_map/pallas_call | solution.py:604
  22.6 0.0 collective-permute-done.2.x_first
  22.6 3.4 %shard_map.95 = (f32[3,16,16,256]{3,2,1,0:T(8,128)}, f32[32,8,128]{2,1,0:T(8,128)S(1)}) custom-call(f32[3,10,16,256]{3,2,1,0:T(8,128)S(1)} %get-tuple-element.29.u_mid, f32[16,8,128]{2,1,0:T(8,128)S(1)} %get-tuple-element.30.packet_mid, f32[4,2,3,2,24,256]{5,4,3,2,1,0:T(8,128)S(1)} %get-tuple-element.31.u_edge, ...), custom_call_target="tpu_custom_call" | custom-call | tf_op jit(solution)/shard_map/pallas_call | solution.py:613
  26.0 2.1 %collective-permute-start.7 = (f32[4,8,4,128]{3,2,1,0:T(4,128)S(1)}, f32[4,8,4,128]{3,2,1,0:T(4,128)S(1)}, u32[]{:S(2)}, u32[]{:S(2)}) collective-permute-start(f32[4,8,4,128]{3,2,1,0:T(4,128)S(1)} %get-tuple-element.54), channel_id=1, source_target_pairs={{0,16},{1,2},{2,1},{3,4},{4,3},{5,6},{6,5},{7,8},{8,7},{9,10},{10,... | collective-permute-start | bytes 196616 | tf_op jit(solution)/shard_map/ppermute | solution.py:32
  28.1 2.3 %collective-permute-start.6 = (f32[4,8,4,128]{3,2,1,0:T(4,128)S(1)}, f32[4,8,4,128]{3,2,1,0:T(4,128)S(1)}, u32[]{:S(2)}, u32[]{:S(2)}) collective-permute-start(f32[4,8,4,128]{3,2,1,0:T(4,128)S(1)} %get-tuple-element.55), channel_id=1, source_target_pairs={{0,1},{1,0},{2,3},{3,2},{4,5},{5,4},{6,7},{7,6},{8,9},{9,8},{10,11... | collective-permute-start | bytes 196616 | tf_op jit(solution)/shard_map/ppermute | solution.py:32
  30.4 2.2 %collective-permute-done.6.y_first = f32[4,8,4,128]{3,2,1,0:T(4,128)S(1)} collective-permute-done((f32[4,8,4,128]{3,2,1,0:T(4,128)S(1)}, f32[4,8,4,128]{3,2,1,0:T(4,128)S(1)}, u32[]{:S(2)}, u32[]{:S(2)}) %collective-permute-start.6) | collective-permute-done | bytes 65568 | tf_op jit(solution)/shard_map/ppermute | solution.py:32
  32.7 0.6 collective-permute-start.9
  33.3 1.6 %collective-permute-start.8 = (f32[4,4,16,128]{3,2,1,0:T(8,128)S(1)}, f32[4,4,16,128]{3,2,1,0:T(8,128)S(1)}, u32[]{:S(2)}, u32[]{:S(2)}) collective-permute-start(f32[4,4,16,128]{3,2,1,0:T(8,128)S(1)} %get-tuple-element.49), channel_id=1, source_target_pairs={{0,16},{1,17},{2,18},{3,19},{4,20},{5,21},{6,22},{7,23},{8,24},{9,... | collective-permute-start | bytes 393224 | tf_op jit(solution)/shard_map/ppermute | solution.py:32
  34.8 2.4 %collective-permute-done.9.x_second = f32[4,4,16,128]{3,2,1,0:T(8,128)S(1)} collective-permute-done((f32[4,4,16,128]{3,2,1,0:T(8,128)S(1)}, f32[4,4,16,128]{3,2,1,0:T(8,128)S(1)}, u32[]{:S(2)}, u32[]{:S(2)}) %collective-permute-start.9) | collective-permute-done | bytes 131104 | tf_op jit(solution)/shard_map/ppermute | solution.py:32
  37.2 1.2 %shard_map.96 = (f32[3,8,8,128]{3,2,1,0:T(8,128)}, f32[16,4,128]{2,1,0:T(4,128)S(1)}) custom-call(f32[4,8,8,128]{3,2,1,0:T(8,128)S(1)} %bitcast.12, f32[4,8,4,128]{3,2,1,0:T(4,128)S(1)} %collective-permute-done.6.y_first, f32[4,8,4,128]{3,2,1,0:T(4,128)S(1)} %collective-permute-done.7.y_second, f32[4,4,16,128]{3,2,1,0:T(8,128)S(1)} %collective-permute-done.8.x_first, ...), custom_call_target="tpu_custom_call" | custom-call | tf_op jit(solution)/shard_map/pallas_call | solution.py:650
  38.4 0.8 collective-permute-start.11
  39.1 4.1 %collective-permute-start.10 = (f32[4,4,4,128]{3,2,1,0:T(4,128)S(1)}, f32[4,4,4,128]{3,2,1,0:T(4,128)S(1)}, u32[]{:S(2)}, u32[]{:S(2)}) collective-permute-start(f32[4,4,4,128]{3,2,1,0:T(4,128)S(1)} %bitcast.16), channel_id=1, source_target_pairs={{0,1},{1,0},{2,3},{3,2},{4,5},{5,4},{6,7},{7,6},{8,9},{9,8},{10,11... | collective-permute-start | bytes 98312 | tf_op jit(solution)/shard_map/ppermute | solution.py:32
  43.2 2.0 %collective-permute-done.10.y_first = f32[4,4,4,128]{3,2,1,0:T(4,128)S(1)} collective-permute-done((f32[4,4,4,128]{3,2,1,0:T(4,128)S(1)}, f32[4,4,4,128]{3,2,1,0:T(4,128)S(1)}, u32[]{:S(2)}, u32[]{:S(2)}) %collective-permute-start.10) | collective-permute-done | bytes 32800 | tf_op jit(solution)/shard_map/ppermute | solution.py:32
  45.3 0.1 fusion.2
  45.4 0.1 collective-permute-start.13
  45.5 2.0 %collective-permute-start.12 = (f32[4,4,8,128]{3,2,1,0:T(8,128)S(1)}, f32[4,4,8,128]{3,2,1,0:T(8,128)S(1)}, u32[]{:S(2)}, u32[]{:S(2)}) collective-permute-start(f32[4,4,8,128]{3,2,1,0:T(8,128)S(1)} %fusion.2), channel_id=1, source_target_pairs={{0,16},{1,17},{2,18},{3,19},{4,20},{5,21},{6,22},{7,23},{8,24},{9,... | collective-permute-start | bytes 196616 | tf_op jit(solution)/shard_map/ppermute | solution.py:32
  47.5 1.7 %collective-permute-done.13.x_second = f32[4,4,8,128]{3,2,1,0:T(8,128)S(1)} collective-permute-done((f32[4,4,8,128]{3,2,1,0:T(8,128)S(1)}, f32[4,4,8,128]{3,2,1,0:T(8,128)S(1)}, u32[]{:S(2)}, u32[]{:S(2)}) %collective-permute-start.13) | collective-permute-done | bytes 65568 | tf_op jit(solution)/shard_map/ppermute | solution.py:32
  49.1 1.2 %shard_map.97 = (f32[3,4,4,64]{3,2,1,0:T(4,128)}, f32[4,128]{1,0:T(4,128)S(1)}) custom-call(f32[4,4,4,128]{3,2,1,0:T(4,128)S(1)} %bitcast.18, f32[4,4,4,128]{3,2,1,0:T(4,128)S(1)} %collective-permute-done.10.y_first, f32[4,4,4,128]{3,2,1,0:T(4,128)S(1)} %collective-permute-done.11.y_second, f32[4,4,8,128]{3,2,1,0:T(8,128)S(1)} %collective-permute-done.12.x_first, ...), custom_call_target="tpu_custom_call" | custom-call | tf_op jit(solution)/shard_map/pallas_call | solution.py:650
  50.3 17.7 %all_to_all.10.column = f32[16,4,128]{2,1,0:T(4,128)S(1)} all-to-all(f32[16,4,128]{2,1,0:T(4,128)S(1)} %broadcast_in_dim.2), channel_id=1, replica_groups=mesh['gx'=16,'gy'=16] {'gx'}, dimensions={0} | all-to-all | bytes 65536 | tf_op jit(solution)/shard_map/all_to_all | solution.py:662
  68.0 0.1 shard_map.98
  68.0 18.6 %all_to_all.11.g = f32[16,48,128]{2,1,0:T(8,128)S(1)} all-to-all(f32[16,48,128]{2,1,0:T(8,128)S(1)} %shard_map.98), channel_id=1, replica_groups=mesh['gx'=16,'gy'=16] {'gy'}, dimensions={0} | all-to-all | bytes 786432 | tf_op jit(solution)/shard_map/all_to_all | solution.py:672
  86.6 3.1 %shard_map.99 = (f32[3,2,2,32]{3,2,1,0:T(2,128)}, f32[3,1,1,16]{3,2,1,0:T(1,128)}, f32[3,1,1,16]{3,2,1,0:T(1,128)}) custom-call(f32[16,48,128]{2,1,0:T(8,128)S(1)} %all_to_all.11.g), custom_call_target="tpu_custom_call" | custom-call | tf_op jit(solution)/shard_map/pallas_call | solution.py:675
  (24 shorter events, 0.2 us)
Async XLA Ops:
  3.5 12.7 %collective-permute-start = (f32[7,16,4,256]{3,2,1,0:T(4,128)}, f32[7,16,4,256]{3,2,1,0:T(4,128)}, u32[]{:S(2)}, u32[]{:S(2)}) collective-permute-start(f32[7,16,4,256]{3,2,1,0:T(4,128)} %get-tuple-element.27), channel_id=1, source_target_pairs={{0,1},{1,0},{2,3},{3,2},{4,5},{5,4},{6,7},{7,6},{8,9},{9,8},{10,11... | collective-permute-start | bytes 1376264 | tf_op jit(solution)/shard_map/ppermute | solution.py:32
  5.3 11.0 %collective-permute-start.1 = (f32[7,16,4,256]{3,2,1,0:T(4,128)}, f32[7,16,4,256]{3,2,1,0:T(4,128)}, u32[]{:S(2)}, u32[]{:S(2)}) collective-permute-start(f32[7,16,4,256]{3,2,1,0:T(4,128)} %get-tuple-element.28), channel_id=1, source_target_pairs={{0,16},{1,2},{2,1},{3,4},{4,3},{5,6},{6,5},{7,8},{8,7},{9,10},{10,... | collective-permute-start | bytes 1376264 | tf_op jit(solution)/shard_map/ppermute | solution.py:32
  5.3 12.4 %copy-start = (f32[3,16,16,256]{3,2,1,0:T(8,128)S(1)}, f32[3,16,16,256]{3,2,1,0:T(8,128)}, u32[]{:S(2)}) copy-start(f32[3,16,16,256]{3,2,1,0:T(8,128)} %u_in.5) | copy-start | bytes 2359300
  5.3 12.4 %copy-start.1 = (f32[3,16,16,256]{3,2,1,0:T(8,128)S(1)}, f32[3,16,16,256]{3,2,1,0:T(8,128)}, u32[]{:S(2)}) copy-start(f32[3,16,16,256]{3,2,1,0:T(8,128)} %f_in.5) | copy-start | bytes 2359300
  5.3 12.4 %copy-start.2 = (s32[16,16,256]{2,1,0:T(8,128)S(1)}, s32[16,16,256]{2,1,0:T(8,128)}, u32[]{:S(2)}) copy-start(s32[16,16,256]{2,1,0:T(8,128)} %types.5) | copy-start | bytes 786436
  5.3 12.4 %copy-start.3 = (f32[4]{0:T(128)S(1)}, f32[4]{0:T(128)}, u32[]{:S(2)}) copy-start(f32[4]{0:T(128)} %viscosities.5) | copy-start | bytes 52
  8.3 14.3 %collective-permute-start.2 = (f32[25,16,256]{2,1,0:T(8,128)}, f32[25,16,256]{2,1,0:T(8,128)S(1)}, u32[]{:S(2)}, u32[]{:S(2)}) collective-permute-start(f32[25,16,256]{2,1,0:T(8,128)} %get-tuple-element.35), channel_id=1, source_target_pairs={{0,16},{1,17},{2,18},{3,19},{4,20},{5,21},{6,22},{7,23},{8,24},{9,... | collective-permute-start | bytes 1228808 | tf_op jit(solution)/shard_map/ppermute | solution.py:32
  8.9 13.7 %collective-permute-start.3 = (f32[25,16,256]{2,1,0:T(8,128)}, f32[25,16,256]{2,1,0:T(8,128)S(1)}, u32[]{:S(2)}, u32[]{:S(2)}) collective-permute-start(f32[25,16,256]{2,1,0:T(8,128)} %get-tuple-element.36), channel_id=1, source_target_pairs={{0,1},{1,0},{2,3},{3,2},{4,5},{5,4},{6,7},{7,6},{8,9},{9,8},{10,11... | collective-permute-start | bytes 1228808 | tf_op jit(solution)/shard_map/ppermute | solution.py:32
  17.4 5.2 %collective-permute-start.4 = (f32[18,8,256]{2,1,0:T(8,128)S(1)}, f32[18,8,256]{2,1,0:T(8,128)S(1)}, u32[]{:S(2)}, u32[]{:S(2)}) collective-permute-start(f32[18,8,256]{2,1,0:T(8,128)S(1)} %get-tuple-element.37), channel_id=1, source_target_pairs={{0,16},{1,17},{2,18},{3,19},{4,20},{5,21},{6,22},{7,23},{8,24},{9,... | collective-permute-start | bytes 442376 | tf_op jit(solution)/shard_map/ppermute | solution.py:32
  17.5 5.1 %collective-permute-start.5 = (f32[18,8,256]{2,1,0:T(8,128)S(1)}, f32[18,8,256]{2,1,0:T(8,128)S(1)}, u32[]{:S(2)}, u32[]{:S(2)}) collective-permute-start(f32[18,8,256]{2,1,0:T(8,128)S(1)} %get-tuple-element.38), channel_id=1, source_target_pairs={{0,1},{1,0},{2,3},{3,2},{4,5},{5,4},{6,7},{7,6},{8,9},{9,8},{10,11... | collective-permute-start | bytes 442376 | tf_op jit(solution)/shard_map/ppermute | solution.py:32
  26.0 4.4 %collective-permute-start.7 = (f32[4,8,4,128]{3,2,1,0:T(4,128)S(1)}, f32[4,8,4,128]{3,2,1,0:T(4,128)S(1)}, u32[]{:S(2)}, u32[]{:S(2)}) collective-permute-start(f32[4,8,4,128]{3,2,1,0:T(4,128)S(1)} %get-tuple-element.54), channel_id=1, source_target_pairs={{0,16},{1,2},{2,1},{3,4},{4,3},{5,6},{6,5},{7,8},{8,7},{9,10},{10,... | collective-permute-start | bytes 196616 | tf_op jit(solution)/shard_map/ppermute | solution.py:32
  28.1 4.5 %collective-permute-start.6 = (f32[4,8,4,128]{3,2,1,0:T(4,128)S(1)}, f32[4,8,4,128]{3,2,1,0:T(4,128)S(1)}, u32[]{:S(2)}, u32[]{:S(2)}) collective-permute-start(f32[4,8,4,128]{3,2,1,0:T(4,128)S(1)} %get-tuple-element.55), channel_id=1, source_target_pairs={{0,1},{1,0},{2,3},{3,2},{4,5},{5,4},{6,7},{7,6},{8,9},{9,8},{10,11... | collective-permute-start | bytes 196616 | tf_op jit(solution)/shard_map/ppermute | solution.py:32
  32.7 4.5 %collective-permute-start.9 = (f32[4,4,16,128]{3,2,1,0:T(8,128)S(1)}, f32[4,4,16,128]{3,2,1,0:T(8,128)S(1)}, u32[]{:S(2)}, u32[]{:S(2)}) collective-permute-start(f32[4,4,16,128]{3,2,1,0:T(8,128)S(1)} %get-tuple-element.48), channel_id=1, source_target_pairs={{0,1},{1,0},{2,3},{3,2},{4,5},{5,4},{6,7},{7,6},{8,9},{9,8},{10,11... | collective-permute-start | bytes 393224 | tf_op jit(solution)/shard_map/ppermute | solution.py:32
  33.3 3.9 %collective-permute-start.8 = (f32[4,4,16,128]{3,2,1,0:T(8,128)S(1)}, f32[4,4,16,128]{3,2,1,0:T(8,128)S(1)}, u32[]{:S(2)}, u32[]{:S(2)}) collective-permute-start(f32[4,4,16,128]{3,2,1,0:T(8,128)S(1)} %get-tuple-element.49), channel_id=1, source_target_pairs={{0,16},{1,17},{2,18},{3,19},{4,20},{5,21},{6,22},{7,23},{8,24},{9,... | collective-permute-start | bytes 393224 | tf_op jit(solution)/shard_map/ppermute | solution.py:32
  38.4 4.8 %collective-permute-start.11 = (f32[4,4,4,128]{3,2,1,0:T(4,128)S(1)}, f32[4,4,4,128]{3,2,1,0:T(4,128)S(1)}, u32[]{:S(2)}, u32[]{:S(2)}) collective-permute-start(f32[4,4,4,128]{3,2,1,0:T(4,128)S(1)} %bitcast.15), channel_id=1, source_target_pairs={{0,16},{1,2},{2,1},{3,4},{4,3},{5,6},{6,5},{7,8},{8,7},{9,10},{10,... | collective-permute-start | bytes 98312 | tf_op jit(solution)/shard_map/ppermute | solution.py:32
  39.1 6.1 %collective-permute-start.10 = (f32[4,4,4,128]{3,2,1,0:T(4,128)S(1)}, f32[4,4,4,128]{3,2,1,0:T(4,128)S(1)}, u32[]{:S(2)}, u32[]{:S(2)}) collective-permute-start(f32[4,4,4,128]{3,2,1,0:T(4,128)S(1)} %bitcast.16), channel_id=1, source_target_pairs={{0,1},{1,0},{2,3},{3,2},{4,5},{5,4},{6,7},{7,6},{8,9},{9,8},{10,11... | collective-permute-start | bytes 98312 | tf_op jit(solution)/shard_map/ppermute | solution.py:32
  45.4 3.8 %collective-permute-start.13 = (f32[4,4,8,128]{3,2,1,0:T(8,128)S(1)}, f32[4,4,8,128]{3,2,1,0:T(8,128)S(1)}, u32[]{:S(2)}, u32[]{:S(2)}) collective-permute-start(f32[4,4,8,128]{3,2,1,0:T(8,128)S(1)} %fusion.2), channel_id=1, source_target_pairs={{0,1},{1,0},{2,3},{3,2},{4,5},{5,4},{6,7},{7,6},{8,9},{9,8},{10,11... | collective-permute-start | bytes 196616 | tf_op jit(solution)/shard_map/ppermute | solution.py:32
  45.5 3.7 %collective-permute-start.12 = (f32[4,4,8,128]{3,2,1,0:T(8,128)S(1)}, f32[4,4,8,128]{3,2,1,0:T(8,128)S(1)}, u32[]{:S(2)}, u32[]{:S(2)}) collective-permute-start(f32[4,4,8,128]{3,2,1,0:T(8,128)S(1)} %fusion.2), channel_id=1, source_target_pairs={{0,16},{1,17},{2,18},{3,19},{4,20},{5,21},{6,22},{7,23},{8,24},{9,... | collective-permute-start | bytes 196616 | tf_op jit(solution)/shard_map/ppermute | solution.py:32

commit v7 on v6

--- a/solution.py
+++ b/solution.py
@@ -286,15 +286,16 @@
         field[body, :rows] = p_in[c]
         field[body, rows:rows + HALO] = jnp.where(even_y, y_first[c], y_second[c])
         field[body, total_rows - HALO:] = jnp.where(even_y, y_second[c], y_first[c])
-        below = jnp.where(even_x, x_second[c], x_first[c])
-        above = jnp.where(even_x, x_first[c], x_second[c])
-        for start, value in ((0, below), (HALO + own, above)):
+        width = HALO - 1 if c < 3 else HALO
+        first, second = (packet_x[(HALO - 1) * c:(HALO - 1) * c + width] for packet_x in (x_first, x_second))
+        below, above = jnp.where(even_x, second, first), jnp.where(even_x, first, second)
+        for start, value in ((HALO - width, below), (HALO + own, above)):
             if value.shape[1] == total_rows:
-                field[start:start + HALO] = value
+                field[start:start + width] = value
                 continue
             half = value.shape[1]
             left = lax.broadcasted_iota(jnp.int32, value.shape[1:], 1) < 64
-            for i in range(HALO):
+            for i in range(width):
                 field[start + i, :half] = jnp.where(left, value[i], 0.0)
                 field[start + i, half:] = jnp.where(left, pltpu.roll(value[i], 64, 1), 0.0)
     shape = m.shape[1:]
@@ -642,6 +643,10 @@
                 jnp.concatenate([tall[:, :, :2 * HALO, :64], tall[:, :, 2 * HALO:, :64]], axis=3)
                 for tall in (top, bottom)
             )
+        top, bottom = (
+            jnp.concatenate([planes[c, at:at + HALO - 1] for c in range(3)] + [planes[3]], axis=0)
+            for planes, at in ((top, 1), (bottom, 0))
+        )
         x_halo = swapped(jnp.where(even_x, top, bottom), jnp.where(even_x, bottom, top), "gx")
         if grid_level == 1:
             packet_shape, pooled_shape = (4 * own // 2, rows // 2, 128), (4 * own // 2, rows, 128)

time: 91.4 us -> 91.1 us (level)
  no operation moved by 1% of the time
where the time goes in v7:
time: 91.1 us; the launch traced here: 89.5 us
  blocking collectives  36.2 us (40%)
  Pallas kernels  20.8 us (23%)
  starting transfers between devices  16.1 us (18%)
  waiting for transfers between devices  15.2 us (17%)
    all_to_all x1, blocking collectives, on_device(): gathered = lax.all_to_all(window, 'gy', 0, 0)  18.6 us
    all_to_all x1, blocking collectives, on_device(): lax.all_to_all(jnp.broadcast_to(packet[None], (count_x, 4, 128)), 'gx', 0...  17.7 us
    ppermute x14, starting transfers between devices, pair_swap(): return lax.ppermute(value, ('gx', 'gy'), route)  16.1 us
    ppermute x14, waiting for transfers between devices, pair_swap(): return lax.ppermute(value, ('gx', 'gy'), route)  15.2 us
    pallas_call x1, Pallas kernels, on_device(): pl.pallas_call(inner_kernel, out_shape=tuple((jax.ShapeDtypeStruct(shape,...  4.91 us
    pallas_call x1, Pallas kernels, on_device(): pl.pallas_call(outer_kernel, out_shape=(jax.ShapeDtypeStruct(velocity_gue...  3.37 us
    pallas_call x1, Pallas kernels, on_device(): pl.pallas_call(last_kernel, out_shape=tuple((jax.ShapeDtypeStruct(shape,...  3.12 us
    pallas_call x1, Pallas kernels, on_device(): pl.pallas_call(pack_planes_kernel, out_shape=(x_edge, x_edge), in_specs=i...  3.01 us
  transfers between devices with their start and end apart: 14, of which 5 were waited for; matrix products, arithmetic and copies ran while one was open for 0% of the time, Pallas kernels for 10%

profile of v7, /device:TPU:32, one launch (start us, length us, event | category | flops | bytes accessed | tf_op | source)
XLA Modules:
  0.0 89.5 jit_solution(14180046846408190153)
XLA Ops:
  0.6 2.9 %shard_map.91 = (f32[7,16,4,256]{3,2,1,0:T(4,128)}, f32[7,16,4,256]{3,2,1,0:T(4,128)}, f32[8,128]{1,0:T(8,128)}) custom-call(f32[4]{0:T(128)} %viscosities.5, f32[3,16,16,256]{3,2,1,0:T(8,128)} %u_in.5, f32[3,16,16,256]{3,2,1,0:T(8,128)} %f_in.5, s32[16,16,256]{2,1,0:T(8,128)} %types.5), custom_call_target="tpu_custom_call" | custom-call | tf_op jit(solution)/shard_map/pallas_call | solution.py:569
  3.5 1.7 %collective-permute-start = (f32[7,16,4,256]{3,2,1,0:T(4,128)}, f32[7,16,4,256]{3,2,1,0:T(4,128)}, u32[]{:S(2)}, u32[]{:S(2)}) collective-permute-start(f32[7,16,4,256]{3,2,1,0:T(4,128)} %get-tuple-element.27), channel_id=1, source_target_pairs={{0,1},{1,0},{2,3},{3,2},{4,5},{5,4},{6,7},{7,6},{8,9},{9,8},{10,11... | collective-permute-start | bytes 1376264 | tf_op jit(solution)/shard_map/ppermute | solution.py:32
  5.3 0.0 copy-start.3
  5.3 3.0 %shard_map.93 = (f32[25,16,256]{2,1,0:T(8,128)}, f32[25,16,256]{2,1,0:T(8,128)}) custom-call(f32[4]{0:T(128)} %viscosities.5, f32[8,128]{1,0:T(8,128)} %get-tuple-element.34.turn, f32[3,16,16,256]{3,2,1,0:T(8,128)} %u_in.5, f32[3,16,16,256]{3,2,1,0:T(8,128)} %f_in.5, s32[16,16,256]{2,1,0:T(8,128)} %types.5), custom_call_target="tpu_custom_call" | custom-call | tf_op jit(solution)/shard_map/pallas_call | solution.py:578
  8.3 0.6 collective-permute-start.2
  8.9 0.0 collective-permute-start.3
  8.9 7.3 %collective-permute-done.y_first = f32[7,16,4,256]{3,2,1,0:T(4,128)} collective-permute-done((f32[7,16,4,256]{3,2,1,0:T(4,128)}, f32[7,16,4,256]{3,2,1,0:T(4,128)}, u32[]{:S(2)}, u32[]{:S(2)}) %collective-permute-start) | collective-permute-done | bytes 458784 | tf_op jit(solution)/shard_map/ppermute | solution.py:32
  16.2 1.2 %shard_map.94 = (f32[18,8,256]{2,1,0:T(8,128)S(1)}, f32[18,8,256]{2,1,0:T(8,128)S(1)}) custom-call(f32[7,16,4,256]{3,2,1,0:T(4,128)} %collective-permute-done.y_first, f32[7,16,4,256]{3,2,1,0:T(4,128)} %collective-permute-done.1.y_second), custom_call_target="tpu_custom_call" | custom-call | tf_op jit(solution)/shard_map/pallas_call | solution.py:588
  17.4 0.1 collective-permute-start.4
  17.5 0.1 collective-permute-start.5
  17.7 4.9 %shard_map.92 = (f32[3,10,16,256]{3,2,1,0:T(8,128)S(1)}, f32[16,8,128]{2,1,0:T(8,128)S(1)}, f32[4,2,3,2,24,256]{5,4,3,2,1,0:T(8,128)S(1)}, f32[2,3,4,24,256]{4,3,2,1,0:T(8,128)S(1)}, f32[2,5,24,256]{3,2,1,0:T(8,128)S(1)}) custom-call(f32[4]{0:T(128)S(1)} %copy-done.3, f32[3,16,16,256]{3,2,1,0:T(8,128)S(1)} %copy-done, f32[3,16,16,256]{3,2,1,0:T(8,128)S(1)} %copy-done.1, ...), custom_call_target="tpu_custom_call" | custom-call | flops 60000000 | bytes 6000000 | tf_op jit(solution)/shard_map/pallas_call | solution.py:605
  22.6 0.0 collective-permute-done.2.x_first
  22.6 3.4 %shard_map.95 = (f32[3,16,16,256]{3,2,1,0:T(8,128)}, f32[32,8,128]{2,1,0:T(8,128)S(1)}) custom-call(f32[3,10,16,256]{3,2,1,0:T(8,128)S(1)} %get-tuple-element.29.u_mid, f32[16,8,128]{2,1,0:T(8,128)S(1)} %get-tuple-element.30.packet_mid, f32[4,2,3,2,24,256]{5,4,3,2,1,0:T(8,128)S(1)} %get-tuple-element.31.u_edge, ...), custom_call_target="tpu_custom_call" | custom-call | tf_op jit(solution)/shard_map/pallas_call | solution.py:614
  26.0 2.1 %collective-permute-start.7 = (f32[4,8,4,128]{3,2,1,0:T(4,128)S(1)}, f32[4,8,4,128]{3,2,1,0:T(4,128)S(1)}, u32[]{:S(2)}, u32[]{:S(2)}) collective-permute-start(f32[4,8,4,128]{3,2,1,0:T(4,128)S(1)} %get-tuple-element.60), channel_id=1, source_target_pairs={{0,16},{1,2},{2,1},{3,4},{4,3},{5,6},{6,5},{7,8},{8,7},{9,10},{10,... | collective-permute-start | bytes 196616 | tf_op jit(solution)/shard_map/ppermute | solution.py:32
  28.1 2.3 %collective-permute-start.6 = (f32[4,8,4,128]{3,2,1,0:T(4,128)S(1)}, f32[4,8,4,128]{3,2,1,0:T(4,128)S(1)}, u32[]{:S(2)}, u32[]{:S(2)}) collective-permute-start(f32[4,8,4,128]{3,2,1,0:T(4,128)S(1)} %get-tuple-element.61), channel_id=1, source_target_pairs={{0,1},{1,0},{2,3},{3,2},{4,5},{5,4},{6,7},{7,6},{8,9},{9,8},{10,11... | collective-permute-start | bytes 196616 | tf_op jit(solution)/shard_map/ppermute | solution.py:32
  30.4 2.2 %collective-permute-done.6.y_first = f32[4,8,4,128]{3,2,1,0:T(4,128)S(1)} collective-permute-done((f32[4,8,4,128]{3,2,1,0:T(4,128)S(1)}, f32[4,8,4,128]{3,2,1,0:T(4,128)S(1)}, u32[]{:S(2)}, u32[]{:S(2)}) %collective-permute-start.6) | collective-permute-done | bytes 65568 | tf_op jit(solution)/shard_map/ppermute | solution.py:32
  32.8 0.7 collective-permute-start.9
  33.5 1.6 %collective-permute-start.8 = (f32[13,16,128]{2,1,0:T(8,128)S(1)}, f32[13,16,128]{2,1,0:T(8,128)S(1)}, u32[]{:S(2)}, u32[]{:S(2)}) collective-permute-start(f32[13,16,128]{2,1,0:T(8,128)S(1)} %get-tuple-element.49), channel_id=1, source_target_pairs={{0,16},{1,17},{2,18},{3,19},{4,20},{5,21},{6,22},{7,23},{8,24},{9,... | collective-permute-start | bytes 319496 | tf_op jit(solution)/shard_map/ppermute | solution.py:32
  35.1 2.1 %collective-permute-done.9.x_second = f32[13,16,128]{2,1,0:T(8,128)S(1)} collective-permute-done((f32[13,16,128]{2,1,0:T(8,128)S(1)}, f32[13,16,128]{2,1,0:T(8,128)S(1)}, u32[]{:S(2)}, u32[]{:S(2)}) %collective-permute-start.9) | collective-permute-done | bytes 106528 | tf_op jit(solution)/shard_map/ppermute | solution.py:32
  37.2 1.2 %shard_map.96 = (f32[3,8,8,128]{3,2,1,0:T(8,128)}, f32[16,4,128]{2,1,0:T(4,128)S(1)}) custom-call(f32[4,8,8,128]{3,2,1,0:T(8,128)S(1)} %bitcast.42, f32[4,8,4,128]{3,2,1,0:T(4,128)S(1)} %collective-permute-done.6.y_first, f32[4,8,4,128]{3,2,1,0:T(4,128)S(1)} %collective-permute-done.7.y_second, f32[13,16,128]{2,1,0:T(8,128)S(1)} %collective-permute-done.8.x_first, ...), custom_call_target="tpu_custom_call" | custom-call | tf_op jit(solution)/shard_map/pallas_call | solution.py:655
  38.3 0.8 collective-permute-start.11
  39.1 4.1 %collective-permute-start.10 = (f32[4,4,4,128]{3,2,1,0:T(4,128)S(1)}, f32[4,4,4,128]{3,2,1,0:T(4,128)S(1)}, u32[]{:S(2)}, u32[]{:S(2)}) collective-permute-start(f32[4,4,4,128]{3,2,1,0:T(4,128)S(1)} %bitcast.46), channel_id=1, source_target_pairs={{0,1},{1,0},{2,3},{3,2},{4,5},{5,4},{6,7},{7,6},{8,9},{9,8},{10,11... | collective-permute-start | bytes 98312 | tf_op jit(solution)/shard_map/ppermute | solution.py:32
  43.2 2.0 %collective-permute-done.10.y_first = f32[4,4,4,128]{3,2,1,0:T(4,128)S(1)} collective-permute-done((f32[4,4,4,128]{3,2,1,0:T(4,128)S(1)}, f32[4,4,4,128]{3,2,1,0:T(4,128)S(1)}, u32[]{:S(2)}, u32[]{:S(2)}) %collective-permute-start.10) | collective-permute-done | bytes 32800 | tf_op jit(solution)/shard_map/ppermute | solution.py:32
  45.2 0.1 fusion
  45.4 0.1 collective-permute-start.13
  45.5 2.0 %collective-permute-start.12 = (f32[13,8,128]{2,1,0:T(8,128)S(1)}, f32[13,8,128]{2,1,0:T(8,128)S(1)}, u32[]{:S(2)}, u32[]{:S(2)}) collective-permute-start(f32[13,8,128]{2,1,0:T(8,128)S(1)} %get-tuple-element.63), channel_id=1, source_target_pairs={{0,16},{1,17},{2,18},{3,19},{4,20},{5,21},{6,22},{7,23},{8,24},{9,... | collective-permute-start | bytes 159752 | tf_op jit(solution)/shard_map/ppermute | solution.py:32
  47.5 1.5 %collective-permute-done.13.x_second = f32[13,8,128]{2,1,0:T(8,128)S(1)} collective-permute-done((f32[13,8,128]{2,1,0:T(8,128)S(1)}, f32[13,8,128]{2,1,0:T(8,128)S(1)}, u32[]{:S(2)}, u32[]{:S(2)}) %collective-permute-start.13) | collective-permute-done | bytes 53280 | tf_op jit(solution)/shard_map/ppermute | solution.py:32
  49.0 1.0 %shard_map.97 = (f32[3,4,4,64]{3,2,1,0:T(4,128)}, f32[4,128]{1,0:T(4,128)S(1)}) custom-call(f32[4,4,4,128]{3,2,1,0:T(4,128)S(1)} %bitcast.48, f32[4,4,4,128]{3,2,1,0:T(4,128)S(1)} %collective-permute-done.10.y_first, f32[4,4,4,128]{3,2,1,0:T(4,128)S(1)} %collective-permute-done.11.y_second, f32[13,8,128]{2,1,0:T(8,128)S(1)} %collective-permute-done.12.x_first, ...), custom_call_target="tpu_custom_call" | custom-call | tf_op jit(solution)/shard_map/pallas_call | solution.py:655
  50.1 17.7 %all_to_all.10.column = f32[16,4,128]{2,1,0:T(4,128)S(1)} all-to-all(f32[16,4,128]{2,1,0:T(4,128)S(1)} %broadcast_in_dim.2), channel_id=1, replica_groups=mesh['gx'=16,'gy'=16] {'gx'}, dimensions={0} | all-to-all | bytes 65536 | tf_op jit(solution)/shard_map/all_to_all | solution.py:667
  67.7 0.1 shard_map.98
  67.8 18.6 %all_to_all.11.g = f32[16,48,128]{2,1,0:T(8,128)S(1)} all-to-all(f32[16,48,128]{2,1,0:T(8,128)S(1)} %shard_map.98), channel_id=1, replica_groups=mesh['gx'=16,'gy'=16] {'gy'}, dimensions={0} | all-to-all | bytes 786432 | tf_op jit(solution)/shard_map/all_to_all | solution.py:677
  86.4 3.1 %shard_map.99 = (f32[3,2,2,32]{3,2,1,0:T(2,128)}, f32[3,1,1,16]{3,2,1,0:T(1,128)}, f32[3,1,1,16]{3,2,1,0:T(1,128)}) custom-call(f32[16,48,128]{2,1,0:T(8,128)S(1)} %all_to_all.11.g), custom_call_target="tpu_custom_call" | custom-call | tf_op jit(solution)/shard_map/pallas_call | solution.py:680
  (31 shorter events, 0.2 us)
Async XLA Ops:
  3.5 12.7 %collective-permute-start = (f32[7,16,4,256]{3,2,1,0:T(4,128)}, f32[7,16,4,256]{3,2,1,0:T(4,128)}, u32[]{:S(2)}, u32[]{:S(2)}) collective-permute-start(f32[7,16,4,256]{3,2,1,0:T(4,128)} %get-tuple-element.27), channel_id=1, source_target_pairs={{0,1},{1,0},{2,3},{3,2},{4,5},{5,4},{6,7},{7,6},{8,9},{9,8},{10,11... | collective-permute-start | bytes 1376264 | tf_op jit(solution)/shard_map/ppermute | solution.py:32
  5.3 11.0 %collective-permute-start.1 = (f32[7,16,4,256]{3,2,1,0:T(4,128)}, f32[7,16,4,256]{3,2,1,0:T(4,128)}, u32[]{:S(2)}, u32[]{:S(2)}) collective-permute-start(f32[7,16,4,256]{3,2,1,0:T(4,128)} %get-tuple-element.28), channel_id=1, source_target_pairs={{0,16},{1,2},{2,1},{3,4},{4,3},{5,6},{6,5},{7,8},{8,7},{9,10},{10,... | collective-permute-start | bytes 1376264 | tf_op jit(solution)/shard_map/ppermute | solution.py:32
  5.3 12.4 %copy-start = (f32[3,16,16,256]{3,2,1,0:T(8,128)S(1)}, f32[3,16,16,256]{3,2,1,0:T(8,128)}, u32[]{:S(2)}) copy-start(f32[3,16,16,256]{3,2,1,0:T(8,128)} %u_in.5) | copy-start | bytes 2359300
  5.3 12.4 %copy-start.1 = (f32[3,16,16,256]{3,2,1,0:T(8,128)S(1)}, f32[3,16,16,256]{3,2,1,0:T(8,128)}, u32[]{:S(2)}) copy-start(f32[3,16,16,256]{3,2,1,0:T(8,128)} %f_in.5) | copy-start | bytes 2359300
  5.3 12.4 %copy-start.2 = (s32[16,16,256]{2,1,0:T(8,128)S(1)}, s32[16,16,256]{2,1,0:T(8,128)}, u32[]{:S(2)}) copy-start(s32[16,16,256]{2,1,0:T(8,128)} %types.5) | copy-start | bytes 786436
  5.3 12.4 %copy-start.3 = (f32[4]{0:T(128)S(1)}, f32[4]{0:T(128)}, u32[]{:S(2)}) copy-start(f32[4]{0:T(128)} %viscosities.5) | copy-start | bytes 52
  8.3 14.3 %collective-permute-start.2 = (f32[25,16,256]{2,1,0:T(8,128)}, f32[25,16,256]{2,1,0:T(8,128)S(1)}, u32[]{:S(2)}, u32[]{:S(2)}) collective-permute-start(f32[25,16,256]{2,1,0:T(8,128)} %get-tuple-element.35), channel_id=1, source_target_pairs={{0,16},{1,17},{2,18},{3,19},{4,20},{5,21},{6,22},{7,23},{8,24},{9,... | collective-permute-start | bytes 1228808 | tf_op jit(solution)/shard_map/ppermute | solution.py:32
  8.9 13.7 %collective-permute-start.3 = (f32[25,16,256]{2,1,0:T(8,128)}, f32[25,16,256]{2,1,0:T(8,128)S(1)}, u32[]{:S(2)}, u32[]{:S(2)}) collective-permute-start(f32[25,16,256]{2,1,0:T(8,128)} %get-tuple-element.36), channel_id=1, source_target_pairs={{0,1},{1,0},{2,3},{3,2},{4,5},{5,4},{6,7},{7,6},{8,9},{9,8},{10,11... | collective-permute-start | bytes 1228808 | tf_op jit(solution)/shard_map/ppermute | solution.py:32
  17.4 5.2 %collective-permute-start.4 = (f32[18,8,256]{2,1,0:T(8,128)S(1)}, f32[18,8,256]{2,1,0:T(8,128)S(1)}, u32[]{:S(2)}, u32[]{:S(2)}) collective-permute-start(f32[18,8,256]{2,1,0:T(8,128)S(1)} %get-tuple-element.37), channel_id=1, source_target_pairs={{0,16},{1,17},{2,18},{3,19},{4,20},{5,21},{6,22},{7,23},{8,24},{9,... | collective-permute-start | bytes 442376 | tf_op jit(solution)/shard_map/ppermute | solution.py:32
  17.5 5.1 %collective-permute-start.5 = (f32[18,8,256]{2,1,0:T(8,128)S(1)}, f32[18,8,256]{2,1,0:T(8,128)S(1)}, u32[]{:S(2)}, u32[]{:S(2)}) collective-permute-start(f32[18,8,256]{2,1,0:T(8,128)S(1)} %get-tuple-element.38), channel_id=1, source_target_pairs={{0,1},{1,0},{2,3},{3,2},{4,5},{5,4},{6,7},{7,6},{8,9},{9,8},{10,11... | collective-permute-start | bytes 442376 | tf_op jit(solution)/shard_map/ppermute | solution.py:32
  26.0 4.4 %collective-permute-start.7 = (f32[4,8,4,128]{3,2,1,0:T(4,128)S(1)}, f32[4,8,4,128]{3,2,1,0:T(4,128)S(1)}, u32[]{:S(2)}, u32[]{:S(2)}) collective-permute-start(f32[4,8,4,128]{3,2,1,0:T(4,128)S(1)} %get-tuple-element.60), channel_id=1, source_target_pairs={{0,16},{1,2},{2,1},{3,4},{4,3},{5,6},{6,5},{7,8},{8,7},{9,10},{10,... | collective-permute-start | bytes 196616 | tf_op jit(solution)/shard_map/ppermute | solution.py:32
  28.1 4.5 %collective-permute-start.6 = (f32[4,8,4,128]{3,2,1,0:T(4,128)S(1)}, f32[4,8,4,128]{3,2,1,0:T(4,128)S(1)}, u32[]{:S(2)}, u32[]{:S(2)}) collective-permute-start(f32[4,8,4,128]{3,2,1,0:T(4,128)S(1)} %get-tuple-element.61), channel_id=1, source_target_pairs={{0,1},{1,0},{2,3},{3,2},{4,5},{5,4},{6,7},{7,6},{8,9},{9,8},{10,11... | collective-permute-start | bytes 196616 | tf_op jit(solution)/shard_map/ppermute | solution.py:32
  32.8 4.4 %collective-permute-start.9 = (f32[13,16,128]{2,1,0:T(8,128)S(1)}, f32[13,16,128]{2,1,0:T(8,128)S(1)}, u32[]{:S(2)}, u32[]{:S(2)}) collective-permute-start(f32[13,16,128]{2,1,0:T(8,128)S(1)} %get-tuple-element.48), channel_id=1, source_target_pairs={{0,1},{1,0},{2,3},{3,2},{4,5},{5,4},{6,7},{7,6},{8,9},{9,8},{10,11... | collective-permute-start | bytes 319496 | tf_op jit(solution)/shard_map/ppermute | solution.py:32
  33.5 3.7 %collective-permute-start.8 = (f32[13,16,128]{2,1,0:T(8,128)S(1)}, f32[13,16,128]{2,1,0:T(8,128)S(1)}, u32[]{:S(2)}, u32[]{:S(2)}) collective-permute-start(f32[13,16,128]{2,1,0:T(8,128)S(1)} %get-tuple-element.49), channel_id=1, source_target_pairs={{0,16},{1,17},{2,18},{3,19},{4,20},{5,21},{6,22},{7,23},{8,24},{9,... | collective-permute-start | bytes 319496 | tf_op jit(solution)/shard_map/ppermute | solution.py:32
  38.3 4.8 %collective-permute-start.11 = (f32[4,4,4,128]{3,2,1,0:T(4,128)S(1)}, f32[4,4,4,128]{3,2,1,0:T(4,128)S(1)}, u32[]{:S(2)}, u32[]{:S(2)}) collective-permute-start(f32[4,4,4,128]{3,2,1,0:T(4,128)S(1)} %bitcast.45), channel_id=1, source_target_pairs={{0,16},{1,2},{2,1},{3,4},{4,3},{5,6},{6,5},{7,8},{8,7},{9,10},{10,... | collective-permute-start | bytes 98312 | tf_op jit(solution)/shard_map/ppermute | solution.py:32
  39.1 6.1 %collective-permute-start.10 = (f32[4,4,4,128]{3,2,1,0:T(4,128)S(1)}, f32[4,4,4,128]{3,2,1,0:T(4,128)S(1)}, u32[]{:S(2)}, u32[]{:S(2)}) collective-permute-start(f32[4,4,4,128]{3,2,1,0:T(4,128)S(1)} %bitcast.46), channel_id=1, source_target_pairs={{0,1},{1,0},{2,3},{3,2},{4,5},{5,4},{6,7},{7,6},{8,9},{9,8},{10,11... | collective-permute-start | bytes 98312 | tf_op jit(solution)/shard_map/ppermute | solution.py:32
  45.4 3.6 %collective-permute-start.13 = (f32[13,8,128]{2,1,0:T(8,128)S(1)}, f32[13,8,128]{2,1,0:T(8,128)S(1)}, u32[]{:S(2)}, u32[]{:S(2)}) collective-permute-start(f32[13,8,128]{2,1,0:T(8,128)S(1)} %get-tuple-element.62), channel_id=1, source_target_pairs={{0,1},{1,0},{2,3},{3,2},{4,5},{5,4},{6,7},{7,6},{8,9},{9,8},{10,11... | collective-permute-start | bytes 159752 | tf_op jit(solution)/shard_map/ppermute | solution.py:32
  45.5 3.5 %collective-permute-start.12 = (f32[13,8,128]{2,1,0:T(8,128)S(1)}, f32[13,8,128]{2,1,0:T(8,128)S(1)}, u32[]{:S(2)}, u32[]{:S(2)}) collective-permute-start(f32[13,8,128]{2,1,0:T(8,128)S(1)} %get-tuple-element.63), channel_id=1, source_target_pairs={{0,16},{1,17},{2,18},{3,19},{4,20},{5,21},{6,22},{7,23},{8,24},{9,... | collective-permute-start | bytes 159752 | tf_op jit(solution)/shard_map/ppermute | solution.py:32
